TPU v7x, 32 devices: a whole 2x2x4 slice. The times are simulated.
32 devices in a mesh: dom: 8 (over z, y), col: 4 (over x, core).
Axes of the slice: x: 2, y: 2, z: 4, core: 2. Of those that a mesh axis runs over, the one named last changes fastest.
Arguments:
- embeddings: bfloat16 [2, 200, 32768], P(None, 'col', 'dom'), may hold values from -3 to 3
- relations: bfloat16 [2, 200, 512], P(None, 'col'), may hold values from -3 to 3
- source_ids: int32 [4, 8192], P(None, 'dom'), may hold values from 0 to 4095
- relation_ids: int32 [4, 8192], P(None, 'dom'), may hold values from 0 to 511
- target_ids: int32 [4, 8192], P(None, 'dom'), may hold values from 0 to 4095
- negative_ids: int32 [4, 32, 256], P(None, 'dom'), may hold values from 0 to 127
- served_rows: int32 [64, 16], P('dom'), may hold values from 0 to 4095
Outputs:
- entity_grad: float32 [2, 200, 32768], P(None, 'col', 'dom')
All inputs are finite; a program needn't handle non-finite values.
Results may differ from a plain program's by a relative error of at most 0.007.
Values may be sent and summed in bfloat16 or wider, within the bound.
No kernel may reach another device: no remote copies, remote signals or barrier semaphores. Data moves between devices by JAX's collectives and lax.ppermute only.
A program may use at most 128 MiB of HBM per device.

v0:
```python
import functools

import jax
import jax.numpy as jnp
from jax import lax
from jax.experimental import pallas as pl
from jax.experimental.pallas import tpu as pltpu
from jax.sharding import PartitionSpec as P

BF16 = jnp.bfloat16
F32 = jnp.float32
I32 = jnp.int32
LANES = 128
PACK = 16
TILE = 256
VMEM_BYTES = 56 << 20


def rotate(shard, axis, by):
    size = lax.axis_size(axis)
    return lax.ppermute(shard, axis, [(i, (i + by) % size) for i in range(size)])


def swap(shard, axis, bit):
    size = lax.axis_size(axis)
    return lax.ppermute(shard, axis, [(i, i ^ bit) for i in range(size)])


def call(kernel, out_shape, args, grid=None, in_specs=None, out_specs=None, scratch=(), flops=0, moved=0):
    kwargs = {}
    if grid is not None:
        kwargs = dict(grid=grid, in_specs=in_specs, out_specs=out_specs)
    return pl.pallas_call(
        kernel,
        out_shape=out_shape,
        scratch_shapes=list(scratch),
        compiler_params=pltpu.CompilerParams(vmem_limit_bytes=VMEM_BYTES),
        cost_estimate=pl.CostEstimate(flops=int(flops), bytes_accessed=int(moved), transcendentals=0),
        **kwargs,
    )(*args)


def struct(*shape, dtype=BF16):
    return jax.ShapeDtypeStruct(shape, dtype)


def hot_rows(count, ids):
    return (lax.broadcasted_iota(I32, (count, ids.shape[1]), 0) == ids).astype(BF16)


def lane_row(block):
    return jnp.concatenate([block[k : k + 1, :] for k in range(block.shape[0])], axis=1)


def received_ids(packet_ref, me, bucket):
    size = packet_ref.shape[0]
    coded = packet_ref[lax.rem(me + bucket, size), PACK:, :].astype(F32)
    half = coded.shape[0] // 2
    return (coded[:half] * float(TILE) + coded[half:]).astype(I32)


def pool_rows(packet_ref):
    size = packet_ref.shape[0]
    return packet_ref[:, :PACK, :].reshape(size * PACK, LANES)


def prepare_kernel(pos_ref, emb_ref, rel_ref, served_ref, ids_ref, embp_ref, relp_ref, packet_ref, wide, coded):
    columns = emb_ref.shape[1]
    pad = embp_ref.shape[0] // 2
    me = pos_ref[0]
    entities = emb_ref.shape[2]
    relation_count = rel_ref.shape[2]
    wide[...] = jnp.zeros_like(wide)
    for half in range(2):
        wide[half * pad : half * pad + columns, :relation_count] = rel_ref[half].astype(F32)
    relp_ref[...] = wide[:, :relation_count].astype(BF16)
    for half in range(2):
        wide[half * pad : half * pad + columns, :] = emb_ref[half].astype(F32)
    embp_ref[...] = wide[...].astype(BF16)
    fetched = jnp.dot(embp_ref[...], hot_rows(entities, served_ref[...]), preferred_element_type=F32)
    fetched = jnp.concatenate([fetched, jnp.zeros((LANES - 2 * pad, fetched.shape[1]), F32)], axis=0)
    size = packet_ref.shape[0]
    packet_ref[:, :PACK, :] = fetched.T.astype(BF16).reshape(size, PACK, LANES)
    buckets, edges = ids_ref.shape
    for bucket in range(buckets):
        block = jnp.concatenate(
            [ids_ref[bucket : bucket + 1, k : k + LANES] for k in range(0, edges, LANES)], axis=0
        )
        high = lax.shift_right_logical(block, 8)
        coded[bucket] = jnp.concatenate([high, block - high * TILE], axis=0).astype(F32).astype(BF16)
    for to in range(size):
        bucket = jnp.minimum(lax.rem(me - to + size, size), buckets - 1)
        packet_ref[to, PACK:, :] = coded[bucket]


def product_kernel(bucket, emb_ref, rel_ref, source_ref, relation_ref, product_ref, rows_ref):
    pad = emb_ref.shape[0] // 2
    source = jnp.dot(
        emb_ref[...], hot_rows(emb_ref.shape[1], source_ref[bucket : bucket + 1, :]), preferred_element_type=F32
    )
    rel = jnp.dot(
        rel_ref[...], hot_rows(rel_ref.shape[1], relation_ref[bucket : bucket + 1, :]), preferred_element_type=F32
    )
    rows_ref[...] = rel.astype(BF16)
    s0, s1, r0, r1 = source[:pad], source[pad:], rel[:pad], rel[pad:]
    product_ref[...] = jnp.concatenate([s0 * r0 - s1 * r1, s0 * r1 + s1 * r0], axis=0).astype(BF16)


def target_kernel(bucket, pos_ref, emb_ref, ids_ref, out_ref):
    if bucket == 0:
        ids = ids_ref[0:1, :]
    else:
        ids = lane_row(received_ids(ids_ref, pos_ref[0], bucket))
    out_ref[...] = jnp.dot(
        emb_ref[...], hot_rows(emb_ref.shape[1], ids), preferred_element_type=F32
    ).astype(BF16)


def score_kernel(pos_ref, packet_ref, *refs):
    buckets = len(refs) - 2
    products, (mine_ref, theirs_ref) = refs[:buckets], refs[buckets:]
    core = pos_ref[1]
    height, edges = products[0].shape
    pool = pool_rows(packet_ref)[:, :height]
    for bucket in range(buckets):
        half, place = divmod(bucket, buckets // 2)
        scores = jnp.dot(pool, products[bucket][...], preferred_element_type=F32)
        spot = slice(place * edges, (place + 1) * edges)

        @pl.when(core == half)
        def _():
            mine_ref[:, spot] = scores

        @pl.when(core != half)
        def _():
            theirs_ref[:, spot] = scores.astype(BF16)


def slope_kernel(pos_ref, own_ref, other_ref, negatives_ref, out_ref):
    core = pos_ref[1]
    count, width = own_ref.shape
    buckets, spans, negs = negatives_ref.shape
    span_len = width // (buckets // 2 * spans)
    for place in range(buckets // 2):
        for span in range(spans):
            drawn = negatives_ref[core * (buckets // 2) + place, span : span + 1, :]
            times = jnp.sum(
                (lax.broadcasted_iota(I32, (count, negs), 0) == drawn).astype(F32), axis=1, keepdims=True
            )
            start = (place * spans + span) * span_len
            spot = slice(start, start + span_len)
            scores = own_ref[:, spot].astype(F32) + other_ref[:, spot].astype(F32)
            out_ref[:, spot] = (times * jax.nn.sigmoid(scores)).astype(BF16)


def bucket_slopes(core, mine_ref, theirs_ref, bucket, buckets, edges):
    half, place = divmod(bucket, buckets // 2)
    spot = slice(place * edges, (place + 1) * edges)
    return jnp.where(core == half, mine_ref[:, spot], theirs_ref[:, spot])


def pool_grad_kernel(pos_ref, mine_ref, theirs_ref, *refs):
    buckets = len(refs) - 1
    out_ref = refs[-1]
    core = pos_ref[1]
    height, edges = refs[0].shape
    total = None
    for bucket in range(buckets):
        slopes = bucket_slopes(core, mine_ref, theirs_ref, bucket, buckets, edges)
        part = lax.dot_general(
            slopes, refs[bucket][...], (((1,), (1,)), ((), ())), preferred_element_type=F32
        )
        total = part if total is None else total + part
    total = jnp.concatenate([total, jnp.zeros((total.shape[0], LANES - height), F32)], axis=1)
    out_ref[...] = total.astype(BF16).reshape(out_ref.shape)


def positive_kernel(*refs):
    out_ref = refs[-1]
    pairs = len(refs) // 2
    rows = []
    for k in range(pairs):
        rows.append(
            jnp.sum(refs[2 * k][...].astype(F32) * refs[2 * k + 1][...].astype(F32), axis=0, keepdims=True)
        )
    rows.append(jnp.zeros((out_ref.shape[0] - pairs, out_ref.shape[1]), F32))
    out_ref[...] = jnp.concatenate(rows, axis=0).astype(BF16)


def final_kernel(buckets, pos_ref, mine_ref, theirs_ref, packet_ref, returned_ref, served_ref, source_ref, target_ref,
                 own_ref, near_ref, far_ref, *refs):
    relation_rows = refs[:buckets]
    targets = refs[buckets : 2 * buckets]
    products = refs[2 * buckets : 3 * buckets]
    out_ref, values, cols = refs[3 * buckets :]
    step = pl.program_id(0)
    height, edges = targets[0].shape
    pad = height // 2
    columns = out_ref.shape[1]
    tiles = out_ref.shape[2] // TILE

    @pl.when(step == 0)
    def _():
        me, core = pos_ref[0], pos_ref[1]
        positive = (
            own_ref[...].astype(F32)
            + near_ref[...].astype(F32)
            + far_ref[0].astype(F32)
            + far_ref[1].astype(F32)
        )
        slope = -jax.nn.sigmoid(-positive)
        pool = pool_rows(packet_ref).astype(F32).T[:height].astype(BF16)
        rows = []
        for bucket in range(buckets):
            slopes = bucket_slopes(core, mine_ref, theirs_ref, bucket, buckets, edges)
            query = jnp.dot(pool, slopes, preferred_element_type=F32)
            total = slope[bucket : bucket + 1] * targets[bucket][...].astype(F32) + query
            rel = relation_rows[bucket][...].astype(F32)
            t0, t1, r0, r1 = total[:pad], total[pad:], rel[:pad], rel[pad:]
            values[:, bucket * edges : (bucket + 1) * edges] = jnp.concatenate(
                [t0 * r0 + t1 * r1, t1 * r0 - t0 * r1], axis=0
            ).astype(BF16)
            rows.append(source_ref[bucket : bucket + 1, :])
        for bucket in range(buckets):
            place = 0 if bucket == 0 else buckets - 1 + bucket
            spot = slice((buckets + bucket) * edges, (buckets + bucket + 1) * edges)
            values[:, spot] = (slope[place : place + 1] * products[bucket][...].astype(F32)).astype(BF16)
            if bucket == 0:
                rows.append(target_ref[0:1, :])
            else:
                rows.append(lane_row(received_ids(packet_ref, me, bucket)))
        back = returned_ref[...].reshape(-1, LANES).astype(F32).T[:height]
        values[:, 2 * buckets * edges :] = back.astype(BF16)
        rows.append(served_ref[...])
        at = 0
        for row in rows:
            for k in range(0, row.shape[1], LANES):
                cols[at : at + LANES, :] = jnp.broadcast_to(row[:, k : k + LANES], (LANES, LANES)).T
                at += LANES

    lane = lax.broadcasted_iota(I32, cols.shape, 1)
    for tile in range(tiles):
        base = (step * tiles + tile) * TILE
        ids = cols[...]
        hot = jnp.concatenate(
            [(ids == lane + (base + k)).astype(BF16) for k in range(0, TILE, LANES)], axis=1
        )
        total = jnp.dot(values[...], hot, preferred_element_type=F32)
        for half in range(2):
            out_ref[half, :, tile * TILE : (tile + 1) * TILE] = total[half * pad : half * pad + columns]


def body(embeddings, relations, source_ids, relation_ids, target_ids, negative_ids, served_rows):
    halves, columns, entities = embeddings.shape
    buckets, edges = source_ids.shape
    relation_count = relations.shape[2]
    size = lax.axis_size("dom")
    pad = -(-columns // 8) * 8
    height = 2 * pad
    pool_count = served_rows.size
    served = served_rows.reshape(1, pool_count)
    position = jnp.stack([lax.axis_index("dom"), lax.axis_index("col") & 1]).astype(I32)
    smem = pl.BlockSpec(memory_space=pltpu.SMEM)
    packet_rows = PACK + 2 * edges // LANES

    def whole(array):
        return pl.BlockSpec(array.shape, lambda *_: (0,) * array.ndim)

    def local(kernel, out, *args, scratch=(), flops=0):
        outs = out if isinstance(out, tuple) else (out,)
        moved = sum(a.size * a.dtype.itemsize for a in args + outs)
        return call(
            kernel,
            out,
            args,
            grid=(1,),
            in_specs=[smem if a is position else whole(a) for a in args],
            out_specs=jax.tree.map(whole, out),
            scratch=scratch,
            flops=flops,
            moved=moved,
        )

    emb, rel, packet = local(
        prepare_kernel,
        (struct(height, entities), struct(height, relation_count), struct(size, packet_rows, LANES)),
        position, embeddings, relations, served, target_ids,
        scratch=(pltpu.VMEM((height, entities), F32), pltpu.VMEM((buckets, packet_rows - PACK, LANES), BF16)),
        flops=2 * LANES * entities * pool_count,
    )
    packet = lax.all_to_all(packet, "dom", split_axis=0, concat_axis=0, tiled=True)
    products, relation_rows = [], []
    for bucket in range(buckets):
        product, rows = local(
            functools.partial(product_kernel, bucket),
            (struct(height, edges), struct(height, edges)),
            emb, rel, source_ids, relation_ids,
            flops=2 * LANES * (entities + relation_count) * edges,
        )
        products.append(product)
        relation_rows.append(rows)
    owned_targets = []
    for bucket in range(buckets):
        owned_targets.append(
            local(
                functools.partial(target_kernel, bucket),
                struct(height, edges),
                position, emb, target_ids if bucket == 0 else packet,
                flops=2 * LANES * entities * edges,
            )
        )
    targets = [owned_targets[0]] + [rotate(owned_targets[b], "dom", b) for b in range(1, buckets)]
    owned_products = [products[0]] + [rotate(products[b], "dom", -b) for b in range(1, buckets)]

    width = buckets // 2 * edges
    mine, theirs = local(
        score_kernel,
        (struct(pool_count, width, dtype=F32), struct(pool_count, width)),
        position, packet, *products,
        flops=2 * LANES * pool_count * edges * buckets,
    )
    pair = (mine + swap(theirs, "col", 1).astype(F32)).astype(BF16)
    slopes_mine = local(
        slope_kernel, struct(pool_count, width), position, pair, swap(pair, "col", 2), negative_ids,
    )
    slopes_theirs = swap(slopes_mine, "col", 1)
    pool_grad = local(
        pool_grad_kernel, struct(size, PACK, LANES), position, slopes_mine, slopes_theirs, *products,
        flops=2 * LANES * pool_count * edges * buckets,
    )
    returned = lax.all_to_all(pool_grad, "dom", split_axis=0, concat_axis=0, tiled=True)

    pairs = [products[0], owned_targets[0]]
    for b in range(1, buckets):
        pairs += [products[b], targets[b]]
    for b in range(1, buckets):
        pairs += [owned_products[b], owned_targets[b]]
    own = local(positive_kernel, struct(16, edges), *pairs)
    near = swap(own, "col", 1)
    far = swap(jnp.stack([own, near]), "col", 2)

    args = [position, slopes_mine, slopes_theirs, packet, returned, served, source_ids, target_ids, own, near, far]
    args += relation_rows + targets + owned_products
    total = 2 * buckets * edges + pool_count
    steps = 4
    return call(
        functools.partial(final_kernel, buckets),
        struct(halves, columns, entities, dtype=F32),
        args,
        grid=(steps,),
        in_specs=[smem if a is position else whole(a) for a in args],
        out_specs=pl.BlockSpec((halves, columns, entities // steps), lambda i: (0, 0, i)),
        scratch=(pltpu.VMEM((height, total), BF16), pltpu.VMEM((total, LANES), I32)),
        flops=2 * LANES * total * entities,
        moved=sum(a.size * a.dtype.itemsize for a in args) + 4 * halves * columns * entities,
    )


def solution(mesh):
    placed = (
        P(None, "col", "dom"),
        P(None, "col", None),
        P(None, "dom"),
        P(None, "dom"),
        P(None, "dom"),
        P(None, "dom", None),
        P("dom", None),
    )
    return jax.shard_map(
        body, mesh=mesh, in_specs=placed, out_specs=P(None, "col", "dom"), check_vma=False
    )
```

profile of v0, /device:TPU:0, one launch (start us, length us, event | category | flops | bytes accessed | tf_op | source)
XLA Modules:
  0.0 122.3 jit_solution(9244067218036817587)
XLA Ops:
  0.0 1.4 %reshape.3.served_ref = s32[1,128]{1,0:T(1,128)} reshape(s32[8,16]{1,0:T(8,128)} %param.13) | data formatting | bytes 1024 | tf_op jit(solution)/shard_map/reshape | solution.py:261
  1.4 1.5 %copy.9.rel_ref = bf16[2,50,512]{2,1,0:T(8,128)(2,1)} copy(bf16[2,50,512]{2,0,1:T(2,128)(2,1)} %param.8) | data formatting | bytes 204800 | tf_op args[1]
  2.9 2.5 %copy.8.emb_ref = bf16[2,50,4096]{2,1,0:T(8,128)(2,1)} copy(bf16[2,50,4096]{2,0,1:T(2,128)(2,1)} %param.7) | data formatting | bytes 1638400 | tf_op args[0]
  5.4 0.6 pad_add_fusion.pos_ref
  6.0 2.6 %shard_map.73 = (bf16[112,4096]{1,0:T(8,128)(2,1)}, bf16[112,512]{1,0:T(8,128)(2,1)}, bf16[8,32,128]{2,1,0:T(8,128)(2,1)}) custom-call(s32[2]{0:T(128)} %pad_add_fusion.pos_ref, bf16[2,50,4096]{2,1,0:T(8,128)(2,1)} %copy.8.emb_ref, bf16[2,50,512]{2,1,0:T(8,128)(2,1)} %copy.9.rel_ref, s32[1,128]{1,0:T(1,128)} %reshape.3.served_ref, s32[4,1024]{1,0:T(4,128)} %target_ref.1), custom_call_target="tpu_custom_call" | custom-call | flops 134217728 | bytes 2036232 | tf_op jit(solution)/shard_map/pallas_call | solution.py:33
  8.6 7.3 %all-to-all-start = ((bf16[8,32,128]{2,1,0:T(8,128)(2,1)}), bf16[8,32,128]{2,1,0:T(8,128)(2,1)S(1)}, u32[]{:S(2)}, u32[]{:S(2)}) async-start(bf16[8,32,128]{2,1,0:T(8,128)(2,1)} %get-tuple-element.18), calls=%async_computation | async-start | bytes 131072 | tf_op jit(solution)/shard_map/all_to_all | solution.py:291
  15.9 3.6 %shard_map.77 = (bf16[112,1024]{1,0:T(8,128)(2,1)}, bf16[112,1024]{1,0:T(8,128)(2,1)}) custom-call(bf16[112,4096]{1,0:T(8,128)(2,1)} %get-tuple-element.19.emb_ref, bf16[112,512]{1,0:T(8,128)(2,1)} %get-tuple-element.20.rel_ref, s32[4,1024]{1,0:T(4,128)} %source_ref.9, s32[4,1024]{1,0:T(4,128)} %relation_ref.7), custom_call_target="tpu_custom_call" | custom-call | flops 1207959552 | bytes 1523712 | tf_op jit(solution)/shard_map/pallas_call | solution.py:33
  19.4 3.6 %shard_map.76 = (bf16[112,1024]{1,0:T(8,128)(2,1)}, bf16[112,1024]{1,0:T(8,128)(2,1)}) custom-call(bf16[112,4096]{1,0:T(8,128)(2,1)} %get-tuple-element.19.emb_ref, bf16[112,512]{1,0:T(8,128)(2,1)} %get-tuple-element.20.rel_ref, s32[4,1024]{1,0:T(4,128)} %source_ref.9, s32[4,1024]{1,0:T(4,128)} %relation_ref.7), custom_call_target="tpu_custom_call" | custom-call | flops 1207959552 | bytes 1523712 | tf_op jit(solution)/shard_map/pallas_call | solution.py:33
  23.0 3.6 %shard_map.75 = (bf16[112,1024]{1,0:T(8,128)(2,1)}, bf16[112,1024]{1,0:T(8,128)(2,1)}) custom-call(bf16[112,4096]{1,0:T(8,128)(2,1)} %get-tuple-element.19.emb_ref, bf16[112,512]{1,0:T(8,128)(2,1)} %get-tuple-element.20.rel_ref, s32[4,1024]{1,0:T(4,128)} %source_ref.9, s32[4,1024]{1,0:T(4,128)} %relation_ref.7), custom_call_target="tpu_custom_call" | custom-call | flops 1207959552 | bytes 1523712 | tf_op jit(solution)/shard_map/pallas_call | solution.py:33
  26.5 3.6 %shard_map.74 = (bf16[112,1024]{1,0:T(8,128)(2,1)}, bf16[112,1024]{1,0:T(8,128)(2,1)}) custom-call(bf16[112,4096]{1,0:T(8,128)(2,1)} %get-tuple-element.19.emb_ref, bf16[112,512]{1,0:T(8,128)(2,1)} %get-tuple-element.20.rel_ref, s32[4,1024]{1,0:T(4,128)} %source_ref.9, s32[4,1024]{1,0:T(4,128)} %relation_ref.7), custom_call_target="tpu_custom_call" | custom-call | flops 1207959552 | bytes 1523712 | tf_op jit(solution)/shard_map/pallas_call | solution.py:33
  30.1 0.0 all-to-all-done.packet_ref.ids_ref
  30.1 0.0 copy-start.6
  30.1 0.6 copy-done.6
  30.7 3.3 %shard_map.78 = (f32[128,2048]{1,0:T(8,128)}, bf16[128,2048]{1,0:T(8,128)(2,1)}) custom-call(s32[2]{0:T(128)} %pad_add_fusion.pos_ref, bf16[8,32,128]{2,1,0:T(8,128)(2,1)} %copy-done.6, bf16[112,1024]{1,0:T(8,128)(2,1)} %get-tuple-element.21.refs_0_.refs_8_, bf16[112,1024]{1,0:T(8,128)(2,1)} %get-tuple-element.22.refs_1_.refs_2_, ...), custom_call_target="tpu_custom_call" | custom-call | flops 134217728 | bytes 2555912 | tf_op jit(solution)/shard_map/pallas_call | solution.py:33
  34.1 0.0 collective-permute-start
  34.1 2.1 %collective-permute-done = bf16[128,2048]{1,0:T(8,128)(2,1)S(1)} collective-permute-done((bf16[128,2048]{1,0:T(8,128)(2,1)}, bf16[128,2048]{1,0:T(8,128)(2,1)S(1)}, u32[]{:S(2)}, u32[]{:S(2)}) %collective-permute-start) | collective-permute-done | bytes 524320 | tf_op jit(solution)/shard_map/ppermute | solution.py:26
  36.2 1.3 %add_convert_fusion.own_ref = bf16[128,2048]{1,0:T(8,128)(2,1)S(1)} fusion(f32[128,2048]{1,0:T(8,128)} %get-tuple-element.25, bf16[128,2048]{1,0:T(8,128)(2,1)S(1)} %collective-permute-done), kind=kLoop, calls=%fused_computation | loop fusion | flops 786432 | bytes 2097152 | tf_op jit(solution)/shard_map/convert_element_type | solution.py:322
  37.5 0.0 copy-start
  37.5 1.6 %collective-permute-start.1 = (bf16[128,2048]{1,0:T(8,128)(2,1)S(1)}, bf16[128,2048]{1,0:T(8,128)(2,1)S(1)}, u32[]{:S(2)}, u32[]{:S(2)}) collective-permute-start(bf16[128,2048]{1,0:T(8,128)(2,1)S(1)} %add_convert_fusion.own_ref), channel_id=1, source_target_pairs={{0,2},{1,3},{2,0},{3,1},{4,6},{5,7},{6,4},{7,5},{8,10},{9,11},{10,... | collective-permute-start | bytes 1572872 | tf_op jit(solution)/shard_map/ppermute | solution.py:26
  39.1 0.0 copy-done.1
  39.1 3.8 %collective-permute-start.8 = (bf16[112,1024]{1,0:T(8,128)(2,1)S(1)}, bf16[112,1024]{1,0:T(8,128)(2,1)S(1)}, u32[]{:S(2)}, u32[]{:S(2)}) collective-permute-start(bf16[112,1024]{1,0:T(8,128)(2,1)S(1)} %copy-done.1), channel_id=1, source_target_pairs={{0,20},{4,24},{8,28},{12,0},{16,4},{20,8},{24,12},{28,16},{1,21},{... | collective-permute-start | bytes 688136 | tf_op jit(solution)/shard_map/ppermute | solution.py:21
  42.9 0.0 copy-done.2
  42.9 1.5 %collective-permute-start.7 = (bf16[112,1024]{1,0:T(8,128)(2,1)S(1)}, bf16[112,1024]{1,0:T(8,128)(2,1)S(1)}, u32[]{:S(2)}, u32[]{:S(2)}) collective-permute-start(bf16[112,1024]{1,0:T(8,128)(2,1)S(1)} %copy-done.2), channel_id=1, source_target_pairs={{0,24},{4,28},{8,0},{12,4},{16,8},{20,12},{24,16},{28,20},{1,25},{... | collective-permute-start | bytes 688136 | tf_op jit(solution)/shard_map/ppermute | solution.py:21
  44.4 0.0 copy-done.3
  44.4 0.5 collective-permute-start.6
  45.0 3.2 %shard_map.82.refs_9_ = bf16[112,1024]{1,0:T(8,128)(2,1)} custom-call(s32[2]{0:T(128)} %pad_add_fusion.pos_ref, bf16[112,4096]{1,0:T(8,128)(2,1)} %get-tuple-element.19.emb_ref, bf16[8,32,128]{2,1,0:T(8,128)(2,1)} %copy-done.6), custom_call_target="tpu_custom_call" | custom-call | flops 1073741824 | bytes 1212424 | tf_op jit(solution)/shard_map/pallas_call | solution.py:33
  48.2 0.0 copy-done
  48.2 1.5 %collective-permute-start.3 = (bf16[112,1024]{1,0:T(8,128)(2,1)}, bf16[112,1024]{1,0:T(8,128)(2,1)S(1)}, u32[]{:S(2)}, u32[]{:S(2)}) collective-permute-start(bf16[112,1024]{1,0:T(8,128)(2,1)} %shard_map.82.refs_9_), channel_id=1, source_target_pairs={{0,4},{4,8},{8,12},{12,16},{16,20},{20,24},{24,28},{28,0},{1,5},{5... | collective-permute-start | bytes 688136 | tf_op jit(solution)/shard_map/ppermute | solution.py:21
  49.6 1.9 %collective-permute-done.1.other_ref = bf16[128,2048]{1,0:T(8,128)(2,1)S(1)} collective-permute-done((bf16[128,2048]{1,0:T(8,128)(2,1)S(1)}, bf16[128,2048]{1,0:T(8,128)(2,1)S(1)}, u32[]{:S(2)}, u32[]{:S(2)}) %collective-permute-start.1) | collective-permute-done | bytes 524320 | tf_op jit(solution)/shard_map/ppermute | solution.py:26
  51.6 0.8 copy-done.5
  52.4 2.3 %shard_map.79.mine_ref = bf16[128,2048]{1,0:T(8,128)(2,1)} custom-call(s32[2]{0:T(128)} %pad_add_fusion.pos_ref, bf16[128,2048]{1,0:T(8,128)(2,1)} %copy-done, bf16[128,2048]{1,0:T(8,128)(2,1)} %copy-done.5, s32[4,4,256]{2,1,0:T(4,128)} %negatives_ref.1), custom_call_target="tpu_custom_call" | custom-call | bytes 1589256 | tf_op jit(solution)/shard_map/pallas_call | solution.py:33
  54.7 0.0 collective-permute-start.2
  54.7 3.2 %shard_map.84.refs_13_ = bf16[112,1024]{1,0:T(8,128)(2,1)} custom-call(s32[2]{0:T(128)} %pad_add_fusion.pos_ref, bf16[112,4096]{1,0:T(8,128)(2,1)} %get-tuple-element.19.emb_ref, bf16[8,32,128]{2,1,0:T(8,128)(2,1)} %copy-done.6), custom_call_target="tpu_custom_call" | custom-call | flops 1073741824 | bytes 1212424 | tf_op jit(solution)/shard_map/pallas_call | solution.py:33
  57.9 3.2 %shard_map.83.refs_11_ = bf16[112,1024]{1,0:T(8,128)(2,1)} custom-call(s32[2]{0:T(128)} %pad_add_fusion.pos_ref, bf16[112,4096]{1,0:T(8,128)(2,1)} %get-tuple-element.19.emb_ref, bf16[8,32,128]{2,1,0:T(8,128)(2,1)} %copy-done.6), custom_call_target="tpu_custom_call" | custom-call | flops 1073741824 | bytes 1212424 | tf_op jit(solution)/shard_map/pallas_call | solution.py:33
  61.1 0.0 collective-permute-done.8.refs_12_.refs_11_
  61.2 2.9 %collective-permute-start.4 = (bf16[112,1024]{1,0:T(8,128)(2,1)}, bf16[112,1024]{1,0:T(8,128)(2,1)S(1)}, u32[]{:S(2)}, u32[]{:S(2)}) collective-permute-start(bf16[112,1024]{1,0:T(8,128)(2,1)} %shard_map.83.refs_11_), channel_id=1, source_target_pairs={{0,8},{4,12},{8,16},{12,20},{16,24},{20,28},{24,0},{28,4},{1,9},{5... | collective-permute-start | bytes 688136 | tf_op jit(solution)/shard_map/ppermute | solution.py:21
  64.0 0.0 collective-permute-done.7.refs_10_
  64.0 0.0 copy-done.13
  64.0 1.6 %collective-permute-start.5 = (bf16[112,1024]{1,0:T(8,128)(2,1)S(1)}, bf16[112,1024]{1,0:T(8,128)(2,1)S(1)}, u32[]{:S(2)}, u32[]{:S(2)}) collective-permute-start(bf16[112,1024]{1,0:T(8,128)(2,1)S(1)} %copy-done.13), channel_id=1, source_target_pairs={{0,12},{4,16},{8,20},{12,24},{16,28},{20,0},{24,4},{28,8},{1,13},{... | collective-permute-start | bytes 688136 | tf_op jit(solution)/shard_map/ppermute | solution.py:21
  65.7 3.2 %shard_map.81.refs_1_.refs_4_ = bf16[112,1024]{1,0:T(8,128)(2,1)} custom-call(s32[2]{0:T(128)} %pad_add_fusion.pos_ref, bf16[112,4096]{1,0:T(8,128)(2,1)} %get-tuple-element.19.emb_ref, s32[4,1024]{1,0:T(4,128)} %target_ref.1), custom_call_target="tpu_custom_call" | custom-call | flops 1073741824 | bytes 1163272 | tf_op jit(solution)/shard_map/pallas_call | solution.py:33
  68.8 0.0 copy-done.7
  68.8 0.0 copy-done.8
  68.8 0.0 collective-permute-done.6.refs_8_.refs_9_
  68.9 0.0 collective-permute-done.3.refs_3_.refs_5_
  68.9 2.8 %collective-permute-done.4.refs_5_.refs_6_ = bf16[112,1024]{1,0:T(8,128)(2,1)S(1)} collective-permute-done((bf16[112,1024]{1,0:T(8,128)(2,1)}, bf16[112,1024]{1,0:T(8,128)(2,1)S(1)}, u32[]{:S(2)}, u32[]{:S(2)}) %collective-permute-start.4) | collective-permute-done | bytes 229408 | tf_op jit(solution)/shard_map/ppermute | solution.py:21
  71.7 11.9 %collective-permute-done.5.refs_7_ = bf16[112,1024]{1,0:T(8,128)(2,1)S(1)} collective-permute-done((bf16[112,1024]{1,0:T(8,128)(2,1)S(1)}, bf16[112,1024]{1,0:T(8,128)(2,1)S(1)}, u32[]{:S(2)}, u32[]{:S(2)}) %collective-permute-start.5) | collective-permute-done | bytes 229408 | tf_op jit(solution)/shard_map/ppermute | solution.py:21
  83.6 0.0 copy-done.11
  83.6 0.0 copy-start.12
  83.6 0.7 copy-done.12
  84.3 2.7 %shard_map.85.own_ref = bf16[16,1024]{1,0:T(8,128)(2,1)} custom-call(bf16[112,1024]{1,0:T(8,128)(2,1)} %get-tuple-element.21.refs_0_.refs_8_, bf16[112,1024]{1,0:T(8,128)(2,1)} %shard_map.81.refs_1_.refs_4_, bf16[112,1024]{1,0:T(8,128)(2,1)} %get-tuple-element.22.refs_1_.refs_2_, bf16[112,1024]{1,0:T(8,128)(2,1)} %copy-done.10, ...), custom_call_target="tpu_custom_call" | custom-call | bytes 3244032 | tf_op jit(solution)/shard_map/pallas_call | solution.py:33
  87.0 0.0 collective-permute-start.9
  87.0 1.4 %collective-permute-done.9.near_ref = bf16[16,1024]{1,0:T(8,128)(2,1)S(1)} collective-permute-done((bf16[16,1024]{1,0:T(8,128)(2,1)}, bf16[16,1024]{1,0:T(8,128)(2,1)S(1)}, u32[]{:S(2)}, u32[]{:S(2)}) %collective-permute-start.9) | collective-permute-done | bytes 32800 | tf_op jit(solution)/shard_map/ppermute | solution.py:26
  88.4 0.8 pad_maximum_fusion
  89.2 0.6 collective-permute-start.10
  89.8 0.0 collective-permute-done.2.theirs_ref
  89.8 0.8 copy-done.4
  90.6 2.5 %shard_map.80 = bf16[8,16,128]{2,1,0:T(8,128)(2,1)} custom-call(s32[2]{0:T(128)} %pad_add_fusion.pos_ref, bf16[128,2048]{1,0:T(8,128)(2,1)} %shard_map.79.mine_ref, bf16[128,2048]{1,0:T(8,128)(2,1)} %copy-done.4, bf16[112,1024]{1,0:T(8,128)(2,1)} %get-tuple-element.21.refs_0_.refs_8_, bf16[112,1024]{1,0:T(8,128)(2,1)} %get-tuple-element.22.refs_1_.refs_2_, ...), custom_call_target="tpu_custom_call" | custom-call | flops 134217728 | bytes 1998856 | tf_op jit(solution)/shard_map/pallas_call | solution.py:33
  93.1 3.3 %all-to-all-start.1 = ((bf16[8,16,128]{2,1,0:T(8,128)(2,1)}), bf16[8,16,128]{2,1,0:T(8,128)(2,1)S(1)}, u32[]{:S(2)}, u32[]{:S(2)}) async-start(bf16[8,16,128]{2,1,0:T(8,128)(2,1)} %shard_map.80), calls=%async_computation.1 | async-start | bytes 65536 | tf_op jit(solution)/shard_map/all_to_all | solution.py:331
  96.4 0.0 collective-permute-done.10.far_ref
  96.4 6.6 %all-to-all-done.1.returned_ref = bf16[8,16,128]{2,1,0:T(8,128)(2,1)S(1)} async-done(((bf16[8,16,128]{2,1,0:T(8,128)(2,1)}), bf16[8,16,128]{2,1,0:T(8,128)(2,1)S(1)}, u32[]{:S(2)}, u32[]{:S(2)}) %all-to-all-start.1) | async-done | bytes 32800 | tf_op jit(solution)/shard_map/all_to_all | solution.py:331
  103.0 0.0 copy-done.15
  103.0 0.6 copy-done.14
  103.6 14.7 %shard_map.86 = f32[2,50,4096]{2,1,0:T(8,128)} custom-call(s32[2]{0:T(128)} %pad_add_fusion.pos_ref, bf16[128,2048]{1,0:T(8,128)(2,1)} %shard_map.79.mine_ref, bf16[128,2048]{1,0:T(8,128)(2,1)} %copy-done.4, bf16[8,32,128]{2,1,0:T(8,128)(2,1)} %copy-done.6, bf16[8,16,128]{2,1,0:T(8,128)(2,1)} %copy-done.14, s32[1,128]{1,0:T(1,128)} %reshape.3.served_ref, ...), custom_call_target="tpu_custom_call" | custom-call | flops 8724152320 | bytes 5702152 | tf_op jit(solution)/shard_map/pallas_call | solution.py:33
  118.4 3.9 %copy.10 = f32[2,50,4096]{2,0,1:T(2,128)} copy(f32[2,50,4096]{2,1,0:T(8,128)} %shard_map.86) | data formatting | bytes 3276800 | tf_op jit(solution)/shard_map/pallas_call | solution.py:33
  (17 shorter events, 0.0 us)
Async XLA Ops:
  8.6 21.5 %all-to-all-start = ((bf16[8,32,128]{2,1,0:T(8,128)(2,1)}), bf16[8,32,128]{2,1,0:T(8,128)(2,1)S(1)}, u32[]{:S(2)}, u32[]{:S(2)}) async-start(bf16[8,32,128]{2,1,0:T(8,128)(2,1)} %get-tuple-element.18), calls=%async_computation | async-start | bytes 131072 | tf_op jit(solution)/shard_map/all_to_all | solution.py:291
  30.1 9.0 %copy-start.1 = (bf16[112,1024]{1,0:T(8,128)(2,1)S(1)}, bf16[112,1024]{1,0:T(8,128)(2,1)}, u32[]{:S(2)}) copy-start(bf16[112,1024]{1,0:T(8,128)(2,1)} %get-tuple-element.24.refs_3_.refs_6_) | copy-start | bytes 688132
  30.1 12.8 %copy-start.2 = (bf16[112,1024]{1,0:T(8,128)(2,1)S(1)}, bf16[112,1024]{1,0:T(8,128)(2,1)}, u32[]{:S(2)}) copy-start(bf16[112,1024]{1,0:T(8,128)(2,1)} %get-tuple-element.23.refs_2_.refs_4_) | copy-start | bytes 688132
  30.1 14.4 %copy-start.3 = (bf16[112,1024]{1,0:T(8,128)(2,1)S(1)}, bf16[112,1024]{1,0:T(8,128)(2,1)}, u32[]{:S(2)}) copy-start(bf16[112,1024]{1,0:T(8,128)(2,1)} %get-tuple-element.22.refs_1_.refs_2_) | copy-start | bytes 688132
  30.1 0.6 copy-start.6
  34.1 2.1 %collective-permute-start = (bf16[128,2048]{1,0:T(8,128)(2,1)}, bf16[128,2048]{1,0:T(8,128)(2,1)S(1)}, u32[]{:S(2)}, u32[]{:S(2)}) collective-permute-start(bf16[128,2048]{1,0:T(8,128)(2,1)} %get-tuple-element.26), channel_id=1, source_target_pairs={{0,1},{1,0},{2,3},{3,2},{4,5},{5,4},{6,7},{7,6},{8,9},{9,8},{10,11... | collective-permute-start | bytes 1572872 | tf_op jit(solution)/shard_map/ppermute | solution.py:26
  37.5 10.6 %copy-start = (bf16[128,2048]{1,0:T(8,128)(2,1)}, bf16[128,2048]{1,0:T(8,128)(2,1)S(1)}, u32[]{:S(2)}) copy-start(bf16[128,2048]{1,0:T(8,128)(2,1)S(1)} %add_convert_fusion.own_ref) | copy-start | bytes 1572868
  37.5 14.0 %collective-permute-start.1 = (bf16[128,2048]{1,0:T(8,128)(2,1)S(1)}, bf16[128,2048]{1,0:T(8,128)(2,1)S(1)}, u32[]{:S(2)}, u32[]{:S(2)}) collective-permute-start(bf16[128,2048]{1,0:T(8,128)(2,1)S(1)} %add_convert_fusion.own_ref), channel_id=1, source_target_pairs={{0,2},{1,3},{2,0},{3,1},{4,6},{5,7},{6,4},{7,5},{8,10},{9,11},{10,... | collective-permute-start | bytes 1572872 | tf_op jit(solution)/shard_map/ppermute | solution.py:26
  39.1 22.0 %collective-permute-start.8 = (bf16[112,1024]{1,0:T(8,128)(2,1)S(1)}, bf16[112,1024]{1,0:T(8,128)(2,1)S(1)}, u32[]{:S(2)}, u32[]{:S(2)}) collective-permute-start(bf16[112,1024]{1,0:T(8,128)(2,1)S(1)} %copy-done.1), channel_id=1, source_target_pairs={{0,20},{4,24},{8,28},{12,0},{16,4},{20,8},{24,12},{28,16},{1,21},{... | collective-permute-start | bytes 688136 | tf_op jit(solution)/shard_map/ppermute | solution.py:21
  42.9 21.1 %collective-permute-start.7 = (bf16[112,1024]{1,0:T(8,128)(2,1)S(1)}, bf16[112,1024]{1,0:T(8,128)(2,1)S(1)}, u32[]{:S(2)}, u32[]{:S(2)}) collective-permute-start(bf16[112,1024]{1,0:T(8,128)(2,1)S(1)} %copy-done.2), channel_id=1, source_target_pairs={{0,24},{4,28},{8,0},{12,4},{16,8},{20,12},{24,16},{28,20},{1,25},{... | collective-permute-start | bytes 688136 | tf_op jit(solution)/shard_map/ppermute | solution.py:21
  44.4 24.4 %collective-permute-start.6 = (bf16[112,1024]{1,0:T(8,128)(2,1)S(1)}, bf16[112,1024]{1,0:T(8,128)(2,1)S(1)}, u32[]{:S(2)}, u32[]{:S(2)}) collective-permute-start(bf16[112,1024]{1,0:T(8,128)(2,1)S(1)} %copy-done.3), channel_id=1, source_target_pairs={{0,28},{4,0},{8,4},{12,8},{16,12},{20,16},{24,20},{28,24},{1,29},{... | collective-permute-start | bytes 688136 | tf_op jit(solution)/shard_map/ppermute | solution.py:21
  48.2 20.7 %collective-permute-start.3 = (bf16[112,1024]{1,0:T(8,128)(2,1)}, bf16[112,1024]{1,0:T(8,128)(2,1)S(1)}, u32[]{:S(2)}, u32[]{:S(2)}) collective-permute-start(bf16[112,1024]{1,0:T(8,128)(2,1)} %shard_map.82.refs_9_), channel_id=1, source_target_pairs={{0,4},{4,8},{8,12},{12,16},{16,20},{20,24},{24,28},{28,0},{1,5},{5... | collective-permute-start | bytes 688136 | tf_op jit(solution)/shard_map/ppermute | solution.py:21
  51.6 0.8 copy-start.5
  54.7 35.1 %collective-permute-start.2 = (bf16[128,2048]{1,0:T(8,128)(2,1)}, bf16[128,2048]{1,0:T(8,128)(2,1)S(1)}, u32[]{:S(2)}, u32[]{:S(2)}) collective-permute-start(bf16[128,2048]{1,0:T(8,128)(2,1)} %shard_map.79.mine_ref), channel_id=1, source_target_pairs={{0,1},{1,0},{2,3},{3,2},{4,5},{5,4},{6,7},{7,6},{8,9},{9,8},{10,11... | collective-permute-start | bytes 1572872 | tf_op jit(solution)/shard_map/ppermute | solution.py:26
  57.9 6.1 %copy-start.13 = (bf16[112,1024]{1,0:T(8,128)(2,1)S(1)}, bf16[112,1024]{1,0:T(8,128)(2,1)}, u32[]{:S(2)}) copy-start(bf16[112,1024]{1,0:T(8,128)(2,1)} %shard_map.84.refs_13_) | copy-start | bytes 688132
  61.1 7.7 %copy-start.7 = (bf16[112,1024]{1,0:T(8,128)(2,1)}, bf16[112,1024]{1,0:T(8,128)(2,1)S(1)}, u32[]{:S(2)}) copy-start(bf16[112,1024]{1,0:T(8,128)(2,1)S(1)} %collective-permute-done.8.refs_12_.refs_11_) | copy-start | bytes 688132
  61.2 10.5 %collective-permute-start.4 = (bf16[112,1024]{1,0:T(8,128)(2,1)}, bf16[112,1024]{1,0:T(8,128)(2,1)S(1)}, u32[]{:S(2)}, u32[]{:S(2)}) collective-permute-start(bf16[112,1024]{1,0:T(8,128)(2,1)} %shard_map.83.refs_11_), channel_id=1, source_target_pairs={{0,8},{4,12},{8,16},{12,20},{16,24},{20,28},{24,0},{28,4},{1,9},{5... | collective-permute-start | bytes 688136 | tf_op jit(solution)/shard_map/ppermute | solution.py:21
  64.0 4.8 %copy-start.8 = (bf16[112,1024]{1,0:T(8,128)(2,1)}, bf16[112,1024]{1,0:T(8,128)(2,1)S(1)}, u32[]{:S(2)}) copy-start(bf16[112,1024]{1,0:T(8,128)(2,1)S(1)} %collective-permute-done.7.refs_10_) | copy-start | bytes 688132
  64.0 19.5 %collective-permute-start.5 = (bf16[112,1024]{1,0:T(8,128)(2,1)S(1)}, bf16[112,1024]{1,0:T(8,128)(2,1)S(1)}, u32[]{:S(2)}, u32[]{:S(2)}) collective-permute-start(bf16[112,1024]{1,0:T(8,128)(2,1)S(1)} %copy-done.13), channel_id=1, source_target_pairs={{0,12},{4,16},{8,20},{12,24},{16,28},{20,0},{24,4},{28,8},{1,13},{... | collective-permute-start | bytes 688136 | tf_op jit(solution)/shard_map/ppermute | solution.py:21
  68.8 14.7 %copy-start.9 = (bf16[112,1024]{1,0:T(8,128)(2,1)}, bf16[112,1024]{1,0:T(8,128)(2,1)S(1)}, u32[]{:S(2)}) copy-start(bf16[112,1024]{1,0:T(8,128)(2,1)S(1)} %collective-permute-done.6.refs_8_.refs_9_) | copy-start | bytes 688132
  68.9 14.7 %copy-start.10 = (bf16[112,1024]{1,0:T(8,128)(2,1)}, bf16[112,1024]{1,0:T(8,128)(2,1)S(1)}, u32[]{:S(2)}) copy-start(bf16[112,1024]{1,0:T(8,128)(2,1)S(1)} %collective-permute-done.3.refs_3_.refs_5_) | copy-start | bytes 688132
  71.7 11.9 %copy-start.11 = (bf16[112,1024]{1,0:T(8,128)(2,1)}, bf16[112,1024]{1,0:T(8,128)(2,1)S(1)}, u32[]{:S(2)}) copy-start(bf16[112,1024]{1,0:T(8,128)(2,1)S(1)} %collective-permute-done.4.refs_5_.refs_6_) | copy-start | bytes 688132
  83.6 0.7 copy-start.12
  87.0 1.4 %collective-permute-start.9 = (bf16[16,1024]{1,0:T(8,128)(2,1)}, bf16[16,1024]{1,0:T(8,128)(2,1)S(1)}, u32[]{:S(2)}, u32[]{:S(2)}) collective-permute-start(bf16[16,1024]{1,0:T(8,128)(2,1)} %shard_map.85.own_ref), channel_id=1, source_target_pairs={{0,1},{1,0},{2,3},{3,2},{4,5},{5,4},{6,7},{7,6},{8,9},{9,8},{10,11... | collective-permute-start | bytes 98312 | tf_op jit(solution)/shard_map/ppermute | solution.py:26
  88.4 14.6 %copy-start.15 = (bf16[16,1024]{1,0:T(8,128)(2,1)}, bf16[16,1024]{1,0:T(8,128)(2,1)S(1)}, u32[]{:S(2)}) copy-start(bf16[16,1024]{1,0:T(8,128)(2,1)S(1)} %collective-permute-done.9.near_ref) | copy-start | bytes 98308
  89.2 7.2 %collective-permute-start.10 = (bf16[2,16,1024]{2,1,0:T(8,128)(2,1)S(1)}, bf16[2,16,1024]{2,1,0:T(8,128)(2,1)S(1)}, u32[]{:S(2)}, u32[]{:S(2)}) collective-permute-start(bf16[2,16,1024]{2,1,0:T(8,128)(2,1)S(1)} %pad_maximum_fusion), channel_id=1, source_target_pairs={{0,2},{1,3},{2,0},{3,1},{4,6},{5,7},{6,4},{7,5},{8,10},{9,11},{10,... | collective-permute-start | bytes 196616 | tf_op jit(solution)/shard_map/ppermute | solution.py:26
  89.8 0.8 copy-start.4
  93.1 10.0 %all-to-all-start.1 = ((bf16[8,16,128]{2,1,0:T(8,128)(2,1)}), bf16[8,16,128]{2,1,0:T(8,128)(2,1)S(1)}, u32[]{:S(2)}, u32[]{:S(2)}) async-start(bf16[8,16,128]{2,1,0:T(8,128)(2,1)} %shard_map.80), calls=%async_computation.1 | async-start | bytes 65536 | tf_op jit(solution)/shard_map/all_to_all | solution.py:331
  96.4 6.6 %copy-start.16 = (bf16[2,16,1024]{2,1,0:T(8,128)(2,1)}, bf16[2,16,1024]{2,1,0:T(8,128)(2,1)S(1)}, u32[]{:S(2)}) copy-start(bf16[2,16,1024]{2,1,0:T(8,128)(2,1)S(1)} %collective-permute-done.10.far_ref) | copy-start | bytes 196612
  103.0 0.6 copy-start.14
where the time goes:
time: 123 us; the launch traced here: 122 us
  Pallas kernels  55.2 us (45%)
  waiting for transfers between devices  26.7 us (22%)
  starting transfers between devices  24.6 us (20%)
  local copies, waits for them, and re-layouts  12.9 us (10%)
  other arithmetic  2.68 us (2%)
    pallas_call x14, Pallas kernels, call(): pl.pallas_call(kernel, out_shape=out_shape, scratch_shapes=list(scratch),...  55.2 us
    ppermute x6, waiting for transfers between devices, rotate(): lax.ppermute(shard, axis, [(i, (i + by) % size) for i in range(size)])  14.7 us
    ppermute x6, starting transfers between devices, rotate(): lax.ppermute(shard, axis, [(i, (i + by) % size) for i in range(size)])  11.8 us
    unnamed x36, local copies, waits for them, and re-layouts  7.6 us
    all_to_all x1, starting transfers between devices, body(): lax.all_to_all(packet, 'dom', split_axis=0, concat_axis=0, tiled=True)  7.28 us
    all_to_all x1, waiting for transfers between devices, body(): lax.all_to_all(pool_grad, 'dom', split_axis=0, concat_axis=0, tiled=True)  6.6 us
    ppermute x5, waiting for transfers between devices, swap(): return lax.ppermute(shard, axis, [(i, i ^ bit) for i in range(size)])  5.45 us
    pallas_call x1, local copies, waits for them, and re-layouts, call(): pl.pallas_call(kernel, out_shape=out_shape, scratch_shapes=list(scratch),...  3.93 us
  transfers between devices with their start and end apart: 13, of which 6 were waited for; matrix products, arithmetic and copies ran while one was open for 1% of the time, Pallas kernels for 28%

commit v1 on v0

v1 whole, which is shorter than its diff:
```python
import functools

import jax
import jax.numpy as jnp
from jax import lax
from jax.experimental import pallas as pl
from jax.experimental.pallas import tpu as pltpu
from jax.sharding import PartitionSpec as P

BF16 = jnp.bfloat16
F32 = jnp.float32
I32 = jnp.int32
LANES = 128
PACK = 16
TILE = 256
VMEM_BASE = 9 << 20
VMEM_PER_POOL_ROW = 24 << 10


def rotate(shard, axis, by):
    size = lax.axis_size(axis)
    return lax.ppermute(shard, axis, [(i, (i + by) % size) for i in range(size)])


def swap(shard, axis, bit):
    size = lax.axis_size(axis)
    return lax.ppermute(shard, axis, [(i, i ^ bit) for i in range(size)])


def exchange(first, rest, axis):
    size = 2 * first.shape[0]
    half = size // 2
    parts, origins = (first[None], swap(rest, axis, half)[None]), [0, half]
    while half > 1:
        held = jnp.concatenate(parts, axis=0)
        half //= 2
        parts = (held[:, :half], swap(held[:, half:], axis, half))
        origins = origins + [origin ^ half for origin in origins]
    return parts, tuple(origins)


def struct(*shape, dtype=BF16):
    return jax.ShapeDtypeStruct(shape, dtype)


def hot_rows(count, ids):
    return (lax.broadcasted_iota(I32, (count, ids.shape[1]), 0) == ids).astype(BF16)


def lane_row(block):
    return jnp.concatenate([block[k : k + 1, :] for k in range(block.shape[0])], axis=1)


def lines(array):
    halves, columns, count = array.shape
    cut = array.reshape(halves, columns, count // LANES, LANES)
    return cut.transpose(1, 2, 0, 3).reshape(-1, LANES)


def from_lines(array, halves, columns, count):
    cut = array.reshape(columns, count // LANES, halves, LANES)
    return cut.transpose(2, 0, 1, 3).reshape(halves, columns, count)


def unpack_lines(lines_ref, wide, out_ref):
    pad = out_ref.shape[0] // 2
    chunks = out_ref.shape[1] // LANES
    rows = lines_ref.shape[0]
    columns = rows // (2 * chunks)
    wide[:rows, :] = lines_ref[...].astype(F32)
    for k in range(chunks):
        parts = []
        for half in range(2):
            parts.append(wide[pl.ds(2 * k + half, columns, stride=2 * chunks), :])
            parts.append(jnp.zeros((pad - columns, LANES), F32))
        out_ref[:, k * LANES : (k + 1) * LANES] = jnp.concatenate(parts, axis=0).astype(BF16)


def prepare_kernel(targets_at, pos_ref, ids_ref, served_ref, emb_ref, embp_ref, packet_ref, row_ref, wide, coded):
    height = embp_ref.shape[0]
    me = pos_ref[0]
    edges = ids_ref.shape[1]
    buckets = coded.shape[0]
    for bucket in range(buckets):
        row = targets_at + bucket
        block = jnp.concatenate([ids_ref[row : row + 1, k : k + LANES] for k in range(0, edges, LANES)], axis=0)
        high = lax.shift_right_logical(block, 8)
        coded[bucket] = jnp.concatenate([high, block - high * TILE], axis=0).astype(F32).astype(BF16)
    size = packet_ref.shape[0]
    row_ref[...] = jnp.concatenate([served_ref[k : k + 1, :] for k in range(size)], axis=1)
    unpack_lines(emb_ref, wide, embp_ref)
    fetched = jnp.dot(embp_ref[...], hot_rows(embp_ref.shape[1], row_ref[...]), preferred_element_type=F32)
    fetched = jnp.concatenate([fetched, jnp.zeros((LANES - height, fetched.shape[1]), F32)], axis=0)
    packet_ref[:, :PACK, :] = fetched.T.astype(BF16).reshape(size, PACK, LANES)
    for to in range(size):
        bucket = jnp.minimum(lax.rem(me - to + size, size), buckets - 1)
        packet_ref[to, PACK:, :] = coded[bucket]


def settle_kernel(targets_at, pos_ref, ids_ref, packet_ref, pool_ref, asked_ref):
    me = pos_ref[0]
    size = packet_ref.shape[0]
    pool_ref[...] = packet_ref[:, :PACK, :].reshape(pool_ref.shape)
    asked_ref[0:1, :] = ids_ref[targets_at : targets_at + 1, :]
    for bucket in range(1, asked_ref.shape[0]):
        coded = packet_ref[lax.rem(me + bucket, size), PACK:, :].astype(F32)
        half = coded.shape[0] // 2
        asked_ref[bucket : bucket + 1, :] = lane_row((coded[:half] * float(TILE) + coded[half:]).astype(I32))


def relation_kernel(rel_ref, relp_ref, wide):
    unpack_lines(rel_ref, wide, relp_ref)


def take(rows_ref, ids):
    return jnp.dot(rows_ref[...], hot_rows(rows_ref.shape[1], ids), preferred_element_type=F32)


def make_product(emb_ref, rel_ref, ids_ref, buckets, bucket, product_ref, rows_ref):
    pad = emb_ref.shape[0] // 2
    source = take(emb_ref, ids_ref[bucket : bucket + 1, :])
    rel = take(rel_ref, ids_ref[buckets + bucket : buckets + bucket + 1, :])
    rows_ref[...] = rel.astype(BF16)
    s0, s1, r0, r1 = source[:pad], source[pad:], rel[:pad], rel[pad:]
    product_ref[...] = jnp.concatenate([s0 * r0 - s1 * r1, s0 * r1 + s1 * r0], axis=0).astype(BF16)


def product_kernel(emb_ref, rel_ref, ids_ref, *outs):
    buckets = len(outs) // 2
    for bucket in list(range(1, buckets)) + [0]:
        make_product(emb_ref, rel_ref, ids_ref, buckets, bucket, outs[bucket], outs[buckets + bucket])


def target_kernel(chosen, emb_ref, asked_ref, *refs):
    for bucket, out_ref in zip(chosen, refs[-len(chosen) :]):
        out_ref[...] = take(emb_ref, asked_ref[bucket : bucket + 1, :]).astype(BF16)


def pair_kernel(mine_ref, *refs):
    count = len(refs) // 2
    width = refs[0].shape[1]
    for k in range(count):
        spot = slice(k * width, (k + 1) * width)
        refs[count + k][...] = (mine_ref[:, spot] + refs[k][...].astype(F32)).astype(BF16)


def score_kernel(buckets, pos_ref, pool_ref, *refs):
    products, mine_ref, pieces = refs[:buckets], refs[buckets], refs[buckets + 1 :]
    core = pos_ref[1]
    height, edges = products[0].shape
    per = len(pieces) // (buckets // 2)
    cut = edges // per
    pool = pool_ref[:, :height]
    for bucket in range(buckets):
        half, place = divmod(bucket, buckets // 2)
        scores = jnp.dot(pool, products[bucket][...], preferred_element_type=F32)

        @pl.when(core == half)
        def _():
            mine_ref[:, place * edges : (place + 1) * edges] = scores

        @pl.when(core != half)
        def _():
            for k in range(per):
                pieces[place * per + k][...] = scores[:, k * cut : (k + 1) * cut].astype(BF16)


def slope_kernel(pieces, pos_ref, negatives_ref, *refs):
    out_ref = refs[-1]
    core = pos_ref[1]
    count, width = refs[0].shape
    buckets, spans, negs = negatives_ref.shape
    span_len = width * pieces // (buckets // 2 * spans)
    for place in range(buckets // 2):
        for span in range(spans):
            drawn = negatives_ref[core * (buckets // 2) + place, span : span + 1, :]
            times = jnp.sum(
                (lax.broadcasted_iota(I32, (count, negs), 0) == drawn).astype(F32), axis=1, keepdims=True
            )
            start = (place * spans + span) * span_len
            piece, offset = divmod(start, width)
            spot = slice(offset, offset + span_len)
            scores = refs[piece][:, spot].astype(F32) + refs[pieces + piece][:, spot].astype(F32)
            out_ref[:, start : start + span_len] = (times * jax.nn.sigmoid(scores)).astype(BF16)


def bucket_slopes(core, mine_ref, theirs_ref, bucket, buckets, edges):
    half, place = divmod(bucket, buckets // 2)
    spot = slice(place * edges, (place + 1) * edges)
    return jnp.where(core == half, mine_ref[:, spot], theirs_ref[:, spot])


def pool_grad_kernel(buckets, groups, ring, pos_ref, mine_ref, theirs_ref, pool_ref, *refs):
    held, query_ref = refs[-1], refs[-2]
    outs = refs[-2 - len(groups) : -2]
    core = pos_ref[1]
    height, edges = refs[0].shape
    pool = pool_ref[...].astype(F32).T[:height].astype(BF16)
    total = None
    for bucket in range(buckets):
        slopes = bucket_slopes(core, mine_ref, theirs_ref, bucket, buckets, edges)
        query_ref[:, bucket * edges : (bucket + 1) * edges] = jnp.dot(pool, slopes, preferred_element_type=F32)
        part = lax.dot_general(
            slopes, refs[bucket][...], (((1,), (1,)), ((), ())), preferred_element_type=F32
        )
        total = part if total is None else total + part
    total = jnp.concatenate([total, jnp.zeros((total.shape[0], LANES - height), F32)], axis=1)
    held[...] = total.astype(BF16).reshape(held.shape)
    me = pos_ref[0]
    size = held.shape[0]
    for group, out_ref in zip(groups, outs):
        for k, offset in enumerate(group):
            out_ref[k] = held[lax.rem(me + offset, size) if ring else me ^ offset]


def positive_kernel(*refs):
    out_ref = refs[-1]
    pairs = len(refs) // 2
    rows = []
    for k in range(pairs):
        rows.append(
            jnp.sum(refs[2 * k][...].astype(F32) * refs[2 * k + 1][...].astype(F32), axis=0, keepdims=True)
        )
    rows.append(jnp.zeros((out_ref.shape[0] - pairs, out_ref.shape[1]), F32))
    out_ref[...] = jnp.concatenate(rows, axis=0).astype(BF16)


def scale_kernel(buckets, columns, own_ref, near_ref, far_ref, *refs):
    positive = (
        own_ref[...].astype(F32) + near_ref[...].astype(F32) + far_ref[0].astype(F32) + far_ref[1].astype(F32)
    )
    slope = -jax.nn.sigmoid(-positive)
    last = buckets - 1
    targets, product, riders = refs[:buckets], refs[buckets], refs[buckets + 1 : -buckets - 2]
    slope_ref, outs = refs[-buckets - 2], refs[-buckets - 1 :]
    slope_ref[...] = slope
    for bucket in range(buckets):
        outs[bucket][...] = (slope[bucket : bucket + 1] * targets[bucket][...].astype(F32)).astype(BF16)
    outs[buckets][...] = (slope[last : last + 1] * product[...].astype(F32)).astype(BF16)
    for k, out_ref in enumerate(outs[1:last] + outs[buckets:]):
        if riders:
            value = out_ref[...].astype(F32)
            rows = [value[:columns]]
            for rider in riders:
                block = rider[k].astype(F32)
                rows += [lane_row(block[k : k + 8]) for k in range(0, PACK, 8)]
            rows.append(value[columns + 2 * len(riders) :])
            out_ref[...] = jnp.concatenate(rows, axis=0).astype(BF16)


def rider_blocks(pull_ref, columns, count):
    rows = pull_ref[...].astype(F32)[columns : columns + 2 * count]
    blocks = []
    for at in range(count):
        lines_of = [
            rows[2 * at + part : 2 * at + part + 1, k * LANES : (k + 1) * LANES] for part in range(2) for k in range(8)
        ]
        blocks.append(jnp.concatenate(lines_of, axis=0).astype(BF16))
    return blocks


def source_values(total, relation_ref):
    rel = relation_ref[...].astype(F32)
    pad = rel.shape[0] // 2
    t0, t1, r0, r1 = total[:pad], total[pad:], rel[:pad], rel[pad:]
    return jnp.concatenate([t0 * r0 + t1 * r1, t1 * r0 - t0 * r1], axis=0).astype(BF16)


def write_columns(cols, rows):
    at = 0
    for row in rows:
        for k in range(0, row.shape[1], LANES):
            cols[at : at + LANES, :] = jnp.broadcast_to(row[:, k : k + LANES], (LANES, LANES)).T
            at += LANES


def scattered(values, cols, base):
    lane = lax.broadcasted_iota(I32, cols.shape, 1)
    ids = cols[...]
    hot = jnp.concatenate([(ids == lane + (base + k)).astype(BF16) for k in range(0, TILE, LANES)], axis=1)
    return jnp.dot(values[...], hot, preferred_element_type=F32)


def fill(values, cols, columns_of, rows):
    at = 0
    for value in columns_of:
        values[:, at : at + value.shape[1]] = value
        at += value.shape[1]
    write_columns(cols, rows)


def scatter_all(out_ref, values, cols, held_ref=None):
    for tile in range(out_ref.shape[1] // TILE):
        spot = slice(tile * TILE, (tile + 1) * TILE)
        total = scattered(values, cols, tile * TILE)
        out_ref[:, spot] = total if held_ref is None else total + held_ref[:, spot]


def home_kernel(ids_ref, asked_ref, slope_ref, query_ref, *refs):
    out_ref, values, cols = refs[-3:]
    buckets, edges = asked_ref.shape
    last = buckets - 1
    products, pulls, relation_rows = refs[:last], refs[last : last + 2], refs[last + 2 : last + 4]
    columns_of = [
        (slope_ref[bucket : bucket + 1] * products[bucket][...].astype(F32)).astype(BF16) for bucket in range(last)
    ]
    rows = [asked_ref[bucket : bucket + 1, :] for bucket in range(last)]
    for bucket, pull, rel in zip((0, last), pulls, relation_rows):
        query = query_ref[:, bucket * edges : (bucket + 1) * edges]
        columns_of.append(source_values(pull[...].astype(F32) + query, rel))
        rows.append(ids_ref[bucket : bucket + 1, :])
    fill(values, cols, columns_of, rows)
    scatter_all(out_ref, values, cols)


def middle_kernel(ids_ref, query_ref, *refs):
    held_ref, out_ref, values, cols = refs[-4:]
    count = (len(refs) - 4) // 2
    relation_rows, pulls = refs[:count], refs[count : 2 * count]
    edges = pulls[0].shape[1]
    columns_of, rows = [], []
    for k in range(count):
        query = query_ref[:, (k + 1) * edges : (k + 2) * edges]
        columns_of.append(source_values(pulls[k][...].astype(F32) + query, relation_rows[k]))
        rows.append(ids_ref[k + 1 : k + 2, :])
    fill(values, cols, columns_of, rows)
    scatter_all(out_ref, values, cols, held_ref)


def final_kernel(plan, origins, pos_ref, asked_ref, served_ref, push_ref, *refs):
    held_ref, out_ref, values, cols, back = refs[-5:]
    buckets, edges = asked_ref.shape
    others = refs[:-5]
    step = pl.program_id(0)
    height = push_ref.shape[0]
    pad = height // 2
    columns, lines_here, _ = out_ref.shape
    flat = out_ref.reshape(columns * lines_here, LANES)

    @pl.when(step == 0)
    def _():
        me = pos_ref[0]
        size = back.shape[0]
        if plan is not None:
            carriers, hop, left = plan
            pulls, home, direct = others[: len(carriers) - 1], others[len(carriers) - 1], others[len(carriers) :]
            back[me] = home[0]
            for carrier, ref in zip(carriers, (*pulls, push_ref)):
                for block, way in zip(rider_blocks(ref, columns, 2), (carrier, carrier + hop)):
                    back[lax.rem(me + 2 * size - way, size)] = block
            for way, ref in zip(left, direct):
                back[lax.rem(me + size - way, size)] = ref[0]
        else:
            blocks = [part[k, 0] for part in others for k in range(part.shape[0])]
            for origin, block in zip(origins, blocks):
                back[me ^ origin] = block
        returned = back[...].reshape(-1, LANES).astype(F32).T[:height].astype(BF16)
        fill(values, cols, [push_ref[...], returned], [asked_ref[buckets - 1 : buckets, :], served_ref[...]])

    tiles = lines_here * LANES // (2 * TILE)
    for tile in range(tiles):
        spot = slice(tile * TILE, (tile + 1) * TILE)
        total = scattered(values, cols, (step * tiles + tile) * TILE) + held_ref[:, spot]
        for k in range(TILE // LANES):
            for half in range(2):
                row = 2 * (tile * (TILE // LANES) + k) + half
                flat[pl.ds(row, columns, stride=lines_here), :] = total[
                    half * pad : half * pad + columns, k * LANES : (k + 1) * LANES
                ]


def body(embeddings, relations, source_ids, relation_ids, target_ids, negative_ids, served_rows):
    halves, columns, entities = embeddings.shape
    buckets, edges = source_ids.shape
    relation_count = relations.shape[2]
    size = lax.axis_size("dom")
    height = -(-columns // 8) * 16
    pool_count = served_rows.size
    position = jnp.stack([lax.axis_index("dom"), lax.axis_index("col") & 1]).astype(I32)
    smem = pl.BlockSpec(memory_space=pltpu.SMEM)
    vmem = pl.BlockSpec(memory_space=pltpu.VMEM)
    anywhere = pl.BlockSpec(memory_space=pl.ANY)
    packet_rows = PACK + 2 * edges // LANES
    limit = VMEM_BASE + pool_count * VMEM_PER_POOL_ROW

    def local(kernel, out, *args, scratch=(), flops=0, grid=None, out_specs=None, specs=None):
        outs = out if isinstance(out, tuple) else (out,)
        chosen = [smem if a is position else vmem for a in args]
        for place, spec in (specs or {}).items():
            chosen[place] = spec
        extra = {} if grid is None else {"grid": grid}
        return pl.pallas_call(
            kernel,
            out_shape=out,
            in_specs=chosen,
            out_specs=jax.tree.map(lambda _: vmem, out) if out_specs is None else out_specs,
            scratch_shapes=list(scratch),
            compiler_params=pltpu.CompilerParams(vmem_limit_bytes=limit),
            cost_estimate=pl.CostEstimate(
                flops=int(flops),
                bytes_accessed=int(sum(a.size * a.dtype.itemsize for a in args + outs)),
                transcendentals=0,
            ),
            **extra,
        )(*args)

    edge_rows = struct(height, edges)
    gather_flops = 2 * LANES * entities * edges
    ids = jnp.concatenate([source_ids, relation_ids, target_ids], axis=0)
    emb_lines, rel_lines = lines(embeddings), lines(relations)
    emb, packet, served = local(
        functools.partial(prepare_kernel, 2 * buckets),
        (struct(height, entities), struct(size, packet_rows, LANES), struct(1, pool_count, dtype=I32)),
        position, ids, served_rows, emb_lines,
        scratch=(
            pltpu.VMEM(emb_lines.shape, F32),
            pltpu.VMEM((buckets, packet_rows - PACK, LANES), BF16),
        ),
        flops=2 * LANES * entities * pool_count,
    )
    packet = lax.all_to_all(packet, "dom", split_axis=0, concat_axis=0, tiled=True)
    pool, asked = local(
        functools.partial(settle_kernel, 2 * buckets),
        (struct(pool_count, LANES), struct(buckets, edges, dtype=I32)),
        position, ids, packet,
    )
    rel = local(
        relation_kernel, struct(height, relation_count), rel_lines, scratch=(pltpu.VMEM(rel_lines.shape, F32),)
    )
    made = local(product_kernel, (edge_rows,) * (2 * buckets), emb, rel, ids, flops=gather_flops * buckets)
    products, relation_rows = made[:buckets], made[buckets:]
    last = buckets - 1

    def take_targets(chosen, *after):
        return local(
            functools.partial(target_kernel, chosen), (edge_rows,) * len(chosen), emb, asked, *after,
            specs={2 + k: anywhere for k in range(len(after))},
            flops=gather_flops * len(chosen),
        )

    owned_products = [products[0]] + [rotate(products[b], "dom", -b) for b in range(1, last)]
    (last_target,) = take_targets((last,))
    last_target = rotate(last_target, "dom", last)
    width = buckets // 2 * edges
    pieces = 4
    piece = struct(pool_count, width // pieces)
    mine, *theirs = local(
        functools.partial(score_kernel, buckets),
        (struct(pool_count, width, dtype=F32),) + (piece,) * pieces,
        position, pool, *products,
        flops=2 * LANES * pool_count * edges * buckets,
    )
    pair = local(pair_kernel, (piece,) * pieces, mine, *[swap(part, "col", 1) for part in theirs])
    targets = [*take_targets(tuple(range(last))), last_target]
    after = [targets[0], *owned_products[1:], last_target]
    slopes_mine = local(
        functools.partial(slope_kernel, pieces), struct(pool_count, width),
        position, negative_ids, *pair, *[swap(part, "col", 2) for part in pair], *after,
        specs={2 + 2 * pieces + k: anywhere for k in range(len(after))},
    )
    slopes_theirs = swap(slopes_mine, "col", 1)
    pairs = [x for b in range(last) for x in (owned_products[b], targets[b])] + [products[last], last_target]
    own = local(positive_kernel, struct(PACK, edges), *pairs)
    near = swap(own, "col", 1)
    far = swap(jnp.stack([own, near]), "col", 2)
    plan = None
    groups = [list(range(size // 2)), list(range(size // 2, size))]
    if size == 2 * buckets and columns + 4 <= height // 2:
        carriers = [*range(1, last), size - last]

        def left_of(hop):
            return sorted(set(range(1, size)) - set(carriers) - {(hop + c) % size for c in carriers})

        hop = min(range(1, size), key=lambda h: len(left_of(h)))
        plan = (tuple(carriers), hop, tuple(left_of(hop)))
        groups = [[0], carriers, [hop + c for c in carriers]] + [[way] for way in left_of(hop)]
    *sent, query = local(
        functools.partial(pool_grad_kernel, buckets, groups, plan is not None),
        tuple(struct(len(group), PACK, LANES) for group in groups)
        + (struct(height, buckets * edges, dtype=F32),),
        position, slopes_mine, slopes_theirs, pool, *products,
        scratch=(pltpu.VMEM((size, PACK, LANES), BF16),),
        flops=4 * LANES * pool_count * edges * buckets,
    )
    if plan is None:
        riders, origins = (), None
        parts, origins = exchange(*sent, "dom")
    else:
        riders, origins = (sent[1], rotate(sent[2], "dom", hop)), None
        direct = [rotate(block, "dom", way) for way, block in zip(plan[2], sent[3:])]
    slope, *scaled = local(
        functools.partial(scale_kernel, buckets, columns),
        (struct(PACK, edges, dtype=F32),) + (edge_rows,) * (buckets + 1),
        own, near, far, *targets, products[last], *riders,
    )
    pulls = [rotate(scaled[b], "dom", b) for b in range(1, last)]
    push = rotate(scaled[buckets], "dom", -last)
    if plan is not None:
        parts = (*pulls, sent[0], *direct)
    count = (buckets + 1) * edges
    held = local(
        home_kernel,
        struct(height, entities, dtype=F32),
        ids, asked, slope, query, *owned_products, scaled[0], scaled[last], relation_rows[0], relation_rows[last],
        scratch=(pltpu.VMEM((height, count), BF16), pltpu.VMEM((count, LANES), I32)),
    )
    count = (last - 1) * edges
    held = local(
        middle_kernel,
        struct(height, entities, dtype=F32),
        ids, query, *relation_rows[1:last], *pulls, held,
        scratch=(pltpu.VMEM((height, count), BF16), pltpu.VMEM((count, LANES), I32)),
        flops=2 * LANES * count * entities,
    )
    steps = 4
    count = edges + pool_count
    args = [position, asked, served, push, *parts, held]
    grad = local(
        functools.partial(final_kernel, plan, origins),
        struct(columns, 2 * entities // LANES, LANES, dtype=F32),
        *args,
        grid=(steps,),
        specs={len(args) - 1: pl.BlockSpec((height, entities // steps), lambda i: (0, i))},
        out_specs=pl.BlockSpec((columns, 2 * entities // LANES // steps, LANES), lambda i: (0, i, 0)),
        scratch=(
            pltpu.VMEM((height, count), BF16),
            pltpu.VMEM((count, LANES), I32),
            pltpu.VMEM((size, PACK, LANES), BF16),
        ),
        flops=2 * LANES * count * entities,
    )
    return from_lines(grad, halves, columns, entities)


def solution(mesh):
    placed = (
        P(None, "col", "dom"),
        P(None, "col", None),
        P(None, "dom"),
        P(None, "dom"),
        P(None, "dom"),
        P(None, "dom", None),
        P("dom", None),
    )
    return jax.shard_map(
        body, mesh=mesh, in_specs=placed, out_specs=P(None, "col", "dom"), check_vma=False
    )
```

time: 123 us -> 78.5 us (0.64)
  Pallas kernels: 55.2 us -> 32.2 us
  waiting for transfers between devices: 26.7 us -> 14.2 us
  local copies, waits for them, and re-layouts: 12.9 us -> 2.72 us
  starting transfers between devices: 24.6 us -> 28 us
  other arithmetic: 2.68 us -> 0.85 us
    pallas_call x14 -> x15, Pallas kernels: 55.2 us -> 32.2 us  [local(): pl.pallas_call(kernel, out_shape=out, in_specs=chosen, out_specs=jax.tree...]
    all_to_all x1 -> x0, waiting for transfers between devices: 6.6 us -> none  [body(): lax.all_to_all(pool_grad, 'dom', split_axis=0, concat_axis=0, tiled=True)]
    ppermute x5 -> x11, starting transfers between devices: 2.18 us -> 7.76 us  [swap(): return lax.ppermute(shard, axis, [(i, i ^ bit) for i in range(size)])]
    unnamed x36 -> x8, local copies, waits for them, and re-layouts: 7.6 us -> 2.72 us
    ppermute x5 -> x11, waiting for transfers between devices: 5.45 us -> 1.5 us  [swap(): return lax.ppermute(shard, axis, [(i, i ^ bit) for i in range(size)])]
    pallas_call x1 -> x0, local copies, waits for them, and re-layouts: 3.93 us -> none  [call(): pl.pallas_call(kernel, out_shape=out_shape, scratch_shapes=list(scratch),...]
    all_to_all x1 -> x0, starting transfers between devices: 3.33 us -> none  [body(): lax.all_to_all(pool_grad, 'dom', split_axis=0, concat_axis=0, tiled=True)]
    ppermute x6 -> x8, waiting for transfers between devices: 14.7 us -> 12.7 us  [rotate(): lax.ppermute(shard, axis, [(i, (i + by) % size) for i in range(size)])]
  transfers between devices with their start and end apart: 13 -> 20, of which waited for: 6 -> 7; matrix products, arithmetic and copies ran while one was open for 1% -> 0% of each run, Pallas kernels for 28% -> 28%
where the time goes in v1:
time: 78.5 us; the launch traced here: 78.1 us
  Pallas kernels  32.2 us (41%)
  starting transfers between devices  28 us (36%)
  waiting for transfers between devices  14.2 us (18%)
  local copies, waits for them, and re-layouts  2.72 us (3%)
  other arithmetic  0.85 us (1%)
    pallas_call x15, Pallas kernels, local(): pl.pallas_call(kernel, out_shape=out, in_specs=chosen, out_specs=jax.tree...  32.2 us
    ppermute x8, starting transfers between devices, rotate(): lax.ppermute(shard, axis, [(i, (i + by) % size) for i in range(size)])  12.9 us
    ppermute x8, waiting for transfers between devices, rotate(): lax.ppermute(shard, axis, [(i, (i + by) % size) for i in range(size)])  12.7 us
    ppermute x11, starting transfers between devices, swap(): return lax.ppermute(shard, axis, [(i, i ^ bit) for i in range(size)])  7.76 us
    all_to_all x1, starting transfers between devices, body(): lax.all_to_all(packet, 'dom', split_axis=0, concat_axis=0, tiled=True)  7.28 us
    unnamed x8, local copies, waits for them, and re-layouts  2.72 us
  transfers between devices with their start and end apart: 20, of which 7 were waited for; matrix products, arithmetic and copies ran while one was open for 0% of the time, Pallas kernels for 28%

profile of v1, /device:TPU:0, one launch (start us, length us, event | category | flops | bytes accessed | tf_op | source)
XLA Modules:
  0.0 78.1 jit_solution(12428084090753410243)
XLA Ops:
  0.0 0.1 pad_add_fusion.1.pos_ref
  0.1 0.8 pad_add_fusion.ids_ref
  0.8 0.0 copy-start
  0.9 1.1 %copy-done = bf16[2,50,4096]{2,0,1:T(2,128)(2,1)S(1)} copy-done((bf16[2,50,4096]{2,0,1:T(2,128)(2,1)S(1)}, bf16[2,50,4096]{2,0,1:T(2,128)(2,1)}, u32[]{:S(2)}) %copy-start) | copy-done | bytes 819224
  2.0 0.0 copy-start.3
  2.0 0.7 copy-done.3
  2.7 2.8 %shard_map.73 = (bf16[112,4096]{1,0:T(8,128)(2,1)S(1)}, bf16[8,32,128]{2,1,0:T(8,128)(2,1)}, s32[1,128]{1,0:T(1,128)S(1)}) custom-call(s32[2]{0:T(128)S(1)} %pad_add_fusion.1.pos_ref, s32[12,1024]{1,0:T(8,128)S(1)} %pad_add_fusion.ids_ref, s32[8,16]{1,0:T(8,128)S(1)} %copy-done.3, bf16[3200,128]{1,0:T(8,128)(2,1)S(1)} %bitcast.19), custom_call_target="tpu_custom_call" | custom-call | flops 134217728 | bytes 1852424 | tf_op jit(solution)/shard_map/pallas_call | solution.py:392
  5.5 7.3 %all-to-all-start = ((bf16[8,32,128]{2,1,0:T(8,128)(2,1)}), bf16[8,32,128]{2,1,0:T(8,128)(2,1)S(1)}, u32[]{:S(2)}, u32[]{:S(2)}) async-start(bf16[8,32,128]{2,1,0:T(8,128)(2,1)} %get-tuple-element.41), calls=%async_computation | async-start | bytes 131072 | tf_op jit(solution)/shard_map/all_to_all | solution.py:421
  12.8 0.0 copy-start.1
  12.8 0.9 %copy-done.1 = bf16[2,50,512]{2,0,1:T(2,128)(2,1)S(1)} copy-done((bf16[2,50,512]{2,0,1:T(2,128)(2,1)S(1)}, bf16[2,50,512]{2,0,1:T(2,128)(2,1)}, u32[]{:S(2)}) %copy-start.1) | copy-done | bytes 102424
  13.7 0.1 shard_map.75.rel_ref
  13.7 6.3 %shard_map.76 = (bf16[112,1024]{1,0:T(8,128)(2,1)S(1)}, bf16[112,1024]{1,0:T(8,128)(2,1)S(1)}, bf16[112,1024]{1,0:T(8,128)(2,1)S(1)}, bf16[112,1024]{1,0:T(8,128...) custom-call(bf16[112,4096]{1,0:T(8,128)(2,1)S(1)} %get-tuple-element, ...), custom_call_target="tpu_custom_call" | custom-call | flops 4294967296 | bytes 2916352 | tf_op jit(solution)/shard_map/pallas_call | solution.py:392
  20.0 0.0 all-to-all-done.packet_ref
  20.0 0.6 shard_map.74
  20.6 1.4 %shard_map.80 = (f32[128,2048]{1,0:T(8,128)S(1)}, bf16[128,512]{1,0:T(8,128)(2,1)S(1)}, bf16[128,512]{1,0:T(8,128)(2,1)S(1)}, bf16[128,512]{1,0:T(8,128)(2,1)S(1)}, bf16[128,512]{1,0:T(8,128)(2,1)S(1)}) custom-call(s32[2]{0:T(128)S(1)} %pad_add_fusion.1.pos_ref, bf16[128,128]{1,0:T(8,128)(2,1)S(1)} %get-tuple-element.52.pool_ref, ...), custom_call_target="tpu_custom_call" | custom-call | flops 134217728 | bytes 2523144 | tf_op jit(solution)/shard_map/pallas_call | solution.py:392
  22.0 0.1 collective-permute-start.5
  22.1 4.8 %collective-permute-start = (bf16[112,1024]{1,0:T(8,128)(2,1)S(1)}, bf16[112,1024]{1,0:T(8,128)(2,1)S(1)}, u32[]{:S(2)}, u32[]{:S(2)}) collective-permute-start(bf16[112,1024]{1,0:T(8,128)(2,1)S(1)} %get-tuple-element.47.refs_1_), channel_id=1, source_target_pairs={{0,28},{4,0},{8,4},{12,8},{16,12},{20,16},{24,20},{28,24},{1,29},{... | collective-permute-start | bytes 688136 | tf_op jit(solution)/shard_map/ppermute | solution.py:22
  26.9 0.6 collective-permute-start.1
  27.5 0.0 collective-permute-start.6
  27.5 0.5 collective-permute-start.7
  28.0 0.0 collective-permute-done.5.refs_0_
  28.0 0.0 collective-permute-start.8
  28.0 1.3 %shard_map.78 = bf16[112,1024]{1,0:T(8,128)(2,1)S(1)} custom-call(bf16[112,4096]{1,0:T(8,128)(2,1)S(1)} %get-tuple-element.44.emb_ref, s32[4,1024]{1,0:T(4,128)S(1)} %get-tuple-element.42.asked_ref), custom_call_target="tpu_custom_call" | custom-call | flops 1073741824 | bytes 1163264 | tf_op jit(solution)/shard_map/pallas_call | solution.py:392
  29.3 0.0 collective-permute-done.6.refs_1_
  29.3 0.2 collective-permute-start.2
  29.6 0.0 collective-permute-done.7.refs_2_
  29.6 0.0 collective-permute-done.8.refs_3_
  29.6 0.1 shard_map.81
  29.7 1.5 %collective-permute-start.9 = (bf16[128,512]{1,0:T(8,128)(2,1)S(1)}, bf16[128,512]{1,0:T(8,128)(2,1)S(1)}, u32[]{:S(2)}, u32[]{:S(2)}) collective-permute-start(bf16[128,512]{1,0:T(8,128)(2,1)S(1)} %get-tuple-element.58.refs_0_), channel_id=1, source_target_pairs={{0,2},{1,3},{2,0},{3,1},{4,6},{5,7},{6,4},{7,5},{8,10},{9,11},{10,... | collective-permute-start | bytes 393224 | tf_op jit(solution)/shard_map/ppermute | solution.py:27
  31.2 0.6 collective-permute-start.10
  31.8 1.1 %collective-permute-done.refs_2_.refs_9_.refs_1_ = bf16[112,1024]{1,0:T(8,128)(2,1)S(1)} collective-permute-done((bf16[112,1024]{1,0:T(8,128)(2,1)S(1)}, bf16[112,1024]{1,0:T(8,128)(2,1)S(1)}, u32[]{:S(2)}, u32[]{:S(2)}) %collective-permute-start) | collective-permute-done | bytes 229408 | tf_op jit(solution)/shard_map/ppermute | solution.py:22
  32.9 1.5 %collective-permute-start.11 = (bf16[128,512]{1,0:T(8,128)(2,1)S(1)}, bf16[128,512]{1,0:T(8,128)(2,1)S(1)}, u32[]{:S(2)}, u32[]{:S(2)}) collective-permute-start(bf16[128,512]{1,0:T(8,128)(2,1)S(1)} %get-tuple-element.60.refs_2_), channel_id=1, source_target_pairs={{0,2},{1,3},{2,0},{3,1},{4,6},{5,7},{6,4},{7,5},{8,10},{9,11},{10,... | collective-permute-start | bytes 393224 | tf_op jit(solution)/shard_map/ppermute | solution.py:27
  34.4 3.4 %collective-permute-done.1.refs_4_.refs_10_.refs_2_ = bf16[112,1024]{1,0:T(8,128)(2,1)S(1)} collective-permute-done((bf16[112,1024]{1,0:T(8,128)(2,1)S(1)}, bf16[112,1024]{1,0:T(8,128)(2,1)S(1)}, u32[]{:S(2)}, u32[]{:S(2)}) %collective-permute-start.1) | collective-permute-done | bytes 229408 | tf_op jit(solution)/shard_map/ppermute | solution.py:22
  37.8 1.5 %collective-permute-start.12 = (bf16[128,512]{1,0:T(8,128)(2,1)S(1)}, bf16[128,512]{1,0:T(8,128)(2,1)S(1)}, u32[]{:S(2)}, u32[]{:S(2)}) collective-permute-start(bf16[128,512]{1,0:T(8,128)(2,1)S(1)} %get-tuple-element.61.refs_3_), channel_id=1, source_target_pairs={{0,2},{1,3},{2,0},{3,1},{4,6},{5,7},{6,4},{7,5},{8,10},{9,11},{10,... | collective-permute-start | bytes 393224 | tf_op jit(solution)/shard_map/ppermute | solution.py:27
  39.3 3.7 %shard_map.77 = (bf16[112,1024]{1,0:T(8,128)(2,1)S(1)}, bf16[112,1024]{1,0:T(8,128)(2,1)S(1)}, bf16[112,1024]{1,0:T(8,128)(2,1)S(1)}) custom-call(bf16[112,4096]{1,0:T(8,128)(2,1)S(1)} %get-tuple-element.44.emb_ref, s32[4,1024]{1,0:T(4,128)S(1)} %get-tuple-element.42.asked_ref), custom_call_target="tpu_custom_call" | custom-call | flops 3221225472 | bytes 1622016 | tf_op jit(solution)/shard_map/pallas_call | solution.py:392
  43.0 1.3 %collective-permute-done.2.refs_7_.refs_11_.refs_3_ = bf16[112,1024]{1,0:T(8,128)(2,1)S(1)} collective-permute-done((bf16[112,1024]{1,0:T(8,128)(2,1)S(1)}, bf16[112,1024]{1,0:T(8,128)(2,1)S(1)}, u32[]{:S(2)}, u32[]{:S(2)}) %collective-permute-start.2) | collective-permute-done | bytes 229408 | tf_op jit(solution)/shard_map/ppermute | solution.py:22
  44.3 0.0 collective-permute-done.9.refs_4_
  44.3 0.0 collective-permute-done.10.refs_5_
  44.3 0.0 collective-permute-done.11.refs_6_
  44.3 0.0 collective-permute-done.12.refs_7_
  44.3 0.0 copy-done.2
  44.3 0.9 %shard_map.82.mine_ref = bf16[128,2048]{1,0:T(8,128)(2,1)S(1)} custom-call(s32[2]{0:T(128)S(1)} %pad_add_fusion.1.pos_ref, s32[4,4,256]{2,1,0:T(4,128)S(1)} %copy-done.2, bf16[128,512]{1,0:T(8,128)(2,1)S(1)} %get-tuple-element.58.refs_0_, bf16[128,512]{1,0:T(8,128)(2,1)S(1)} %get-tuple-element.59.refs_1_, bf16[128,512]{1,0:T(8,128)(2,1)S(1)} %get-tuple-element.60.refs_2_, ...), custom_call_target="tpu_custom_call" | custom-call | bytes 2506760 | tf_op jit(solution)/shard_map/pallas_call | solution.py:392
  45.2 0.1 collective-permute-start.13
  45.3 0.1 shard_map.79.own_ref
  45.4 0.6 collective-permute-start.3
  46.0 1.2 %collective-permute-done.3.near_ref = bf16[16,1024]{1,0:T(8,128)(2,1)S(1)} collective-permute-done((bf16[16,1024]{1,0:T(8,128)(2,1)S(1)}, bf16[16,1024]{1,0:T(8,128)(2,1)S(1)}, u32[]{:S(2)}, u32[]{:S(2)}) %collective-permute-start.3) | collective-permute-done | bytes 32800 | tf_op jit(solution)/shard_map/ppermute | solution.py:27
  47.2 1.5 %collective-permute-start.4 = (bf16[2,16,1024]{2,1,0:T(8,128)(2,1)S(1)}, bf16[2,16,1024]{2,1,0:T(8,128)(2,1)S(1)}, u32[]{:S(2)}, u32[]{:S(2)}) collective-permute-start(bf16[2,16,1024]{2,1,0:T(8,128)(2,1)S(1)} %pad_maximum_fusion), channel_id=1, source_target_pairs={{0,2},{1,3},{2,0},{3,1},{4,6},{5,7},{6,4},{7,5},{8,10},{9,11},{10,... | collective-permute-start | bytes 196616 | tf_op jit(solution)/shard_map/ppermute | solution.py:27
  48.7 0.0 collective-permute-done.13.theirs_ref
  48.7 1.3 %shard_map.83 = (bf16[1,16,128]{2,1,0:T(8,128)(2,1)S(1)}, bf16[3,16,128]{2,1,0:T(8,128)(2,1)S(1)}, bf16[3,16,128]{2,1,0:T(8,128)(2,1)S(1)}, bf16[1,16,128]{2,1,0:T(8,128)(2,1)S(1)}, f32[112,4096]{1,0:T(8,128)S(1)}) custom-call(s32[2]{0:T(128)S(1)} %pad_add_fusion.1.pos_ref, bf16[128,2048]{1,0:T(8,128)(2,1)S(1)} %shard_map.82.mine_ref, ...), custom_call_target="tpu_custom_call" | custom-call | flops 268435456 | bytes 3866632 | tf_op jit(solution)/shard_map/pallas_call | solution.py:392
  50.0 1.3 %collective-permute-start.14 = (bf16[3,16,128]{2,1,0:T(8,128)(2,1)S(1)}, bf16[3,16,128]{2,1,0:T(8,128)(2,1)S(1)}, u32[]{:S(2)}, u32[]{:S(2)}) collective-permute-start(bf16[3,16,128]{2,1,0:T(8,128)(2,1)S(1)} %get-tuple-element.63), channel_id=1, source_target_pairs={{0,8},{4,12},{8,16},{12,20},{16,24},{20,28},{24,0},{28,4},{1,9},{5... | collective-permute-start | bytes 36872 | tf_op jit(solution)/shard_map/ppermute | solution.py:22
  51.3 0.2 collective-permute-done.4.far_ref
  51.5 4.0 %collective-permute-done.14.refs_6_ = bf16[3,16,128]{2,1,0:T(8,128)(2,1)S(1)} collective-permute-done((bf16[3,16,128]{2,1,0:T(8,128)(2,1)S(1)}, bf16[3,16,128]{2,1,0:T(8,128)(2,1)S(1)}, u32[]{:S(2)}, u32[]{:S(2)}) %collective-permute-start.14) | collective-permute-done | bytes 12320 | tf_op jit(solution)/shard_map/ppermute | solution.py:22
  55.6 0.4 shard_map.84
  55.9 1.0 %collective-permute-start.16 = (bf16[112,1024]{1,0:T(8,128)(2,1)S(1)}, bf16[112,1024]{1,0:T(8,128)(2,1)S(1)}, u32[]{:S(2)}, u32[]{:S(2)}) collective-permute-start(bf16[112,1024]{1,0:T(8,128)(2,1)S(1)} %get-tuple-element.65), channel_id=1, source_target_pairs={{0,4},{4,8},{8,12},{12,16},{16,20},{20,24},{24,28},{28,0},{1,5},{5... | collective-permute-start | bytes 688136 | tf_op jit(solution)/shard_map/ppermute | solution.py:22
  56.9 0.0 collective-permute-start.17
  56.9 4.3 %collective-permute-start.15 = (bf16[112,1024]{1,0:T(8,128)(2,1)S(1)}, bf16[112,1024]{1,0:T(8,128)(2,1)S(1)}, u32[]{:S(2)}, u32[]{:S(2)}) collective-permute-start(bf16[112,1024]{1,0:T(8,128)(2,1)S(1)} %get-tuple-element.64), channel_id=1, source_target_pairs={{0,20},{4,24},{8,28},{12,0},{16,4},{20,8},{24,12},{28,16},{1,21},{... | collective-permute-start | bytes 688136 | tf_op jit(solution)/shard_map/ppermute | solution.py:22
  61.3 0.6 collective-permute-start.18
  61.9 6.3 %shard_map.85.refs_4_ = f32[112,4096]{1,0:T(8,128)S(1)} custom-call(s32[12,1024]{1,0:T(8,128)S(1)} %pad_add_fusion.ids_ref, s32[4,1024]{1,0:T(4,128)S(1)} %get-tuple-element.42.asked_ref, f32[16,1024]{1,0:T(8,128)S(1)} %get-tuple-element.72.slope_ref, f32[112,4096]{1,0:T(8,128)S(1)} %get-tuple-element.69.query_ref, ...), custom_call_target="tpu_custom_call" | custom-call | bytes 5406720 | tf_op jit(solution)/shard_map/pallas_call | solution.py:392
  68.2 0.0 collective-permute-done.16.refs_2_.refs_0_
  68.2 0.0 collective-permute-done.17.refs_3_.refs_1_
  68.2 2.8 %shard_map.86.refs_4_ = f32[112,4096]{1,0:T(8,128)S(1)} custom-call(s32[12,1024]{1,0:T(8,128)S(1)} %pad_add_fusion.ids_ref, f32[112,4096]{1,0:T(8,128)S(1)} %get-tuple-element.69.query_ref, bf16[112,1024]{1,0:T(8,128)(2,1)S(1)} %get-tuple-element.70.refs_0_, bf16[112,1024]{1,0:T(8,128)(2,1)S(1)} %get-tuple-element.71.refs_1_, ...), custom_call_target="tpu_custom_call" | custom-call | flops 2147483648 | bytes 6471680 | tf_op jit(solution)/shard_map/pallas_call | solution.py:392
  71.0 0.0 collective-permute-done.18.refs_3_
  71.1 2.8 %collective-permute-done.15.push_ref = bf16[112,1024]{1,0:T(8,128)(2,1)S(1)} collective-permute-done((bf16[112,1024]{1,0:T(8,128)(2,1)S(1)}, bf16[112,1024]{1,0:T(8,128)(2,1)S(1)}, u32[]{:S(2)}, u32[]{:S(2)}) %collective-permute-start.15) | collective-permute-done | bytes 229408 | tf_op jit(solution)/shard_map/ppermute | solution.py:22
  73.9 4.2 %shard_map.87 = f32[50,64,128]{2,1,0:T(8,128)} custom-call(s32[2]{0:T(128)S(1)} %pad_add_fusion.1.pos_ref, s32[4,1024]{1,0:T(4,128)S(1)} %get-tuple-element.42.asked_ref, s32[1,128]{1,0:T(1,128)S(1)} %get-tuple-element.43.served_ref, bf16[112,1024]{1,0:T(8,128)(2,1)S(1)} %collective-permute-done.15.push_ref, ...), custom_call_target="tpu_custom_call" | custom-call | flops 1207959552 | bytes 4186632 | tf_op jit(solution)/shard_map/pallas_call | solution.py:392
  (2 shorter events, 0.0 us)
Async XLA Ops:
  0.8 1.1 %copy-start = (bf16[2,50,4096]{2,0,1:T(2,128)(2,1)S(1)}, bf16[2,50,4096]{2,0,1:T(2,128)(2,1)}, u32[]{:S(2)}) copy-start(bf16[2,50,4096]{2,0,1:T(2,128)(2,1)} %param.7) | copy-start | bytes 2457604
  2.0 0.7 copy-start.3
  5.5 14.5 %all-to-all-start = ((bf16[8,32,128]{2,1,0:T(8,128)(2,1)}), bf16[8,32,128]{2,1,0:T(8,128)(2,1)S(1)}, u32[]{:S(2)}, u32[]{:S(2)}) async-start(bf16[8,32,128]{2,1,0:T(8,128)(2,1)} %get-tuple-element.41), calls=%async_computation | async-start | bytes 131072 | tf_op jit(solution)/shard_map/all_to_all | solution.py:421
  12.8 0.9 %copy-start.1 = (bf16[2,50,512]{2,0,1:T(2,128)(2,1)S(1)}, bf16[2,50,512]{2,0,1:T(2,128)(2,1)}, u32[]{:S(2)}) copy-start(bf16[2,50,512]{2,0,1:T(2,128)(2,1)} %param.8) | copy-start | bytes 307204
  22.0 6.0 %collective-permute-start.5 = (bf16[128,512]{1,0:T(8,128)(2,1)S(1)}, bf16[128,512]{1,0:T(8,128)(2,1)S(1)}, u32[]{:S(2)}, u32[]{:S(2)}) collective-permute-start(bf16[128,512]{1,0:T(8,128)(2,1)S(1)} %get-tuple-element.54), channel_id=1, source_target_pairs={{0,1},{1,0},{2,3},{3,2},{4,5},{5,4},{6,7},{7,6},{8,9},{9,8},{10,11... | collective-permute-start | bytes 393224 | tf_op jit(solution)/shard_map/ppermute | solution.py:27
  22.1 10.8 %collective-permute-start = (bf16[112,1024]{1,0:T(8,128)(2,1)S(1)}, bf16[112,1024]{1,0:T(8,128)(2,1)S(1)}, u32[]{:S(2)}, u32[]{:S(2)}) collective-permute-start(bf16[112,1024]{1,0:T(8,128)(2,1)S(1)} %get-tuple-element.47.refs_1_), channel_id=1, source_target_pairs={{0,28},{4,0},{8,4},{12,8},{16,12},{20,16},{24,20},{28,24},{1,29},{... | collective-permute-start | bytes 688136 | tf_op jit(solution)/shard_map/ppermute | solution.py:22
  26.9 10.9 %collective-permute-start.1 = (bf16[112,1024]{1,0:T(8,128)(2,1)S(1)}, bf16[112,1024]{1,0:T(8,128)(2,1)S(1)}, u32[]{:S(2)}, u32[]{:S(2)}) collective-permute-start(bf16[112,1024]{1,0:T(8,128)(2,1)S(1)} %get-tuple-element.49.refs_2_), channel_id=1, source_target_pairs={{0,24},{4,28},{8,0},{12,4},{16,8},{20,12},{24,16},{28,20},{1,25},{... | collective-permute-start | bytes 688136 | tf_op jit(solution)/shard_map/ppermute | solution.py:22
  27.5 1.8 %collective-permute-start.6 = (bf16[128,512]{1,0:T(8,128)(2,1)S(1)}, bf16[128,512]{1,0:T(8,128)(2,1)S(1)}, u32[]{:S(2)}, u32[]{:S(2)}) collective-permute-start(bf16[128,512]{1,0:T(8,128)(2,1)S(1)} %get-tuple-element.55), channel_id=1, source_target_pairs={{0,1},{1,0},{2,3},{3,2},{4,5},{5,4},{6,7},{7,6},{8,9},{9,8},{10,11... | collective-permute-start | bytes 393224 | tf_op jit(solution)/shard_map/ppermute | solution.py:27
  27.5 2.1 %collective-permute-start.7 = (bf16[128,512]{1,0:T(8,128)(2,1)S(1)}, bf16[128,512]{1,0:T(8,128)(2,1)S(1)}, u32[]{:S(2)}, u32[]{:S(2)}) collective-permute-start(bf16[128,512]{1,0:T(8,128)(2,1)S(1)} %get-tuple-element.56), channel_id=1, source_target_pairs={{0,1},{1,0},{2,3},{3,2},{4,5},{5,4},{6,7},{7,6},{8,9},{9,8},{10,11... | collective-permute-start | bytes 393224 | tf_op jit(solution)/shard_map/ppermute | solution.py:27
  28.0 1.6 %collective-permute-start.8 = (bf16[128,512]{1,0:T(8,128)(2,1)S(1)}, bf16[128,512]{1,0:T(8,128)(2,1)S(1)}, u32[]{:S(2)}, u32[]{:S(2)}) collective-permute-start(bf16[128,512]{1,0:T(8,128)(2,1)S(1)} %get-tuple-element.57), channel_id=1, source_target_pairs={{0,1},{1,0},{2,3},{3,2},{4,5},{5,4},{6,7},{7,6},{8,9},{9,8},{10,11... | collective-permute-start | bytes 393224 | tf_op jit(solution)/shard_map/ppermute | solution.py:27
  29.3 14.9 %collective-permute-start.2 = (bf16[112,1024]{1,0:T(8,128)(2,1)S(1)}, bf16[112,1024]{1,0:T(8,128)(2,1)S(1)}, u32[]{:S(2)}, u32[]{:S(2)}) collective-permute-start(bf16[112,1024]{1,0:T(8,128)(2,1)S(1)} %shard_map.78), channel_id=1, source_target_pairs={{0,12},{4,16},{8,20},{12,24},{16,28},{20,0},{24,4},{28,8},{1,13},{... | collective-permute-start | bytes 688136 | tf_op jit(solution)/shard_map/ppermute | solution.py:22
  29.7 14.6 %collective-permute-start.9 = (bf16[128,512]{1,0:T(8,128)(2,1)S(1)}, bf16[128,512]{1,0:T(8,128)(2,1)S(1)}, u32[]{:S(2)}, u32[]{:S(2)}) collective-permute-start(bf16[128,512]{1,0:T(8,128)(2,1)S(1)} %get-tuple-element.58.refs_0_), channel_id=1, source_target_pairs={{0,2},{1,3},{2,0},{3,1},{4,6},{5,7},{6,4},{7,5},{8,10},{9,11},{10,... | collective-permute-start | bytes 393224 | tf_op jit(solution)/shard_map/ppermute | solution.py:27
  31.2 13.1 %collective-permute-start.10 = (bf16[128,512]{1,0:T(8,128)(2,1)S(1)}, bf16[128,512]{1,0:T(8,128)(2,1)S(1)}, u32[]{:S(2)}, u32[]{:S(2)}) collective-permute-start(bf16[128,512]{1,0:T(8,128)(2,1)S(1)} %get-tuple-element.59.refs_1_), channel_id=1, source_target_pairs={{0,2},{1,3},{2,0},{3,1},{4,6},{5,7},{6,4},{7,5},{8,10},{9,11},{10,... | collective-permute-start | bytes 393224 | tf_op jit(solution)/shard_map/ppermute | solution.py:27
  32.9 11.4 %collective-permute-start.11 = (bf16[128,512]{1,0:T(8,128)(2,1)S(1)}, bf16[128,512]{1,0:T(8,128)(2,1)S(1)}, u32[]{:S(2)}, u32[]{:S(2)}) collective-permute-start(bf16[128,512]{1,0:T(8,128)(2,1)S(1)} %get-tuple-element.60.refs_2_), channel_id=1, source_target_pairs={{0,2},{1,3},{2,0},{3,1},{4,6},{5,7},{6,4},{7,5},{8,10},{9,11},{10,... | collective-permute-start | bytes 393224 | tf_op jit(solution)/shard_map/ppermute | solution.py:27
  37.8 6.5 %copy-start.2 = (s32[4,4,256]{2,1,0:T(4,128)S(1)}, s32[4,4,256]{2,1,0:T(4,128)}, u32[]{:S(2)}) copy-start(s32[4,4,256]{2,1,0:T(4,128)} %negatives_ref.1) | copy-start | bytes 49156
  37.8 6.5 %collective-permute-start.12 = (bf16[128,512]{1,0:T(8,128)(2,1)S(1)}, bf16[128,512]{1,0:T(8,128)(2,1)S(1)}, u32[]{:S(2)}, u32[]{:S(2)}) collective-permute-start(bf16[128,512]{1,0:T(8,128)(2,1)S(1)} %get-tuple-element.61.refs_3_), channel_id=1, source_target_pairs={{0,2},{1,3},{2,0},{3,1},{4,6},{5,7},{6,4},{7,5},{8,10},{9,11},{10,... | collective-permute-start | bytes 393224 | tf_op jit(solution)/shard_map/ppermute | solution.py:27
  45.2 3.5 %collective-permute-start.13 = (bf16[128,2048]{1,0:T(8,128)(2,1)S(1)}, bf16[128,2048]{1,0:T(8,128)(2,1)S(1)}, u32[]{:S(2)}, u32[]{:S(2)}) collective-permute-start(bf16[128,2048]{1,0:T(8,128)(2,1)S(1)} %shard_map.82.mine_ref), channel_id=1, source_target_pairs={{0,1},{1,0},{2,3},{3,2},{4,5},{5,4},{6,7},{7,6},{8,9},{9,8},{10,11... | collective-permute-start | bytes 1572872 | tf_op jit(solution)/shard_map/ppermute | solution.py:27
  45.4 1.8 %collective-permute-start.3 = (bf16[16,1024]{1,0:T(8,128)(2,1)S(1)}, bf16[16,1024]{1,0:T(8,128)(2,1)S(1)}, u32[]{:S(2)}, u32[]{:S(2)}) collective-permute-start(bf16[16,1024]{1,0:T(8,128)(2,1)S(1)} %shard_map.79.own_ref), channel_id=1, source_target_pairs={{0,1},{1,0},{2,3},{3,2},{4,5},{5,4},{6,7},{7,6},{8,9},{9,8},{10,11... | collective-permute-start | bytes 98312 | tf_op jit(solution)/shard_map/ppermute | solution.py:27
  47.2 4.3 %collective-permute-start.4 = (bf16[2,16,1024]{2,1,0:T(8,128)(2,1)S(1)}, bf16[2,16,1024]{2,1,0:T(8,128)(2,1)S(1)}, u32[]{:S(2)}, u32[]{:S(2)}) collective-permute-start(bf16[2,16,1024]{2,1,0:T(8,128)(2,1)S(1)} %pad_maximum_fusion), channel_id=1, source_target_pairs={{0,2},{1,3},{2,0},{3,1},{4,6},{5,7},{6,4},{7,5},{8,10},{9,11},{10,... | collective-permute-start | bytes 196616 | tf_op jit(solution)/shard_map/ppermute | solution.py:27
  50.0 5.5 %collective-permute-start.14 = (bf16[3,16,128]{2,1,0:T(8,128)(2,1)S(1)}, bf16[3,16,128]{2,1,0:T(8,128)(2,1)S(1)}, u32[]{:S(2)}, u32[]{:S(2)}) collective-permute-start(bf16[3,16,128]{2,1,0:T(8,128)(2,1)S(1)} %get-tuple-element.63), channel_id=1, source_target_pairs={{0,8},{4,12},{8,16},{12,20},{16,24},{20,28},{24,0},{28,4},{1,9},{5... | collective-permute-start | bytes 36872 | tf_op jit(solution)/shard_map/ppermute | solution.py:22
  55.9 12.3 %collective-permute-start.16 = (bf16[112,1024]{1,0:T(8,128)(2,1)S(1)}, bf16[112,1024]{1,0:T(8,128)(2,1)S(1)}, u32[]{:S(2)}, u32[]{:S(2)}) collective-permute-start(bf16[112,1024]{1,0:T(8,128)(2,1)S(1)} %get-tuple-element.65), channel_id=1, source_target_pairs={{0,4},{4,8},{8,12},{12,16},{16,20},{20,24},{24,28},{28,0},{1,5},{5... | collective-permute-start | bytes 688136 | tf_op jit(solution)/shard_map/ppermute | solution.py:22
  56.9 11.3 %collective-permute-start.17 = (bf16[112,1024]{1,0:T(8,128)(2,1)S(1)}, bf16[112,1024]{1,0:T(8,128)(2,1)S(1)}, u32[]{:S(2)}, u32[]{:S(2)}) collective-permute-start(bf16[112,1024]{1,0:T(8,128)(2,1)S(1)} %get-tuple-element.66), channel_id=1, source_target_pairs={{0,8},{4,12},{8,16},{12,20},{16,24},{20,28},{24,0},{28,4},{1,9},{5... | collective-permute-start | bytes 688136 | tf_op jit(solution)/shard_map/ppermute | solution.py:22
  56.9 16.9 %collective-permute-start.15 = (bf16[112,1024]{1,0:T(8,128)(2,1)S(1)}, bf16[112,1024]{1,0:T(8,128)(2,1)S(1)}, u32[]{:S(2)}, u32[]{:S(2)}) collective-permute-start(bf16[112,1024]{1,0:T(8,128)(2,1)S(1)} %get-tuple-element.64), channel_id=1, source_target_pairs={{0,20},{4,24},{8,28},{12,0},{16,4},{20,8},{24,12},{28,16},{1,21},{... | collective-permute-start | bytes 688136 | tf_op jit(solution)/shard_map/ppermute | solution.py:22
  61.3 9.8 %collective-permute-start.18 = (bf16[1,16,128]{2,1,0:T(8,128)(2,1)S(1)}, bf16[1,16,128]{2,1,0:T(8,128)(2,1)S(1)}, u32[]{:S(2)}, u32[]{:S(2)}) collective-permute-start(bf16[1,16,128]{2,1,0:T(8,128)(2,1)S(1)} %get-tuple-element.68), channel_id=1, source_target_pairs={{0,24},{4,28},{8,0},{12,4},{16,8},{20,12},{24,16},{28,20},{1,25},{... | collective-permute-start | bytes 12296 | tf_op jit(solution)/shard_map/ppermute | solution.py:22

commit v2 on v1

--- a/solution.py
+++ b/solution.py
@@ -76,18 +76,19 @@
         out_ref[:, k * LANES : (k + 1) * LANES] = jnp.concatenate(parts, axis=0).astype(BF16)
 
 
-def prepare_kernel(targets_at, pos_ref, ids_ref, served_ref, emb_ref, embp_ref, packet_ref, row_ref, wide, coded):
+def prepare_kernel(buckets, cap, pos_ref, ids_ref, emb_ref, after_ref, embp_ref, packet_ref, row_ref, wide, coded):
     height = embp_ref.shape[0]
     me = pos_ref[0]
     edges = ids_ref.shape[1]
-    buckets = coded.shape[0]
     for bucket in range(buckets):
-        row = targets_at + bucket
+        row = 2 * buckets + bucket
         block = jnp.concatenate([ids_ref[row : row + 1, k : k + LANES] for k in range(0, edges, LANES)], axis=0)
         high = lax.shift_right_logical(block, 8)
         coded[bucket] = jnp.concatenate([high, block - high * TILE], axis=0).astype(F32).astype(BF16)
     size = packet_ref.shape[0]
-    row_ref[...] = jnp.concatenate([served_ref[k : k + 1, :] for k in range(size)], axis=1)
+    row_ref[...] = jnp.concatenate(
+        [ids_ref[3 * buckets + k : 3 * buckets + k + 1, :cap] for k in range(size)], axis=1
+    )
     unpack_lines(emb_ref, wide, embp_ref)
     fetched = jnp.dot(embp_ref[...], hot_rows(embp_ref.shape[1], row_ref[...]), preferred_element_type=F32)
     fetched = jnp.concatenate([fetched, jnp.zeros((LANES - height, fetched.shape[1]), F32)], axis=0)
@@ -359,8 +360,8 @@
 
     tiles = lines_here * LANES // (2 * TILE)
     for tile in range(tiles):
-        spot = slice(tile * TILE, (tile + 1) * TILE)
-        total = scattered(values, cols, (step * tiles + tile) * TILE) + held_ref[:, spot]
+        base = pl.multiple_of((step * tiles + tile) * TILE, TILE)
+        total = scattered(values, cols, base) + held_ref[:, pl.ds(base, TILE)]
         for k in range(TILE // LANES):
             for half in range(2):
                 row = 2 * (tile * (TILE // LANES) + k) + half
@@ -406,12 +407,19 @@
 
     edge_rows = struct(height, edges)
     gather_flops = 2 * LANES * entities * edges
-    ids = jnp.concatenate([source_ids, relation_ids, target_ids], axis=0)
+    ids = jnp.concatenate(
+        [source_ids, relation_ids, target_ids, jnp.pad(served_rows, ((0, 0), (0, edges - served_rows.shape[1])))],
+        axis=0,
+    )
     emb_lines, rel_lines = lines(embeddings), lines(relations)
+    rel = local(
+        relation_kernel, struct(height, relation_count), rel_lines, scratch=(pltpu.VMEM(rel_lines.shape, F32),)
+    )
     emb, packet, served = local(
-        functools.partial(prepare_kernel, 2 * buckets),
+        functools.partial(prepare_kernel, buckets, served_rows.shape[1]),
         (struct(height, entities), struct(size, packet_rows, LANES), struct(1, pool_count, dtype=I32)),
-        position, ids, served_rows, emb_lines,
+        position, ids, emb_lines, rel,
+        specs={3: anywhere},
         scratch=(
             pltpu.VMEM(emb_lines.shape, F32),
             pltpu.VMEM((buckets, packet_rows - PACK, LANES), BF16),
@@ -423,9 +431,6 @@
         functools.partial(settle_kernel, 2 * buckets),
         (struct(pool_count, LANES), struct(buckets, edges, dtype=I32)),
         position, ids, packet,
-    )
-    rel = local(
-        relation_kernel, struct(height, relation_count), rel_lines, scratch=(pltpu.VMEM(rel_lines.shape, F32),)
     )
     made = local(product_kernel, (edge_rows,) * (2 * buckets), emb, rel, ids, flops=gather_flops * buckets)
     products, relation_rows = made[:buckets], made[buckets:]
@@ -442,7 +447,7 @@
     (last_target,) = take_targets((last,))
     last_target = rotate(last_target, "dom", last)
     width = buckets // 2 * edges
-    pieces = 4
+    pieces = 2
     piece = struct(pool_count, width // pieces)
     mine, *theirs = local(
         functools.partial(score_kernel, buckets),
@@ -520,7 +525,6 @@
         struct(columns, 2 * entities // LANES, LANES, dtype=F32),
         *args,
         grid=(steps,),
-        specs={len(args) - 1: pl.BlockSpec((height, entities // steps), lambda i: (0, i))},
         out_specs=pl.BlockSpec((columns, 2 * entities // LANES // steps, LANES), lambda i: (0, i, 0)),
         scratch=(
             pltpu.VMEM((height, count), BF16),

time: 78.5 us -> 77.1 us (0.982)
  starting transfers between devices: 28 us -> 24.6 us
  waiting for transfers between devices: 14.2 us -> 16.7 us
    ppermute x11 -> x7, starting transfers between devices: 7.76 us -> 4.84 us  [swap(): return lax.ppermute(shard, axis, [(i, i ^ bit) for i in range(size)])]
    ppermute x8, waiting for transfers between devices: 12.7 us -> 14.6 us  [rotate(): lax.ppermute(shard, axis, [(i, (i + by) % size) for i in range(size)])]
    unnamed x8 -> x6, local copies, waits for them, and re-layouts: 2.72 us -> 2.04 us
  transfers between devices with their start and end apart: 20 -> 16, of which waited for: 7 -> 7; matrix products, arithmetic and copies ran while one was open for 0% -> 0% of each run, Pallas kernels for 28% -> 29%
where the time goes in v2:
time: 77.1 us; the launch traced here: 76.7 us
  Pallas kernels  32.3 us (42%)
  starting transfers between devices  24.6 us (32%)
  waiting for transfers between devices  16.7 us (22%)
  local copies, waits for them, and re-layouts  2.04 us (3%)
  other arithmetic  0.87 us (1%)
    pallas_call x15, Pallas kernels, local(): pl.pallas_call(kernel, out_shape=out, in_specs=chosen, out_specs=jax.tree...  32.3 us
    ppermute x8, waiting for transfers between devices, rotate(): lax.ppermute(shard, axis, [(i, (i + by) % size) for i in range(size)])  14.6 us
    ppermute x8, starting transfers between devices, rotate(): lax.ppermute(shard, axis, [(i, (i + by) % size) for i in range(size)])  12.5 us
    all_to_all x1, starting transfers between devices, body(): lax.all_to_all(packet, 'dom', split_axis=0, concat_axis=0, tiled=True)  7.28 us
    ppermute x7, starting transfers between devices, swap(): return lax.ppermute(shard, axis, [(i, i ^ bit) for i in range(size)])  4.84 us
    unnamed x6, local copies, waits for them, and re-layouts  2.04 us
  transfers between devices with their start and end apart: 16, of which 7 were waited for; matrix products, arithmetic and copies ran while one was open for 0% of the time, Pallas kernels for 29%

profile of v2, /device:TPU:0, one launch (start us, length us, event | category | flops | bytes accessed | tf_op | source)
XLA Modules:
  0.0 76.7 jit_solution(16908911216706900433)
XLA Ops:
  0.0 0.0 copy-start.1
  0.0 0.9 %copy-done.1 = bf16[2,50,512]{2,0,1:T(2,128)(2,1)S(1)} copy-done((bf16[2,50,512]{2,0,1:T(2,128)(2,1)S(1)}, bf16[2,50,512]{2,0,1:T(2,128)(2,1)}, u32[]{:S(2)}) %copy-start.1) | copy-done | bytes 102424
  0.9 0.1 shard_map.73.after_ref.rel_ref
  1.0 0.1 pad_add_fusion.1.pos_ref
  1.0 0.8 %pad_add_fusion.ids_ref = s32[20,1024]{1,0:T(8,128)S(1)} fusion(s32[8,16]{1,0:T(8,128)} %param.13, s32[4,1024]{1,0:T(4,128)} %param.11, s32[4,1024]{1,0:T(4,128)} %param.10, s32[4,1024]{1,0:T(4,128)} %param.9), kind=kLoop, calls=%fused_computation | loop fusion | flops 61440 | bytes 131584 | tf_op jit(solution)/shard_map/concatenate | solution.py:410
  1.8 0.0 copy-start
  1.8 1.1 %copy-done = bf16[2,50,4096]{2,0,1:T(2,128)(2,1)S(1)} copy-done((bf16[2,50,4096]{2,0,1:T(2,128)(2,1)S(1)}, bf16[2,50,4096]{2,0,1:T(2,128)(2,1)}, u32[]{:S(2)}) %copy-start) | copy-done | bytes 819224
  3.0 2.8 %shard_map.74 = (bf16[112,4096]{1,0:T(8,128)(2,1)S(1)}, bf16[8,32,128]{2,1,0:T(8,128)(2,1)}, s32[1,128]{1,0:T(1,128)S(1)}) custom-call(s32[2]{0:T(128)S(1)} %pad_add_fusion.1.pos_ref, s32[20,1024]{1,0:T(8,128)S(1)} %pad_add_fusion.ids_ref, bf16[3200,128]{1,0:T(8,128)(2,1)S(1)} %bitcast.19, bf16[112,512]{1,0:T(8,128)(2,1)S(1)} %shard_map.73.after_ref.rel_ref), custom_call_target="tpu_custom_call" | custom-call | flops 134217728 | bytes 1999368 | tf_op jit(solution)/shard_map/pallas_call | solution.py:393
  5.8 7.3 %all-to-all-start = ((bf16[8,32,128]{2,1,0:T(8,128)(2,1)}), bf16[8,32,128]{2,1,0:T(8,128)(2,1)S(1)}, u32[]{:S(2)}, u32[]{:S(2)}) async-start(bf16[8,32,128]{2,1,0:T(8,128)(2,1)} %get-tuple-element.37), calls=%async_computation | async-start | bytes 131072 | tf_op jit(solution)/shard_map/all_to_all | solution.py:429
  13.1 6.3 %shard_map.76 = (bf16[112,1024]{1,0:T(8,128)(2,1)S(1)}, bf16[112,1024]{1,0:T(8,128)(2,1)S(1)}, bf16[112,1024]{1,0:T(8,128)(2,1)S(1)}, bf16[112,1024]{1,0:T(8,128...) custom-call(bf16[112,4096]{1,0:T(8,128)(2,1)S(1)} %get-tuple-element, ...), custom_call_target="tpu_custom_call" | custom-call | flops 4294967296 | bytes 2949120 | tf_op jit(solution)/shard_map/pallas_call | solution.py:393
  19.4 0.6 all-to-all-done.packet_ref
  20.0 0.6 shard_map.75
  20.5 1.5 %shard_map.80 = (f32[128,2048]{1,0:T(8,128)S(1)}, bf16[128,1024]{1,0:T(8,128)(2,1)S(1)}, bf16[128,1024]{1,0:T(8,128)(2,1)S(1)}) custom-call(s32[2]{0:T(128)S(1)} %pad_add_fusion.1.pos_ref, bf16[128,128]{1,0:T(8,128)(2,1)S(1)} %get-tuple-element.48.pool_ref, bf16[112,1024]{1,0:T(8,128)(2,1)S(1)} %get-tuple-element.41.refs_0_, ...), custom_call_target="tpu_custom_call" | custom-call | flops 134217728 | bytes 2523144 | tf_op jit(solution)/shard_map/pallas_call | solution.py:393
  22.0 0.1 collective-permute-start.5
  22.1 0.5 collective-permute-start.6
  22.6 4.1 %collective-permute-start = (bf16[112,1024]{1,0:T(8,128)(2,1)S(1)}, bf16[112,1024]{1,0:T(8,128)(2,1)S(1)}, u32[]{:S(2)}, u32[]{:S(2)}) collective-permute-start(bf16[112,1024]{1,0:T(8,128)(2,1)S(1)} %get-tuple-element.43.refs_1_), channel_id=1, source_target_pairs={{0,28},{4,0},{8,4},{12,8},{16,12},{20,16},{24,20},{28,24},{1,29},{... | collective-permute-start | bytes 688136 | tf_op jit(solution)/shard_map/ppermute | solution.py:22
  26.7 0.6 collective-permute-start.1
  27.3 1.3 %shard_map.78 = bf16[112,1024]{1,0:T(8,128)(2,1)S(1)} custom-call(bf16[112,4096]{1,0:T(8,128)(2,1)S(1)} %get-tuple-element.40.emb_ref, s32[4,1024]{1,0:T(4,128)S(1)} %get-tuple-element.38.asked_ref), custom_call_target="tpu_custom_call" | custom-call | flops 1073741824 | bytes 1163264 | tf_op jit(solution)/shard_map/pallas_call | solution.py:393
  28.6 0.2 collective-permute-start.2
  28.9 0.0 collective-permute-done.5.refs_0_
  28.9 0.0 collective-permute-done.6.refs_1_
  28.9 0.1 shard_map.81
  29.0 1.6 %collective-permute-start.7 = (bf16[128,1024]{1,0:T(8,128)(2,1)S(1)}, bf16[128,1024]{1,0:T(8,128)(2,1)S(1)}, u32[]{:S(2)}, u32[]{:S(2)}) collective-permute-start(bf16[128,1024]{1,0:T(8,128)(2,1)S(1)} %get-tuple-element.52.refs_0_), channel_id=1, source_target_pairs={{0,2},{1,3},{2,0},{3,1},{4,6},{5,7},{6,4},{7,5},{8,10},{9,11},{10,... | collective-permute-start | bytes 786440 | tf_op jit(solution)/shard_map/ppermute | solution.py:27
  30.5 0.0 copy-start.2
  30.5 0.5 collective-permute-start.8
  31.1 3.7 %shard_map.77 = (bf16[112,1024]{1,0:T(8,128)(2,1)S(1)}, bf16[112,1024]{1,0:T(8,128)(2,1)S(1)}, bf16[112,1024]{1,0:T(8,128)(2,1)S(1)}) custom-call(bf16[112,4096]{1,0:T(8,128)(2,1)S(1)} %get-tuple-element.40.emb_ref, s32[4,1024]{1,0:T(4,128)S(1)} %get-tuple-element.38.asked_ref), custom_call_target="tpu_custom_call" | custom-call | flops 3221225472 | bytes 1622016 | tf_op jit(solution)/shard_map/pallas_call | solution.py:393
  34.8 0.0 collective-permute-done.refs_2_.refs_5_.refs_1_
  34.8 2.8 %collective-permute-done.1.refs_4_.refs_6_.refs_2_ = bf16[112,1024]{1,0:T(8,128)(2,1)S(1)} collective-permute-done((bf16[112,1024]{1,0:T(8,128)(2,1)S(1)}, bf16[112,1024]{1,0:T(8,128)(2,1)S(1)}, u32[]{:S(2)}, u32[]{:S(2)}) %collective-permute-start.1) | collective-permute-done | bytes 229408 | tf_op jit(solution)/shard_map/ppermute | solution.py:22
  37.6 5.0 %collective-permute-done.2.refs_7_.refs_3_ = bf16[112,1024]{1,0:T(8,128)(2,1)S(1)} collective-permute-done((bf16[112,1024]{1,0:T(8,128)(2,1)S(1)}, bf16[112,1024]{1,0:T(8,128)(2,1)S(1)}, u32[]{:S(2)}, u32[]{:S(2)}) %collective-permute-start.2) | collective-permute-done | bytes 229408 | tf_op jit(solution)/shard_map/ppermute | solution.py:22
  42.6 0.0 collective-permute-done.7.refs_2_
  42.6 0.0 collective-permute-done.8.refs_3_
  42.6 0.0 copy-done.2
  42.6 0.9 %shard_map.82.mine_ref = bf16[128,2048]{1,0:T(8,128)(2,1)S(1)} custom-call(s32[2]{0:T(128)S(1)} %pad_add_fusion.1.pos_ref, s32[4,4,256]{2,1,0:T(4,128)S(1)} %copy-done.2, bf16[128,1024]{1,0:T(8,128)(2,1)S(1)} %get-tuple-element.52.refs_0_, bf16[128,1024]{1,0:T(8,128)(2,1)S(1)} %get-tuple-element.53.refs_1_, ...), custom_call_target="tpu_custom_call" | custom-call | bytes 2506760 | tf_op jit(solution)/shard_map/pallas_call | solution.py:393
  43.5 0.1 collective-permute-start.9
  43.5 0.1 shard_map.79.own_ref
  43.7 0.6 collective-permute-start.3
  44.2 1.2 %collective-permute-done.3.near_ref = bf16[16,1024]{1,0:T(8,128)(2,1)S(1)} collective-permute-done((bf16[16,1024]{1,0:T(8,128)(2,1)S(1)}, bf16[16,1024]{1,0:T(8,128)(2,1)S(1)}, u32[]{:S(2)}, u32[]{:S(2)}) %collective-permute-start.3) | collective-permute-done | bytes 32800 | tf_op jit(solution)/shard_map/ppermute | solution.py:27
  45.5 1.6 %collective-permute-start.4 = (bf16[2,16,1024]{2,1,0:T(8,128)(2,1)S(1)}, bf16[2,16,1024]{2,1,0:T(8,128)(2,1)S(1)}, u32[]{:S(2)}, u32[]{:S(2)}) collective-permute-start(bf16[2,16,1024]{2,1,0:T(8,128)(2,1)S(1)} %pad_maximum_fusion), channel_id=1, source_target_pairs={{0,2},{1,3},{2,0},{3,1},{4,6},{5,7},{6,4},{7,5},{8,10},{9,11},{10,... | collective-permute-start | bytes 196616 | tf_op jit(solution)/shard_map/ppermute | solution.py:27
  47.1 0.0 collective-permute-done.9.theirs_ref
  47.1 1.3 %shard_map.83 = (bf16[1,16,128]{2,1,0:T(8,128)(2,1)S(1)}, bf16[3,16,128]{2,1,0:T(8,128)(2,1)S(1)}, bf16[3,16,128]{2,1,0:T(8,128)(2,1)S(1)}, bf16[1,16,128]{2,1,0:T(8,128)(2,1)S(1)}, f32[112,4096]{1,0:T(8,128)S(1)}) custom-call(s32[2]{0:T(128)S(1)} %pad_add_fusion.1.pos_ref, bf16[128,2048]{1,0:T(8,128)(2,1)S(1)} %shard_map.82.mine_ref, ...), custom_call_target="tpu_custom_call" | custom-call | flops 268435456 | bytes 3866632 | tf_op jit(solution)/shard_map/pallas_call | solution.py:393
  48.3 1.2 %collective-permute-start.10 = (bf16[3,16,128]{2,1,0:T(8,128)(2,1)S(1)}, bf16[3,16,128]{2,1,0:T(8,128)(2,1)S(1)}, u32[]{:S(2)}, u32[]{:S(2)}) collective-permute-start(bf16[3,16,128]{2,1,0:T(8,128)(2,1)S(1)} %get-tuple-element.55), channel_id=1, source_target_pairs={{0,8},{4,12},{8,16},{12,20},{16,24},{20,28},{24,0},{28,4},{1,9},{5... | collective-permute-start | bytes 36872 | tf_op jit(solution)/shard_map/ppermute | solution.py:22
  49.6 0.3 collective-permute-done.4.far_ref
  49.8 4.1 %collective-permute-done.10.refs_6_ = bf16[3,16,128]{2,1,0:T(8,128)(2,1)S(1)} collective-permute-done((bf16[3,16,128]{2,1,0:T(8,128)(2,1)S(1)}, bf16[3,16,128]{2,1,0:T(8,128)(2,1)S(1)}, u32[]{:S(2)}, u32[]{:S(2)}) %collective-permute-start.10) | collective-permute-done | bytes 12320 | tf_op jit(solution)/shard_map/ppermute | solution.py:22
  53.9 0.4 shard_map.84
  54.2 1.6 %collective-permute-start.12 = (bf16[112,1024]{1,0:T(8,128)(2,1)S(1)}, bf16[112,1024]{1,0:T(8,128)(2,1)S(1)}, u32[]{:S(2)}, u32[]{:S(2)}) collective-permute-start(bf16[112,1024]{1,0:T(8,128)(2,1)S(1)} %get-tuple-element.57), channel_id=1, source_target_pairs={{0,4},{4,8},{8,12},{12,16},{16,20},{20,24},{24,28},{28,0},{1,5},{5... | collective-permute-start | bytes 688136 | tf_op jit(solution)/shard_map/ppermute | solution.py:22
  55.9 0.0 collective-permute-start.13
  55.9 3.7 %collective-permute-start.11 = (bf16[112,1024]{1,0:T(8,128)(2,1)S(1)}, bf16[112,1024]{1,0:T(8,128)(2,1)S(1)}, u32[]{:S(2)}, u32[]{:S(2)}) collective-permute-start(bf16[112,1024]{1,0:T(8,128)(2,1)S(1)} %get-tuple-element.56), channel_id=1, source_target_pairs={{0,20},{4,24},{8,28},{12,0},{16,4},{20,8},{24,12},{28,16},{1,21},{... | collective-permute-start | bytes 688136 | tf_op jit(solution)/shard_map/ppermute | solution.py:22
  59.6 0.9 %collective-permute-start.14 = (bf16[1,16,128]{2,1,0:T(8,128)(2,1)S(1)}, bf16[1,16,128]{2,1,0:T(8,128)(2,1)S(1)}, u32[]{:S(2)}, u32[]{:S(2)}) collective-permute-start(bf16[1,16,128]{2,1,0:T(8,128)(2,1)S(1)} %get-tuple-element.60), channel_id=1, source_target_pairs={{0,24},{4,28},{8,0},{12,4},{16,8},{20,12},{24,16},{28,20},{1,25},{... | collective-permute-start | bytes 12296 | tf_op jit(solution)/shard_map/ppermute | solution.py:22
  60.5 6.4 %shard_map.85.refs_4_ = f32[112,4096]{1,0:T(8,128)S(1)} custom-call(s32[20,1024]{1,0:T(8,128)S(1)} %pad_add_fusion.ids_ref, s32[4,1024]{1,0:T(4,128)S(1)} %get-tuple-element.38.asked_ref, f32[16,1024]{1,0:T(8,128)S(1)} %get-tuple-element.64.slope_ref, f32[112,4096]{1,0:T(8,128)S(1)} %get-tuple-element.61.query_ref, ...), custom_call_target="tpu_custom_call" | custom-call | bytes 5439488 | tf_op jit(solution)/shard_map/pallas_call | solution.py:393
  66.9 0.0 collective-permute-done.12.refs_2_.refs_0_
  66.9 0.0 collective-permute-done.13.refs_3_.refs_1_
  66.9 2.8 %shard_map.86.refs_4_ = f32[112,4096]{1,0:T(8,128)S(1)} custom-call(s32[20,1024]{1,0:T(8,128)S(1)} %pad_add_fusion.ids_ref, f32[112,4096]{1,0:T(8,128)S(1)} %get-tuple-element.61.query_ref, bf16[112,1024]{1,0:T(8,128)(2,1)S(1)} %get-tuple-element.62.refs_0_, bf16[112,1024]{1,0:T(8,128)(2,1)S(1)} %get-tuple-element.63.refs_1_, ...), custom_call_target="tpu_custom_call" | custom-call | flops 2147483648 | bytes 6504448 | tf_op jit(solution)/shard_map/pallas_call | solution.py:393
  69.7 0.0 collective-permute-done.14.refs_3_
  69.8 2.8 %collective-permute-done.11.push_ref = bf16[112,1024]{1,0:T(8,128)(2,1)S(1)} collective-permute-done((bf16[112,1024]{1,0:T(8,128)(2,1)S(1)}, bf16[112,1024]{1,0:T(8,128)(2,1)S(1)}, u32[]{:S(2)}, u32[]{:S(2)}) %collective-permute-start.11) | collective-permute-done | bytes 229408 | tf_op jit(solution)/shard_map/ppermute | solution.py:22
  72.5 4.1 %shard_map.87 = f32[50,64,128]{2,1,0:T(8,128)} custom-call(s32[2]{0:T(128)S(1)} %pad_add_fusion.1.pos_ref, s32[4,1024]{1,0:T(4,128)S(1)} %get-tuple-element.38.asked_ref, s32[1,128]{1,0:T(1,128)S(1)} %get-tuple-element.39.served_ref, bf16[112,1024]{1,0:T(8,128)(2,1)S(1)} %collective-permute-done.11.push_ref, ...), custom_call_target="tpu_custom_call" | custom-call | flops 1207959552 | bytes 4186632 | tf_op jit(solution)/shard_map/pallas_call | solution.py:393
  (1 shorter events, 0.0 us)
Async XLA Ops:
  0.0 0.9 %copy-start.1 = (bf16[2,50,512]{2,0,1:T(2,128)(2,1)S(1)}, bf16[2,50,512]{2,0,1:T(2,128)(2,1)}, u32[]{:S(2)}) copy-start(bf16[2,50,512]{2,0,1:T(2,128)(2,1)} %param.8) | copy-start | bytes 307204
  1.8 1.1 %copy-start = (bf16[2,50,4096]{2,0,1:T(2,128)(2,1)S(1)}, bf16[2,50,4096]{2,0,1:T(2,128)(2,1)}, u32[]{:S(2)}) copy-start(bf16[2,50,4096]{2,0,1:T(2,128)(2,1)} %param.7) | copy-start | bytes 2457604
  5.8 14.2 %all-to-all-start = ((bf16[8,32,128]{2,1,0:T(8,128)(2,1)}), bf16[8,32,128]{2,1,0:T(8,128)(2,1)S(1)}, u32[]{:S(2)}, u32[]{:S(2)}) async-start(bf16[8,32,128]{2,1,0:T(8,128)(2,1)} %get-tuple-element.37), calls=%async_computation | async-start | bytes 131072 | tf_op jit(solution)/shard_map/all_to_all | solution.py:429
  22.0 6.9 %collective-permute-start.5 = (bf16[128,1024]{1,0:T(8,128)(2,1)S(1)}, bf16[128,1024]{1,0:T(8,128)(2,1)S(1)}, u32[]{:S(2)}, u32[]{:S(2)}) collective-permute-start(bf16[128,1024]{1,0:T(8,128)(2,1)S(1)} %get-tuple-element.50), channel_id=1, source_target_pairs={{0,1},{1,0},{2,3},{3,2},{4,5},{5,4},{6,7},{7,6},{8,9},{9,8},{10,11... | collective-permute-start | bytes 786440 | tf_op jit(solution)/shard_map/ppermute | solution.py:27
  22.1 6.8 %collective-permute-start.6 = (bf16[128,1024]{1,0:T(8,128)(2,1)S(1)}, bf16[128,1024]{1,0:T(8,128)(2,1)S(1)}, u32[]{:S(2)}, u32[]{:S(2)}) collective-permute-start(bf16[128,1024]{1,0:T(8,128)(2,1)S(1)} %get-tuple-element.51), channel_id=1, source_target_pairs={{0,1},{1,0},{2,3},{3,2},{4,5},{5,4},{6,7},{7,6},{8,9},{9,8},{10,11... | collective-permute-start | bytes 786440 | tf_op jit(solution)/shard_map/ppermute | solution.py:27
  22.6 12.2 %collective-permute-start = (bf16[112,1024]{1,0:T(8,128)(2,1)S(1)}, bf16[112,1024]{1,0:T(8,128)(2,1)S(1)}, u32[]{:S(2)}, u32[]{:S(2)}) collective-permute-start(bf16[112,1024]{1,0:T(8,128)(2,1)S(1)} %get-tuple-element.43.refs_1_), channel_id=1, source_target_pairs={{0,28},{4,0},{8,4},{12,8},{16,12},{20,16},{24,20},{28,24},{1,29},{... | collective-permute-start | bytes 688136 | tf_op jit(solution)/shard_map/ppermute | solution.py:22
  26.7 10.9 %collective-permute-start.1 = (bf16[112,1024]{1,0:T(8,128)(2,1)S(1)}, bf16[112,1024]{1,0:T(8,128)(2,1)S(1)}, u32[]{:S(2)}, u32[]{:S(2)}) collective-permute-start(bf16[112,1024]{1,0:T(8,128)(2,1)S(1)} %get-tuple-element.45.refs_2_), channel_id=1, source_target_pairs={{0,24},{4,28},{8,0},{12,4},{16,8},{20,12},{24,16},{28,20},{1,25},{... | collective-permute-start | bytes 688136 | tf_op jit(solution)/shard_map/ppermute | solution.py:22
  28.6 14.0 %collective-permute-start.2 = (bf16[112,1024]{1,0:T(8,128)(2,1)S(1)}, bf16[112,1024]{1,0:T(8,128)(2,1)S(1)}, u32[]{:S(2)}, u32[]{:S(2)}) collective-permute-start(bf16[112,1024]{1,0:T(8,128)(2,1)S(1)} %shard_map.78), channel_id=1, source_target_pairs={{0,12},{4,16},{8,20},{12,24},{16,28},{20,0},{24,4},{28,8},{1,13},{... | collective-permute-start | bytes 688136 | tf_op jit(solution)/shard_map/ppermute | solution.py:22
  29.0 13.6 %collective-permute-start.7 = (bf16[128,1024]{1,0:T(8,128)(2,1)S(1)}, bf16[128,1024]{1,0:T(8,128)(2,1)S(1)}, u32[]{:S(2)}, u32[]{:S(2)}) collective-permute-start(bf16[128,1024]{1,0:T(8,128)(2,1)S(1)} %get-tuple-element.52.refs_0_), channel_id=1, source_target_pairs={{0,2},{1,3},{2,0},{3,1},{4,6},{5,7},{6,4},{7,5},{8,10},{9,11},{10,... | collective-permute-start | bytes 786440 | tf_op jit(solution)/shard_map/ppermute | solution.py:27
  30.5 12.0 %copy-start.2 = (s32[4,4,256]{2,1,0:T(4,128)S(1)}, s32[4,4,256]{2,1,0:T(4,128)}, u32[]{:S(2)}) copy-start(s32[4,4,256]{2,1,0:T(4,128)} %negatives_ref.1) | copy-start | bytes 49156
  30.5 12.0 %collective-permute-start.8 = (bf16[128,1024]{1,0:T(8,128)(2,1)S(1)}, bf16[128,1024]{1,0:T(8,128)(2,1)S(1)}, u32[]{:S(2)}, u32[]{:S(2)}) collective-permute-start(bf16[128,1024]{1,0:T(8,128)(2,1)S(1)} %get-tuple-element.53.refs_1_), channel_id=1, source_target_pairs={{0,2},{1,3},{2,0},{3,1},{4,6},{5,7},{6,4},{7,5},{8,10},{9,11},{10,... | collective-permute-start | bytes 786440 | tf_op jit(solution)/shard_map/ppermute | solution.py:27
  43.5 3.6 %collective-permute-start.9 = (bf16[128,2048]{1,0:T(8,128)(2,1)S(1)}, bf16[128,2048]{1,0:T(8,128)(2,1)S(1)}, u32[]{:S(2)}, u32[]{:S(2)}) collective-permute-start(bf16[128,2048]{1,0:T(8,128)(2,1)S(1)} %shard_map.82.mine_ref), channel_id=1, source_target_pairs={{0,1},{1,0},{2,3},{3,2},{4,5},{5,4},{6,7},{7,6},{8,9},{9,8},{10,11... | collective-permute-start | bytes 1572872 | tf_op jit(solution)/shard_map/ppermute | solution.py:27
  43.7 1.8 %collective-permute-start.3 = (bf16[16,1024]{1,0:T(8,128)(2,1)S(1)}, bf16[16,1024]{1,0:T(8,128)(2,1)S(1)}, u32[]{:S(2)}, u32[]{:S(2)}) collective-permute-start(bf16[16,1024]{1,0:T(8,128)(2,1)S(1)} %shard_map.79.own_ref), channel_id=1, source_target_pairs={{0,1},{1,0},{2,3},{3,2},{4,5},{5,4},{6,7},{7,6},{8,9},{9,8},{10,11... | collective-permute-start | bytes 98312 | tf_op jit(solution)/shard_map/ppermute | solution.py:27
  45.5 4.3 %collective-permute-start.4 = (bf16[2,16,1024]{2,1,0:T(8,128)(2,1)S(1)}, bf16[2,16,1024]{2,1,0:T(8,128)(2,1)S(1)}, u32[]{:S(2)}, u32[]{:S(2)}) collective-permute-start(bf16[2,16,1024]{2,1,0:T(8,128)(2,1)S(1)} %pad_maximum_fusion), channel_id=1, source_target_pairs={{0,2},{1,3},{2,0},{3,1},{4,6},{5,7},{6,4},{7,5},{8,10},{9,11},{10,... | collective-permute-start | bytes 196616 | tf_op jit(solution)/shard_map/ppermute | solution.py:27
  48.3 5.5 %collective-permute-start.10 = (bf16[3,16,128]{2,1,0:T(8,128)(2,1)S(1)}, bf16[3,16,128]{2,1,0:T(8,128)(2,1)S(1)}, u32[]{:S(2)}, u32[]{:S(2)}) collective-permute-start(bf16[3,16,128]{2,1,0:T(8,128)(2,1)S(1)} %get-tuple-element.55), channel_id=1, source_target_pairs={{0,8},{4,12},{8,16},{12,20},{16,24},{20,28},{24,0},{28,4},{1,9},{5... | collective-permute-start | bytes 36872 | tf_op jit(solution)/shard_map/ppermute | solution.py:22
  54.2 12.7 %collective-permute-start.12 = (bf16[112,1024]{1,0:T(8,128)(2,1)S(1)}, bf16[112,1024]{1,0:T(8,128)(2,1)S(1)}, u32[]{:S(2)}, u32[]{:S(2)}) collective-permute-start(bf16[112,1024]{1,0:T(8,128)(2,1)S(1)} %get-tuple-element.57), channel_id=1, source_target_pairs={{0,4},{4,8},{8,12},{12,16},{16,20},{20,24},{24,28},{28,0},{1,5},{5... | collective-permute-start | bytes 688136 | tf_op jit(solution)/shard_map/ppermute | solution.py:22
  55.9 11.0 %collective-permute-start.13 = (bf16[112,1024]{1,0:T(8,128)(2,1)S(1)}, bf16[112,1024]{1,0:T(8,128)(2,1)S(1)}, u32[]{:S(2)}, u32[]{:S(2)}) collective-permute-start(bf16[112,1024]{1,0:T(8,128)(2,1)S(1)} %get-tuple-element.58), channel_id=1, source_target_pairs={{0,8},{4,12},{8,16},{12,20},{16,24},{20,28},{24,0},{28,4},{1,9},{5... | collective-permute-start | bytes 688136 | tf_op jit(solution)/shard_map/ppermute | solution.py:22
  55.9 16.7 %collective-permute-start.11 = (bf16[112,1024]{1,0:T(8,128)(2,1)S(1)}, bf16[112,1024]{1,0:T(8,128)(2,1)S(1)}, u32[]{:S(2)}, u32[]{:S(2)}) collective-permute-start(bf16[112,1024]{1,0:T(8,128)(2,1)S(1)} %get-tuple-element.56), channel_id=1, source_target_pairs={{0,20},{4,24},{8,28},{12,0},{16,4},{20,8},{24,12},{28,16},{1,21},{... | collective-permute-start | bytes 688136 | tf_op jit(solution)/shard_map/ppermute | solution.py:22
  59.6 10.2 %collective-permute-start.14 = (bf16[1,16,128]{2,1,0:T(8,128)(2,1)S(1)}, bf16[1,16,128]{2,1,0:T(8,128)(2,1)S(1)}, u32[]{:S(2)}, u32[]{:S(2)}) collective-permute-start(bf16[1,16,128]{2,1,0:T(8,128)(2,1)S(1)} %get-tuple-element.60), channel_id=1, source_target_pairs={{0,24},{4,28},{8,0},{12,4},{16,8},{20,12},{24,16},{28,20},{1,25},{... | collective-permute-start | bytes 12296 | tf_op jit(solution)/shard_map/ppermute | solution.py:22

commit v3 on v2

--- a/solution.py
+++ b/solution.py
@@ -98,17 +98,6 @@
         packet_ref[to, PACK:, :] = coded[bucket]
 
 
-def settle_kernel(targets_at, pos_ref, ids_ref, packet_ref, pool_ref, asked_ref):
-    me = pos_ref[0]
-    size = packet_ref.shape[0]
-    pool_ref[...] = packet_ref[:, :PACK, :].reshape(pool_ref.shape)
-    asked_ref[0:1, :] = ids_ref[targets_at : targets_at + 1, :]
-    for bucket in range(1, asked_ref.shape[0]):
-        coded = packet_ref[lax.rem(me + bucket, size), PACK:, :].astype(F32)
-        half = coded.shape[0] // 2
-        asked_ref[bucket : bucket + 1, :] = lane_row((coded[:half] * float(TILE) + coded[half:]).astype(I32))
-
-
 def relation_kernel(rel_ref, relp_ref, wide):
     unpack_lines(rel_ref, wide, relp_ref)
 
@@ -145,13 +134,16 @@
         refs[count + k][...] = (mine_ref[:, spot] + refs[k][...].astype(F32)).astype(BF16)
 
 
-def score_kernel(buckets, pos_ref, pool_ref, *refs):
-    products, mine_ref, pieces = refs[:buckets], refs[buckets], refs[buckets + 1 :]
-    core = pos_ref[1]
+def score_kernel(buckets, pos_ref, packet_ref, ids_ref, *refs):
+    products, (pool_ref, asked_ref, mine_ref), pieces = refs[:buckets], refs[buckets : buckets + 3], refs[buckets + 3 :]
+    me, core = pos_ref[0], pos_ref[1]
+    size = packet_ref.shape[0]
     height, edges = products[0].shape
     per = len(pieces) // (buckets // 2)
     cut = edges // per
-    pool = pool_ref[:, :height]
+    packets = packet_ref[:, :PACK, :].reshape(pool_ref.shape)
+    pool_ref[...] = packets
+    pool = packets[:, :height]
     for bucket in range(buckets):
         half, place = divmod(bucket, buckets // 2)
         scores = jnp.dot(pool, products[bucket][...], preferred_element_type=F32)
@@ -164,6 +156,17 @@
         def _():
             for k in range(per):
                 pieces[place * per + k][...] = scores[:, k * cut : (k + 1) * cut].astype(BF16)
+
+    asked_ref[0:1, :] = ids_ref[2 * buckets : 2 * buckets + 1, :]
+    for bucket in range(1, buckets):
+        coded = packet_ref[lax.rem(me + bucket, size), PACK:, :].astype(F32)
+        half = coded.shape[0] // 2
+        asked_ref[bucket : bucket + 1, :] = lane_row((coded[:half] * float(TILE) + coded[half:]).astype(I32))
+
+
+def join_kernel(own_ref, near_ref, after_ref, out_ref):
+    out_ref[0] = own_ref[...]
+    out_ref[1] = near_ref[...]
 
 
 def slope_kernel(pieces, pos_ref, negatives_ref, *refs):
@@ -226,13 +229,13 @@
     out_ref[...] = jnp.concatenate(rows, axis=0).astype(BF16)
 
 
-def scale_kernel(buckets, columns, own_ref, near_ref, far_ref, *refs):
+def scale_kernel(buckets, columns, count, own_ref, near_ref, far_ref, *refs):
     positive = (
         own_ref[...].astype(F32) + near_ref[...].astype(F32) + far_ref[0].astype(F32) + far_ref[1].astype(F32)
     )
     slope = -jax.nn.sigmoid(-positive)
     last = buckets - 1
-    targets, product, riders = refs[:buckets], refs[buckets], refs[buckets + 1 : -buckets - 2]
+    targets, product, riders = refs[:buckets], refs[buckets], refs[buckets + 1 : buckets + 1 + count]
     slope_ref, outs = refs[-buckets - 2], refs[-buckets - 1 :]
     slope_ref[...] = slope
     for bucket in range(buckets):
@@ -329,45 +332,48 @@
 
 
 def final_kernel(plan, origins, pos_ref, asked_ref, served_ref, push_ref, *refs):
-    held_ref, out_ref, values, cols, back = refs[-5:]
+    held_ref, out_hbm, values, cols, back, out_ref, sems = refs[-7:]
     buckets, edges = asked_ref.shape
-    others = refs[:-5]
-    step = pl.program_id(0)
+    others = refs[:-7]
     height = push_ref.shape[0]
     pad = height // 2
-    columns, lines_here, _ = out_ref.shape
-    flat = out_ref.reshape(columns * lines_here, LANES)
-
-    @pl.when(step == 0)
-    def _():
-        me = pos_ref[0]
-        size = back.shape[0]
-        if plan is not None:
-            carriers, hop, left = plan
-            pulls, home, direct = others[: len(carriers) - 1], others[len(carriers) - 1], others[len(carriers) :]
-            back[me] = home[0]
-            for carrier, ref in zip(carriers, (*pulls, push_ref)):
-                for block, way in zip(rider_blocks(ref, columns, 2), (carrier, carrier + hop)):
-                    back[lax.rem(me + 2 * size - way, size)] = block
-            for way, ref in zip(left, direct):
-                back[lax.rem(me + size - way, size)] = ref[0]
-        else:
-            blocks = [part[k, 0] for part in others for k in range(part.shape[0])]
-            for origin, block in zip(origins, blocks):
-                back[me ^ origin] = block
-        returned = back[...].reshape(-1, LANES).astype(F32).T[:height].astype(BF16)
-        fill(values, cols, [push_ref[...], returned], [asked_ref[buckets - 1 : buckets, :], served_ref[...]])
+    steps, columns, lines_here, _ = out_ref.shape
+    me = pos_ref[0]
+    size = back.shape[0]
+    if plan is not None:
+        carriers, hop, left = plan
+        pulls, home, direct = others[: len(carriers) - 1], others[len(carriers) - 1], others[len(carriers) :]
+        back[me] = home[0]
+        for carrier, ref in zip(carriers, (*pulls, push_ref)):
+            for block, way in zip(rider_blocks(ref, columns, 2), (carrier, carrier + hop)):
+                back[lax.rem(me + 2 * size - way, size)] = block
+        for way, ref in zip(left, direct):
+            back[lax.rem(me + size - way, size)] = ref[0]
+    else:
+        blocks = [part[k, 0] for part in others for k in range(part.shape[0])]
+        for origin, block in zip(origins, blocks):
+            back[me ^ origin] = block
+    returned = back[...].reshape(-1, LANES).astype(F32).T[:height].astype(BF16)
+    fill(values, cols, [push_ref[...], returned], [asked_ref[buckets - 1 : buckets, :], served_ref[...]])
 
     tiles = lines_here * LANES // (2 * TILE)
-    for tile in range(tiles):
-        base = pl.multiple_of((step * tiles + tile) * TILE, TILE)
-        total = scattered(values, cols, base) + held_ref[:, pl.ds(base, TILE)]
-        for k in range(TILE // LANES):
-            for half in range(2):
-                row = 2 * (tile * (TILE // LANES) + k) + half
-                flat[pl.ds(row, columns, stride=lines_here), :] = total[
-                    half * pad : half * pad + columns, k * LANES : (k + 1) * LANES
-                ]
+    copies = []
+    for step in range(steps):
+        flat = out_ref.at[step].reshape(columns * lines_here, LANES)
+        for tile in range(tiles):
+            base = (step * tiles + tile) * TILE
+            total = scattered(values, cols, base) + held_ref[:, base : base + TILE]
+            for k in range(TILE // LANES):
+                for half in range(2):
+                    row = 2 * (tile * (TILE // LANES) + k) + half
+                    flat[pl.ds(row, columns, stride=lines_here), :] = total[
+                        half * pad : half * pad + columns, k * LANES : (k + 1) * LANES
+                    ]
+        there = out_hbm.at[:, step * lines_here : (step + 1) * lines_here, :]
+        copies.append(pltpu.make_async_copy(out_ref.at[step], there, sems.at[step]))
+        copies[-1].start()
+    for copy in copies:
+        copy.wait()
 
 
 def body(embeddings, relations, source_ids, relation_ids, target_ids, negative_ids, served_rows):
@@ -427,11 +433,6 @@
         flops=2 * LANES * entities * pool_count,
     )
     packet = lax.all_to_all(packet, "dom", split_axis=0, concat_axis=0, tiled=True)
-    pool, asked = local(
-        functools.partial(settle_kernel, 2 * buckets),
-        (struct(pool_count, LANES), struct(buckets, edges, dtype=I32)),
-        position, ids, packet,
-    )
     made = local(product_kernel, (edge_rows,) * (2 * buckets), emb, rel, ids, flops=gather_flops * buckets)
     products, relation_rows = made[:buckets], made[buckets:]
     last = buckets - 1
@@ -444,17 +445,22 @@
         )
 
     owned_products = [products[0]] + [rotate(products[b], "dom", -b) for b in range(1, last)]
-    (last_target,) = take_targets((last,))
-    last_target = rotate(last_target, "dom", last)
     width = buckets // 2 * edges
     pieces = 2
     piece = struct(pool_count, width // pieces)
-    mine, *theirs = local(
+    pool, asked, mine, *theirs = local(
         functools.partial(score_kernel, buckets),
-        (struct(pool_count, width, dtype=F32),) + (piece,) * pieces,
-        position, pool, *products,
+        (
+            struct(pool_count, LANES),
+            struct(buckets, edges, dtype=I32),
+            struct(pool_count, width, dtype=F32),
+            *(piece,) * pieces,
+        ),
+        position, packet, ids, *products,
         flops=2 * LANES * pool_count * edges * buckets,
     )
+    (last_target,) = take_targets((last,))
+    last_target = rotate(last_target, "dom", last)
     pair = local(pair_kernel, (piece,) * pieces, mine, *[swap(part, "col", 1) for part in theirs])
     targets = [*take_targets(tuple(range(last))), last_target]
     after = [targets[0], *owned_products[1:], last_target]
@@ -467,7 +473,6 @@
     pairs = [x for b in range(last) for x in (owned_products[b], targets[b])] + [products[last], last_target]
     own = local(positive_kernel, struct(PACK, edges), *pairs)
     near = swap(own, "col", 1)
-    far = swap(jnp.stack([own, near]), "col", 2)
     plan = None
     groups = [list(range(size // 2)), list(range(size // 2, size))]
     if size == 2 * buckets and columns + 4 <= height // 2:
@@ -487,14 +492,18 @@
         scratch=(pltpu.VMEM((size, PACK, LANES), BF16),),
         flops=4 * LANES * pool_count * edges * buckets,
     )
+    joined = local(
+        join_kernel, struct(2, PACK, edges), own, near, query, specs={2: anywhere}
+    )
+    far = swap(joined, "col", 2)
     if plan is None:
-        riders, origins = (), None
+        riders, direct = (), ()
         parts, origins = exchange(*sent, "dom")
     else:
         riders, origins = (sent[1], rotate(sent[2], "dom", hop)), None
         direct = [rotate(block, "dom", way) for way, block in zip(plan[2], sent[3:])]
     slope, *scaled = local(
-        functools.partial(scale_kernel, buckets, columns),
+        functools.partial(scale_kernel, buckets, columns, len(riders)),
         (struct(PACK, edges, dtype=F32),) + (edge_rows,) * (buckets + 1),
         own, near, far, *targets, products[last], *riders,
     )
@@ -517,19 +526,20 @@
         scratch=(pltpu.VMEM((height, count), BF16), pltpu.VMEM((count, LANES), I32)),
         flops=2 * LANES * count * entities,
     )
-    steps = 4
+    steps = 8
     count = edges + pool_count
     args = [position, asked, served, push, *parts, held]
     grad = local(
         functools.partial(final_kernel, plan, origins),
         struct(columns, 2 * entities // LANES, LANES, dtype=F32),
         *args,
-        grid=(steps,),
-        out_specs=pl.BlockSpec((columns, 2 * entities // LANES // steps, LANES), lambda i: (0, i, 0)),
+        out_specs=anywhere,
         scratch=(
             pltpu.VMEM((height, count), BF16),
             pltpu.VMEM((count, LANES), I32),
             pltpu.VMEM((size, PACK, LANES), BF16),
+            pltpu.VMEM((steps, columns, 2 * entities // LANES // steps, LANES), F32),
+            pltpu.SemaphoreType.DMA((steps,)),
         ),
         flops=2 * LANES * count * entities,
     )

time: 77.1 us -> 75.6 us (0.981)
  Pallas kernels: 32.3 us -> 30.7 us
    pallas_call x15, Pallas kernels: 32.3 us -> 30.7 us  [local(): pl.pallas_call(kernel, out_shape=out, in_specs=chosen, out_specs=jax.tree...]
  transfers between devices with their start and end apart: 16 -> 16, of which waited for: 7 -> 6; matrix products, arithmetic and copies ran while one was open for 0% -> 0% of each run, Pallas kernels for 29% -> 29%
where the time goes in v3:
time: 75.6 us; the launch traced here: 75.2 us
  Pallas kernels  30.7 us (41%)
  starting transfers between devices  24.6 us (33%)
  waiting for transfers between devices  16.7 us (22%)
  local copies, waits for them, and re-layouts  2.04 us (3%)
  other arithmetic  0.86 us (1%)
    pallas_call x15, Pallas kernels, local(): pl.pallas_call(kernel, out_shape=out, in_specs=chosen, out_specs=jax.tree...  30.7 us
    ppermute x8, waiting for transfers between devices, rotate(): lax.ppermute(shard, axis, [(i, (i + by) % size) for i in range(size)])  14.9 us
    ppermute x8, starting transfers between devices, rotate(): lax.ppermute(shard, axis, [(i, (i + by) % size) for i in range(size)])  12.4 us
    all_to_all x1, starting transfers between devices, body(): lax.all_to_all(packet, 'dom', split_axis=0, concat_axis=0, tiled=True)  7.28 us
    ppermute x7, starting transfers between devices, swap(): return lax.ppermute(shard, axis, [(i, i ^ bit) for i in range(size)])  4.84 us
    unnamed x6, local copies, waits for them, and re-layouts  2.04 us
  transfers between devices with their start and end apart: 16, of which 6 were waited for; matrix products, arithmetic and copies ran while one was open for 0% of the time, Pallas kernels for 29%

profile of v3, /device:TPU:0, one launch (start us, length us, event | category | flops | bytes accessed | tf_op | source)
XLA Modules:
  0.0 75.2 jit_solution(800934236887865463)
XLA Ops:
  0.0 0.0 copy-start.1
  0.0 0.9 %copy-done.1 = bf16[2,50,512]{2,0,1:T(2,128)(2,1)S(1)} copy-done((bf16[2,50,512]{2,0,1:T(2,128)(2,1)S(1)}, bf16[2,50,512]{2,0,1:T(2,128)(2,1)}, u32[]{:S(2)}) %copy-start.1) | copy-done | bytes 102424
  0.9 0.1 shard_map.73.after_ref.rel_ref
  1.0 0.1 pad_add_fusion.1.pos_ref
  1.0 0.8 %pad_add_fusion.ids_ref = s32[20,1024]{1,0:T(8,128)S(1)} fusion(s32[8,16]{1,0:T(8,128)} %param.13, s32[4,1024]{1,0:T(4,128)} %param.11, s32[4,1024]{1,0:T(4,128)} %param.10, s32[4,1024]{1,0:T(4,128)} %param.9), kind=kLoop, calls=%fused_computation | loop fusion | flops 61440 | bytes 131584 | tf_op jit(solution)/shard_map/concatenate | solution.py:416
  1.8 0.0 copy-start
  1.8 1.1 %copy-done = bf16[2,50,4096]{2,0,1:T(2,128)(2,1)S(1)} copy-done((bf16[2,50,4096]{2,0,1:T(2,128)(2,1)S(1)}, bf16[2,50,4096]{2,0,1:T(2,128)(2,1)}, u32[]{:S(2)}) %copy-start) | copy-done | bytes 819224
  3.0 2.8 %shard_map.74 = (bf16[112,4096]{1,0:T(8,128)(2,1)S(1)}, bf16[8,32,128]{2,1,0:T(8,128)(2,1)}, s32[1,128]{1,0:T(1,128)S(1)}) custom-call(s32[2]{0:T(128)S(1)} %pad_add_fusion.1.pos_ref, s32[20,1024]{1,0:T(8,128)S(1)} %pad_add_fusion.ids_ref, bf16[3200,128]{1,0:T(8,128)(2,1)S(1)} %bitcast.17, bf16[112,512]{1,0:T(8,128)(2,1)S(1)} %shard_map.73.after_ref.rel_ref), custom_call_target="tpu_custom_call" | custom-call | flops 134217728 | bytes 1999368 | tf_op jit(solution)/shard_map/pallas_call | solution.py:399
  5.8 7.3 %all-to-all-start = ((bf16[8,32,128]{2,1,0:T(8,128)(2,1)}), bf16[8,32,128]{2,1,0:T(8,128)(2,1)S(1)}, u32[]{:S(2)}, u32[]{:S(2)}) async-start(bf16[8,32,128]{2,1,0:T(8,128)(2,1)} %get-tuple-element.37), calls=%async_computation | async-start | bytes 131072 | tf_op jit(solution)/shard_map/all_to_all | solution.py:435
  13.1 6.3 %shard_map.75 = (bf16[112,1024]{1,0:T(8,128)(2,1)S(1)}, bf16[112,1024]{1,0:T(8,128)(2,1)S(1)}, bf16[112,1024]{1,0:T(8,128)(2,1)S(1)}, bf16[112,1024]{1,0:T(8,128...) custom-call(bf16[112,4096]{1,0:T(8,128)(2,1)S(1)} %get-tuple-element, ...), custom_call_target="tpu_custom_call" | custom-call | flops 4294967296 | bytes 2949120 | tf_op jit(solution)/shard_map/pallas_call | solution.py:399
  19.4 0.6 all-to-all-done.packet_ref
  20.0 1.5 %shard_map.76 = (bf16[128,128]{1,0:T(8,128)(2,1)S(1)}, s32[4,1024]{1,0:T(4,128)S(1)}, f32[128,2048]{1,0:T(8,128)S(1)}, bf16[128,1024]{1,0:T(8,128)(2,1)S(1)}, bf16[128,1024]{1,0:T(8,128)(2,1)S(1)}) custom-call(s32[2]{0:T(128)S(1)} %pad_add_fusion.1.pos_ref, bf16[8,32,128]{2,1,0:T(8,128)(2,1)S(1)} %all-to-all-done.packet_ref, ...), custom_call_target="tpu_custom_call" | custom-call | flops 134217728 | bytes 2686984 | tf_op jit(solution)/shard_map/pallas_call | solution.py:399
  21.4 0.1 collective-permute-start.4
  21.5 0.5 collective-permute-start.5
  22.0 4.1 %collective-permute-start = (bf16[112,1024]{1,0:T(8,128)(2,1)S(1)}, bf16[112,1024]{1,0:T(8,128)(2,1)S(1)}, u32[]{:S(2)}, u32[]{:S(2)}) collective-permute-start(bf16[112,1024]{1,0:T(8,128)(2,1)S(1)} %get-tuple-element.40.refs_1_), channel_id=1, source_target_pairs={{0,28},{4,0},{8,4},{12,8},{16,12},{20,16},{24,20},{28,24},{1,29},{... | collective-permute-start | bytes 688136 | tf_op jit(solution)/shard_map/ppermute | solution.py:22
  26.1 0.6 collective-permute-start.1
  26.7 1.3 %shard_map.78 = bf16[112,1024]{1,0:T(8,128)(2,1)S(1)} custom-call(bf16[112,4096]{1,0:T(8,128)(2,1)S(1)} %get-tuple-element.38.emb_ref, s32[4,1024]{1,0:T(4,128)S(1)} %get-tuple-element.43.asked_ref), custom_call_target="tpu_custom_call" | custom-call | flops 1073741824 | bytes 1163264 | tf_op jit(solution)/shard_map/pallas_call | solution.py:399
  28.1 0.2 collective-permute-start.2
  28.3 0.0 collective-permute-done.4.refs_0_
  28.3 0.0 collective-permute-done.5.refs_1_
  28.3 0.1 shard_map.80
  28.4 1.6 %collective-permute-start.6 = (bf16[128,1024]{1,0:T(8,128)(2,1)S(1)}, bf16[128,1024]{1,0:T(8,128)(2,1)S(1)}, u32[]{:S(2)}, u32[]{:S(2)}) collective-permute-start(bf16[128,1024]{1,0:T(8,128)(2,1)S(1)} %get-tuple-element.51.refs_0_), channel_id=1, source_target_pairs={{0,2},{1,3},{2,0},{3,1},{4,6},{5,7},{6,4},{7,5},{8,10},{9,11},{10,... | collective-permute-start | bytes 786440 | tf_op jit(solution)/shard_map/ppermute | solution.py:27
  30.0 0.0 copy-start.2
  30.0 0.5 collective-permute-start.7
  30.5 3.7 %shard_map.77 = (bf16[112,1024]{1,0:T(8,128)(2,1)S(1)}, bf16[112,1024]{1,0:T(8,128)(2,1)S(1)}, bf16[112,1024]{1,0:T(8,128)(2,1)S(1)}) custom-call(bf16[112,4096]{1,0:T(8,128)(2,1)S(1)} %get-tuple-element.38.emb_ref, s32[4,1024]{1,0:T(4,128)S(1)} %get-tuple-element.43.asked_ref), custom_call_target="tpu_custom_call" | custom-call | flops 3221225472 | bytes 1622016 | tf_op jit(solution)/shard_map/pallas_call | solution.py:399
  34.3 0.0 collective-permute-done.refs_2_.refs_5_.refs_1_
  34.3 2.8 %collective-permute-done.1.refs_4_.refs_6_.refs_2_ = bf16[112,1024]{1,0:T(8,128)(2,1)S(1)} collective-permute-done((bf16[112,1024]{1,0:T(8,128)(2,1)S(1)}, bf16[112,1024]{1,0:T(8,128)(2,1)S(1)}, u32[]{:S(2)}, u32[]{:S(2)}) %collective-permute-start.1) | collective-permute-done | bytes 229408 | tf_op jit(solution)/shard_map/ppermute | solution.py:22
  37.1 5.0 %collective-permute-done.2.refs_7_.refs_3_ = bf16[112,1024]{1,0:T(8,128)(2,1)S(1)} collective-permute-done((bf16[112,1024]{1,0:T(8,128)(2,1)S(1)}, bf16[112,1024]{1,0:T(8,128)(2,1)S(1)}, u32[]{:S(2)}, u32[]{:S(2)}) %collective-permute-start.2) | collective-permute-done | bytes 229408 | tf_op jit(solution)/shard_map/ppermute | solution.py:22
  42.0 0.0 collective-permute-done.6.refs_2_
  42.0 0.0 collective-permute-done.7.refs_3_
  42.0 0.0 copy-done.2
  42.1 0.9 %shard_map.81.mine_ref = bf16[128,2048]{1,0:T(8,128)(2,1)S(1)} custom-call(s32[2]{0:T(128)S(1)} %pad_add_fusion.1.pos_ref, s32[4,4,256]{2,1,0:T(4,128)S(1)} %copy-done.2, bf16[128,1024]{1,0:T(8,128)(2,1)S(1)} %get-tuple-element.51.refs_0_, bf16[128,1024]{1,0:T(8,128)(2,1)S(1)} %get-tuple-element.52.refs_1_, ...), custom_call_target="tpu_custom_call" | custom-call | bytes 2506760 | tf_op jit(solution)/shard_map/pallas_call | solution.py:399
  42.9 0.1 collective-permute-start.8
  43.0 0.1 shard_map.79.own_ref
  43.1 0.6 collective-permute-start.3
  43.7 1.2 %collective-permute-done.8.theirs_ref = bf16[128,2048]{1,0:T(8,128)(2,1)S(1)} collective-permute-done((bf16[128,2048]{1,0:T(8,128)(2,1)S(1)}, bf16[128,2048]{1,0:T(8,128)(2,1)S(1)}, u32[]{:S(2)}, u32[]{:S(2)}) %collective-permute-start.8) | collective-permute-done | bytes 524320 | tf_op jit(solution)/shard_map/ppermute | solution.py:27
  44.9 1.3 %shard_map.82 = (bf16[1,16,128]{2,1,0:T(8,128)(2,1)S(1)}, bf16[3,16,128]{2,1,0:T(8,128)(2,1)S(1)}, bf16[3,16,128]{2,1,0:T(8,128)(2,1)S(1)}, bf16[1,16,128]{2,1,0:T(8,128)(2,1)S(1)}, f32[112,4096]{1,0:T(8,128)S(1)}) custom-call(s32[2]{0:T(128)S(1)} %pad_add_fusion.1.pos_ref, bf16[128,2048]{1,0:T(8,128)(2,1)S(1)} %shard_map.81.mine_ref, ...), custom_call_target="tpu_custom_call" | custom-call | flops 268435456 | bytes 3866632 | tf_op jit(solution)/shard_map/pallas_call | solution.py:399
  46.2 0.0 collective-permute-done.3.near_ref
  46.2 1.6 %collective-permute-start.9 = (bf16[2,16,1024]{2,1,0:T(8,128)(2,1)S(1)}, bf16[2,16,1024]{2,1,0:T(8,128)(2,1)S(1)}, u32[]{:S(2)}, u32[]{:S(2)}) collective-permute-start(bf16[2,16,1024]{2,1,0:T(8,128)(2,1)S(1)} %shard_map.83), channel_id=1, source_target_pairs={{0,2},{1,3},{2,0},{3,1},{4,6},{5,7},{6,4},{7,5},{8,10},{9,11},{10,... | collective-permute-start | bytes 196616 | tf_op jit(solution)/shard_map/ppermute | solution.py:27
  47.8 1.2 %collective-permute-start.10 = (bf16[3,16,128]{2,1,0:T(8,128)(2,1)S(1)}, bf16[3,16,128]{2,1,0:T(8,128)(2,1)S(1)}, u32[]{:S(2)}, u32[]{:S(2)}) collective-permute-start(bf16[3,16,128]{2,1,0:T(8,128)(2,1)S(1)} %get-tuple-element.56), channel_id=1, source_target_pairs={{0,8},{4,12},{8,16},{12,20},{16,24},{20,28},{24,0},{28,4},{1,9},{5... | collective-permute-start | bytes 36872 | tf_op jit(solution)/shard_map/ppermute | solution.py:22
  49.0 4.3 %collective-permute-done.10.refs_6_ = bf16[3,16,128]{2,1,0:T(8,128)(2,1)S(1)} collective-permute-done((bf16[3,16,128]{2,1,0:T(8,128)(2,1)S(1)}, bf16[3,16,128]{2,1,0:T(8,128)(2,1)S(1)}, u32[]{:S(2)}, u32[]{:S(2)}) %collective-permute-start.10) | collective-permute-done | bytes 12320 | tf_op jit(solution)/shard_map/ppermute | solution.py:22
  53.3 0.0 collective-permute-done.9.far_ref
  53.3 0.4 shard_map.84
  53.6 1.6 %collective-permute-start.12 = (bf16[112,1024]{1,0:T(8,128)(2,1)S(1)}, bf16[112,1024]{1,0:T(8,128)(2,1)S(1)}, u32[]{:S(2)}, u32[]{:S(2)}) collective-permute-start(bf16[112,1024]{1,0:T(8,128)(2,1)S(1)} %get-tuple-element.58), channel_id=1, source_target_pairs={{0,4},{4,8},{8,12},{12,16},{16,20},{20,24},{24,28},{28,0},{1,5},{5... | collective-permute-start | bytes 688136 | tf_op jit(solution)/shard_map/ppermute | solution.py:22
  55.2 0.0 collective-permute-start.13
  55.2 3.7 %collective-permute-start.11 = (bf16[112,1024]{1,0:T(8,128)(2,1)S(1)}, bf16[112,1024]{1,0:T(8,128)(2,1)S(1)}, u32[]{:S(2)}, u32[]{:S(2)}) collective-permute-start(bf16[112,1024]{1,0:T(8,128)(2,1)S(1)} %get-tuple-element.57), channel_id=1, source_target_pairs={{0,20},{4,24},{8,28},{12,0},{16,4},{20,8},{24,12},{28,16},{1,21},{... | collective-permute-start | bytes 688136 | tf_op jit(solution)/shard_map/ppermute | solution.py:22
  59.0 0.9 %collective-permute-start.14 = (bf16[1,16,128]{2,1,0:T(8,128)(2,1)S(1)}, bf16[1,16,128]{2,1,0:T(8,128)(2,1)S(1)}, u32[]{:S(2)}, u32[]{:S(2)}) collective-permute-start(bf16[1,16,128]{2,1,0:T(8,128)(2,1)S(1)} %get-tuple-element.61), channel_id=1, source_target_pairs={{0,24},{4,28},{8,0},{12,4},{16,8},{20,12},{24,16},{28,20},{1,25},{... | collective-permute-start | bytes 12296 | tf_op jit(solution)/shard_map/ppermute | solution.py:22
  59.9 6.4 %shard_map.85.refs_4_ = f32[112,4096]{1,0:T(8,128)S(1)} custom-call(s32[20,1024]{1,0:T(8,128)S(1)} %pad_add_fusion.ids_ref, s32[4,1024]{1,0:T(4,128)S(1)} %get-tuple-element.43.asked_ref, f32[16,1024]{1,0:T(8,128)S(1)} %get-tuple-element.64.slope_ref, f32[112,4096]{1,0:T(8,128)S(1)} %get-tuple-element.54.after_ref.query_ref, ...), custom_call_target="tpu_custom_call" | custom-call | bytes 5439488 | tf_op jit(solution)/shard_map/pallas_call | solution.py:399
  66.2 0.0 collective-permute-done.12.refs_2_.refs_0_
  66.3 0.0 collective-permute-done.13.refs_3_.refs_1_
  66.3 2.8 %shard_map.86.refs_4_ = f32[112,4096]{1,0:T(8,128)S(1)} custom-call(s32[20,1024]{1,0:T(8,128)S(1)} %pad_add_fusion.ids_ref, f32[112,4096]{1,0:T(8,128)S(1)} %get-tuple-element.54.after_ref.query_ref, bf16[112,1024]{1,0:T(8,128)(2,1)S(1)} %get-tuple-element.62.refs_0_, bf16[112,1024]{1,0:T(8,128)(2,1)S(1)} %get-tuple-element.63.refs_1_, ...), custom_call_target="tpu_custom_call" | custom-call | flops 2147483648 | bytes 6504448 | tf_op jit(solution)/shard_map/pallas_call | solution.py:399
  69.1 0.0 collective-permute-done.14.refs_3_
  69.1 2.8 %collective-permute-done.11.push_ref = bf16[112,1024]{1,0:T(8,128)(2,1)S(1)} collective-permute-done((bf16[112,1024]{1,0:T(8,128)(2,1)S(1)}, bf16[112,1024]{1,0:T(8,128)(2,1)S(1)}, u32[]{:S(2)}, u32[]{:S(2)}) %collective-permute-start.11) | collective-permute-done | bytes 229408 | tf_op jit(solution)/shard_map/ppermute | solution.py:22
  71.9 3.1 %shard_map.87 = f32[50,64,128]{2,1,0:T(8,128)} custom-call(s32[2]{0:T(128)S(1)} %pad_add_fusion.1.pos_ref, s32[4,1024]{1,0:T(4,128)S(1)} %get-tuple-element.43.asked_ref, s32[1,128]{1,0:T(1,128)S(1)} %get-tuple-element.44.served_ref, bf16[112,1024]{1,0:T(8,128)(2,1)S(1)} %collective-permute-done.11.push_ref, ...), custom_call_target="tpu_custom_call" | custom-call | flops 1207959552 | bytes 4186632 | tf_op jit(solution)/shard_map/pallas_call | solution.py:399
  (1 shorter events, 0.0 us)
Async XLA Ops:
  0.0 0.9 %copy-start.1 = (bf16[2,50,512]{2,0,1:T(2,128)(2,1)S(1)}, bf16[2,50,512]{2,0,1:T(2,128)(2,1)}, u32[]{:S(2)}) copy-start(bf16[2,50,512]{2,0,1:T(2,128)(2,1)} %param.8) | copy-start | bytes 307204
  1.8 1.1 %copy-start = (bf16[2,50,4096]{2,0,1:T(2,128)(2,1)S(1)}, bf16[2,50,4096]{2,0,1:T(2,128)(2,1)}, u32[]{:S(2)}) copy-start(bf16[2,50,4096]{2,0,1:T(2,128)(2,1)} %param.7) | copy-start | bytes 2457604
  5.8 14.2 %all-to-all-start = ((bf16[8,32,128]{2,1,0:T(8,128)(2,1)}), bf16[8,32,128]{2,1,0:T(8,128)(2,1)S(1)}, u32[]{:S(2)}, u32[]{:S(2)}) async-start(bf16[8,32,128]{2,1,0:T(8,128)(2,1)} %get-tuple-element.37), calls=%async_computation | async-start | bytes 131072 | tf_op jit(solution)/shard_map/all_to_all | solution.py:435
  21.4 6.9 %collective-permute-start.4 = (bf16[128,1024]{1,0:T(8,128)(2,1)S(1)}, bf16[128,1024]{1,0:T(8,128)(2,1)S(1)}, u32[]{:S(2)}, u32[]{:S(2)}) collective-permute-start(bf16[128,1024]{1,0:T(8,128)(2,1)S(1)} %get-tuple-element.49), channel_id=1, source_target_pairs={{0,1},{1,0},{2,3},{3,2},{4,5},{5,4},{6,7},{7,6},{8,9},{9,8},{10,11... | collective-permute-start | bytes 786440 | tf_op jit(solution)/shard_map/ppermute | solution.py:27
  21.5 6.8 %collective-permute-start.5 = (bf16[128,1024]{1,0:T(8,128)(2,1)S(1)}, bf16[128,1024]{1,0:T(8,128)(2,1)S(1)}, u32[]{:S(2)}, u32[]{:S(2)}) collective-permute-start(bf16[128,1024]{1,0:T(8,128)(2,1)S(1)} %get-tuple-element.50), channel_id=1, source_target_pairs={{0,1},{1,0},{2,3},{3,2},{4,5},{5,4},{6,7},{7,6},{8,9},{9,8},{10,11... | collective-permute-start | bytes 786440 | tf_op jit(solution)/shard_map/ppermute | solution.py:27
  22.0 12.3 %collective-permute-start = (bf16[112,1024]{1,0:T(8,128)(2,1)S(1)}, bf16[112,1024]{1,0:T(8,128)(2,1)S(1)}, u32[]{:S(2)}, u32[]{:S(2)}) collective-permute-start(bf16[112,1024]{1,0:T(8,128)(2,1)S(1)} %get-tuple-element.40.refs_1_), channel_id=1, source_target_pairs={{0,28},{4,0},{8,4},{12,8},{16,12},{20,16},{24,20},{28,24},{1,29},{... | collective-permute-start | bytes 688136 | tf_op jit(solution)/shard_map/ppermute | solution.py:22
  26.1 10.9 %collective-permute-start.1 = (bf16[112,1024]{1,0:T(8,128)(2,1)S(1)}, bf16[112,1024]{1,0:T(8,128)(2,1)S(1)}, u32[]{:S(2)}, u32[]{:S(2)}) collective-permute-start(bf16[112,1024]{1,0:T(8,128)(2,1)S(1)} %get-tuple-element.41.refs_2_), channel_id=1, source_target_pairs={{0,24},{4,28},{8,0},{12,4},{16,8},{20,12},{24,16},{28,20},{1,25},{... | collective-permute-start | bytes 688136 | tf_op jit(solution)/shard_map/ppermute | solution.py:22
  28.1 14.0 %collective-permute-start.2 = (bf16[112,1024]{1,0:T(8,128)(2,1)S(1)}, bf16[112,1024]{1,0:T(8,128)(2,1)S(1)}, u32[]{:S(2)}, u32[]{:S(2)}) collective-permute-start(bf16[112,1024]{1,0:T(8,128)(2,1)S(1)} %shard_map.78), channel_id=1, source_target_pairs={{0,12},{4,16},{8,20},{12,24},{16,28},{20,0},{24,4},{28,8},{1,13},{... | collective-permute-start | bytes 688136 | tf_op jit(solution)/shard_map/ppermute | solution.py:22
  28.4 13.6 %collective-permute-start.6 = (bf16[128,1024]{1,0:T(8,128)(2,1)S(1)}, bf16[128,1024]{1,0:T(8,128)(2,1)S(1)}, u32[]{:S(2)}, u32[]{:S(2)}) collective-permute-start(bf16[128,1024]{1,0:T(8,128)(2,1)S(1)} %get-tuple-element.51.refs_0_), channel_id=1, source_target_pairs={{0,2},{1,3},{2,0},{3,1},{4,6},{5,7},{6,4},{7,5},{8,10},{9,11},{10,... | collective-permute-start | bytes 786440 | tf_op jit(solution)/shard_map/ppermute | solution.py:27
  30.0 12.1 %copy-start.2 = (s32[4,4,256]{2,1,0:T(4,128)S(1)}, s32[4,4,256]{2,1,0:T(4,128)}, u32[]{:S(2)}) copy-start(s32[4,4,256]{2,1,0:T(4,128)} %negatives_ref.1) | copy-start | bytes 49156
  30.0 12.0 %collective-permute-start.7 = (bf16[128,1024]{1,0:T(8,128)(2,1)S(1)}, bf16[128,1024]{1,0:T(8,128)(2,1)S(1)}, u32[]{:S(2)}, u32[]{:S(2)}) collective-permute-start(bf16[128,1024]{1,0:T(8,128)(2,1)S(1)} %get-tuple-element.52.refs_1_), channel_id=1, source_target_pairs={{0,2},{1,3},{2,0},{3,1},{4,6},{5,7},{6,4},{7,5},{8,10},{9,11},{10,... | collective-permute-start | bytes 786440 | tf_op jit(solution)/shard_map/ppermute | solution.py:27
  42.9 2.0 %collective-permute-start.8 = (bf16[128,2048]{1,0:T(8,128)(2,1)S(1)}, bf16[128,2048]{1,0:T(8,128)(2,1)S(1)}, u32[]{:S(2)}, u32[]{:S(2)}) collective-permute-start(bf16[128,2048]{1,0:T(8,128)(2,1)S(1)} %shard_map.81.mine_ref), channel_id=1, source_target_pairs={{0,1},{1,0},{2,3},{3,2},{4,5},{5,4},{6,7},{7,6},{8,9},{9,8},{10,11... | collective-permute-start | bytes 1572872 | tf_op jit(solution)/shard_map/ppermute | solution.py:27
  43.1 3.1 %collective-permute-start.3 = (bf16[16,1024]{1,0:T(8,128)(2,1)S(1)}, bf16[16,1024]{1,0:T(8,128)(2,1)S(1)}, u32[]{:S(2)}, u32[]{:S(2)}) collective-permute-start(bf16[16,1024]{1,0:T(8,128)(2,1)S(1)} %shard_map.79.own_ref), channel_id=1, source_target_pairs={{0,1},{1,0},{2,3},{3,2},{4,5},{5,4},{6,7},{7,6},{8,9},{9,8},{10,11... | collective-permute-start | bytes 98312 | tf_op jit(solution)/shard_map/ppermute | solution.py:27
  46.2 7.1 %collective-permute-start.9 = (bf16[2,16,1024]{2,1,0:T(8,128)(2,1)S(1)}, bf16[2,16,1024]{2,1,0:T(8,128)(2,1)S(1)}, u32[]{:S(2)}, u32[]{:S(2)}) collective-permute-start(bf16[2,16,1024]{2,1,0:T(8,128)(2,1)S(1)} %shard_map.83), channel_id=1, source_target_pairs={{0,2},{1,3},{2,0},{3,1},{4,6},{5,7},{6,4},{7,5},{8,10},{9,11},{10,... | collective-permute-start | bytes 196616 | tf_op jit(solution)/shard_map/ppermute | solution.py:27
  47.8 5.5 %collective-permute-start.10 = (bf16[3,16,128]{2,1,0:T(8,128)(2,1)S(1)}, bf16[3,16,128]{2,1,0:T(8,128)(2,1)S(1)}, u32[]{:S(2)}, u32[]{:S(2)}) collective-permute-start(bf16[3,16,128]{2,1,0:T(8,128)(2,1)S(1)} %get-tuple-element.56), channel_id=1, source_target_pairs={{0,8},{4,12},{8,16},{12,20},{16,24},{20,28},{24,0},{28,4},{1,9},{5... | collective-permute-start | bytes 36872 | tf_op jit(solution)/shard_map/ppermute | solution.py:22
  53.6 12.6 %collective-permute-start.12 = (bf16[112,1024]{1,0:T(8,128)(2,1)S(1)}, bf16[112,1024]{1,0:T(8,128)(2,1)S(1)}, u32[]{:S(2)}, u32[]{:S(2)}) collective-permute-start(bf16[112,1024]{1,0:T(8,128)(2,1)S(1)} %get-tuple-element.58), channel_id=1, source_target_pairs={{0,4},{4,8},{8,12},{12,16},{16,20},{20,24},{24,28},{28,0},{1,5},{5... | collective-permute-start | bytes 688136 | tf_op jit(solution)/shard_map/ppermute | solution.py:22
  55.2 11.0 %collective-permute-start.13 = (bf16[112,1024]{1,0:T(8,128)(2,1)S(1)}, bf16[112,1024]{1,0:T(8,128)(2,1)S(1)}, u32[]{:S(2)}, u32[]{:S(2)}) collective-permute-start(bf16[112,1024]{1,0:T(8,128)(2,1)S(1)} %get-tuple-element.59), channel_id=1, source_target_pairs={{0,8},{4,12},{8,16},{12,20},{16,24},{20,28},{24,0},{28,4},{1,9},{5... | collective-permute-start | bytes 688136 | tf_op jit(solution)/shard_map/ppermute | solution.py:22
  55.2 16.7 %collective-permute-start.11 = (bf16[112,1024]{1,0:T(8,128)(2,1)S(1)}, bf16[112,1024]{1,0:T(8,128)(2,1)S(1)}, u32[]{:S(2)}, u32[]{:S(2)}) collective-permute-start(bf16[112,1024]{1,0:T(8,128)(2,1)S(1)} %get-tuple-element.57), channel_id=1, source_target_pairs={{0,20},{4,24},{8,28},{12,0},{16,4},{20,8},{24,12},{28,16},{1,21},{... | collective-permute-start | bytes 688136 | tf_op jit(solution)/shard_map/ppermute | solution.py:22
  59.0 10.1 %collective-permute-start.14 = (bf16[1,16,128]{2,1,0:T(8,128)(2,1)S(1)}, bf16[1,16,128]{2,1,0:T(8,128)(2,1)S(1)}, u32[]{:S(2)}, u32[]{:S(2)}) collective-permute-start(bf16[1,16,128]{2,1,0:T(8,128)(2,1)S(1)} %get-tuple-element.61), channel_id=1, source_target_pairs={{0,24},{4,28},{8,0},{12,4},{16,8},{20,12},{24,16},{28,20},{1,25},{... | collective-permute-start | bytes 12296 | tf_op jit(solution)/shard_map/ppermute | solution.py:22

commit v4 on v3

--- a/solution.py
+++ b/solution.py
@@ -285,12 +285,21 @@
     return jnp.dot(values[...], hot, preferred_element_type=F32)
 
 
-def fill(values, cols, columns_of, rows):
+def fill(values, columns_of):
     at = 0
     for value in columns_of:
         values[:, at : at + value.shape[1]] = value
         at += value.shape[1]
-    write_columns(cols, rows)
+
+
+def columns_kernel(ids_ref, asked_ref, served_ref, after_ref, home_ref, middle_ref, final_ref):
+    buckets = asked_ref.shape[0]
+    last = buckets - 1
+    asked = [asked_ref[bucket : bucket + 1, :] for bucket in range(buckets)]
+    sources = [ids_ref[bucket : bucket + 1, :] for bucket in range(buckets)]
+    write_columns(home_ref, [*asked[:last], sources[0], sources[last]])
+    write_columns(middle_ref, sources[1:last])
+    write_columns(final_ref, [asked[last], served_ref[...]])
 
 
 def scatter_all(out_ref, values, cols, held_ref=None):
@@ -301,38 +310,35 @@
 
 
 def home_kernel(ids_ref, asked_ref, slope_ref, query_ref, *refs):
-    out_ref, values, cols = refs[-3:]
+    cols, out_ref, values = refs[-3:]
     buckets, edges = asked_ref.shape
     last = buckets - 1
     products, pulls, relation_rows = refs[:last], refs[last : last + 2], refs[last + 2 : last + 4]
     columns_of = [
         (slope_ref[bucket : bucket + 1] * products[bucket][...].astype(F32)).astype(BF16) for bucket in range(last)
     ]
-    rows = [asked_ref[bucket : bucket + 1, :] for bucket in range(last)]
     for bucket, pull, rel in zip((0, last), pulls, relation_rows):
         query = query_ref[:, bucket * edges : (bucket + 1) * edges]
         columns_of.append(source_values(pull[...].astype(F32) + query, rel))
-        rows.append(ids_ref[bucket : bucket + 1, :])
-    fill(values, cols, columns_of, rows)
+    fill(values, columns_of)
     scatter_all(out_ref, values, cols)
 
 
 def middle_kernel(ids_ref, query_ref, *refs):
-    held_ref, out_ref, values, cols = refs[-4:]
+    held_ref, cols, out_ref, values = refs[-4:]
     count = (len(refs) - 4) // 2
     relation_rows, pulls = refs[:count], refs[count : 2 * count]
     edges = pulls[0].shape[1]
-    columns_of, rows = [], []
+    columns_of = []
     for k in range(count):
         query = query_ref[:, (k + 1) * edges : (k + 2) * edges]
         columns_of.append(source_values(pulls[k][...].astype(F32) + query, relation_rows[k]))
-        rows.append(ids_ref[k + 1 : k + 2, :])
-    fill(values, cols, columns_of, rows)
+    fill(values, columns_of)
     scatter_all(out_ref, values, cols, held_ref)
 
 
 def final_kernel(plan, origins, pos_ref, asked_ref, served_ref, push_ref, *refs):
-    held_ref, out_hbm, values, cols, back, out_ref, sems = refs[-7:]
+    held_ref, cols, out_hbm, values, back, out_ref, sems = refs[-7:]
     buckets, edges = asked_ref.shape
     others = refs[:-7]
     height = push_ref.shape[0]
@@ -354,7 +360,7 @@
         for origin, block in zip(origins, blocks):
             back[me ^ origin] = block
     returned = back[...].reshape(-1, LANES).astype(F32).T[:height].astype(BF16)
-    fill(values, cols, [push_ref[...], returned], [asked_ref[buckets - 1 : buckets, :], served_ref[...]])
+    fill(values, [push_ref[...], returned])
 
     tiles = lines_here * LANES // (2 * TILE)
     copies = []
@@ -463,7 +469,17 @@
     last_target = rotate(last_target, "dom", last)
     pair = local(pair_kernel, (piece,) * pieces, mine, *[swap(part, "col", 1) for part in theirs])
     targets = [*take_targets(tuple(range(last))), last_target]
-    after = [targets[0], *owned_products[1:], last_target]
+    home_cols, middle_cols, final_cols = local(
+        columns_kernel,
+        (
+            struct((buckets + 1) * edges, LANES, dtype=I32),
+            struct((last - 1) * edges, LANES, dtype=I32),
+            struct(edges + pool_count, LANES, dtype=I32),
+        ),
+        ids, asked, served, targets[0],
+        specs={3: anywhere},
+    )
+    after = [final_cols, *owned_products[1:], last_target]
     slopes_mine = local(
         functools.partial(slope_kernel, pieces), struct(pool_count, width),
         position, negative_ids, *pair, *[swap(part, "col", 2) for part in pair], *after,
@@ -515,20 +531,20 @@
     held = local(
         home_kernel,
         struct(height, entities, dtype=F32),
-        ids, asked, slope, query, *owned_products, scaled[0], scaled[last], relation_rows[0], relation_rows[last],
-        scratch=(pltpu.VMEM((height, count), BF16), pltpu.VMEM((count, LANES), I32)),
+        ids, asked, slope, query, *owned_products, scaled[0], scaled[last], relation_rows[0], relation_rows[last], home_cols,
+        scratch=(pltpu.VMEM((height, count), BF16),),
     )
     count = (last - 1) * edges
     held = local(
         middle_kernel,
         struct(height, entities, dtype=F32),
-        ids, query, *relation_rows[1:last], *pulls, held,
-        scratch=(pltpu.VMEM((height, count), BF16), pltpu.VMEM((count, LANES), I32)),
+        ids, query, *relation_rows[1:last], *pulls, held, middle_cols,
+        scratch=(pltpu.VMEM((height, count), BF16),),
         flops=2 * LANES * count * entities,
     )
     steps = 8
     count = edges + pool_count
-    args = [position, asked, served, push, *parts, held]
+    args = [position, asked, served, push, *parts, held, final_cols]
     grad = local(
         functools.partial(final_kernel, plan, origins),
         struct(columns, 2 * entities // LANES, LANES, dtype=F32),
@@ -536,7 +552,6 @@
         out_specs=anywhere,
         scratch=(
             pltpu.VMEM((height, count), BF16),
-            pltpu.VMEM((count, LANES), I32),
             pltpu.VMEM((size, PACK, LANES), BF16),
             pltpu.VMEM((steps, columns, 2 * entities // LANES // steps, LANES), F32),
             pltpu.SemaphoreType.DMA((steps,)),

time: 75.6 us -> 75.8 us (level)
  Pallas kernels: 30.7 us -> 32.4 us
  waiting for transfers between devices: 16.7 us -> 15.1 us
    pallas_call x15 -> x16, Pallas kernels: 30.7 us -> 32.4 us  [local(): pl.pallas_call(kernel, out_shape=out, in_specs=chosen, out_specs=jax.tree...]
    ppermute x8, waiting for transfers between devices: 14.9 us -> 13.3 us  [rotate(): lax.ppermute(shard, axis, [(i, (i + by) % size) for i in range(size)])]
  transfers between devices with their start and end apart: 16 -> 16, of which waited for: 6 -> 6; matrix products, arithmetic and copies ran while one was open for 0% -> 0% of each run, Pallas kernels for 29% -> 31%
where the time goes in v4:
time: 75.8 us; the launch traced here: 75.4 us
  Pallas kernels  32.4 us (43%)
  starting transfers between devices  24.5 us (32%)
  waiting for transfers between devices  15.1 us (20%)
  local copies, waits for them, and re-layouts  2.04 us (3%)
  other arithmetic  0.86 us (1%)
    pallas_call x16, Pallas kernels, local(): pl.pallas_call(kernel, out_shape=out, in_specs=chosen, out_specs=jax.tree...  32.4 us
    ppermute x8, waiting for transfers between devices, rotate(): lax.ppermute(shard, axis, [(i, (i + by) % size) for i in range(size)])  13.3 us
    ppermute x8, starting transfers between devices, rotate(): lax.ppermute(shard, axis, [(i, (i + by) % size) for i in range(size)])  12.4 us
    all_to_all x1, starting transfers between devices, body(): lax.all_to_all(packet, 'dom', split_axis=0, concat_axis=0, tiled=True)  7.28 us
    ppermute x7, starting transfers between devices, swap(): return lax.ppermute(shard, axis, [(i, i ^ bit) for i in range(size)])  4.89 us
    unnamed x6, local copies, waits for them, and re-layouts  2.04 us
  transfers between devices with their start and end apart: 16, of which 6 were waited for; matrix products, arithmetic and copies ran while one was open for 0% of the time, Pallas kernels for 31%

profile of v4, /device:TPU:0, one launch (start us, length us, event | category | flops | bytes accessed | tf_op | source)
XLA Modules:
  0.0 75.4 jit_solution(17841332007297481880)
XLA Ops:
  0.0 0.0 copy-start.1
  0.0 0.9 %copy-done.1 = bf16[2,50,512]{2,0,1:T(2,128)(2,1)S(1)} copy-done((bf16[2,50,512]{2,0,1:T(2,128)(2,1)S(1)}, bf16[2,50,512]{2,0,1:T(2,128)(2,1)}, u32[]{:S(2)}) %copy-start.1) | copy-done | bytes 102424
  0.9 0.1 shard_map.73.after_ref.rel_ref
  1.0 0.1 pad_add_fusion.1.pos_ref
  1.0 0.8 %pad_add_fusion.ids_ref = s32[20,1024]{1,0:T(8,128)S(1)} fusion(s32[8,16]{1,0:T(8,128)} %param.13, s32[4,1024]{1,0:T(4,128)} %param.11, s32[4,1024]{1,0:T(4,128)} %param.10, s32[4,1024]{1,0:T(4,128)} %param.9), kind=kLoop, calls=%fused_computation | loop fusion | flops 61440 | bytes 131584 | tf_op jit(solution)/shard_map/concatenate | solution.py:422
  1.8 0.0 copy-start
  1.8 1.1 %copy-done = bf16[2,50,4096]{2,0,1:T(2,128)(2,1)S(1)} copy-done((bf16[2,50,4096]{2,0,1:T(2,128)(2,1)S(1)}, bf16[2,50,4096]{2,0,1:T(2,128)(2,1)}, u32[]{:S(2)}) %copy-start) | copy-done | bytes 819224
  3.0 2.8 %shard_map.74 = (bf16[112,4096]{1,0:T(8,128)(2,1)S(1)}, bf16[8,32,128]{2,1,0:T(8,128)(2,1)}, s32[1,128]{1,0:T(1,128)S(1)}) custom-call(s32[2]{0:T(128)S(1)} %pad_add_fusion.1.pos_ref, s32[20,1024]{1,0:T(8,128)S(1)} %pad_add_fusion.ids_ref, bf16[3200,128]{1,0:T(8,128)(2,1)S(1)} %bitcast.17, bf16[112,512]{1,0:T(8,128)(2,1)S(1)} %shard_map.73.after_ref.rel_ref), custom_call_target="tpu_custom_call" | custom-call | flops 134217728 | bytes 1999368 | tf_op jit(solution)/shard_map/pallas_call | solution.py:405
  5.8 7.3 %all-to-all-start = ((bf16[8,32,128]{2,1,0:T(8,128)(2,1)}), bf16[8,32,128]{2,1,0:T(8,128)(2,1)S(1)}, u32[]{:S(2)}, u32[]{:S(2)}) async-start(bf16[8,32,128]{2,1,0:T(8,128)(2,1)} %get-tuple-element.40), calls=%async_computation | async-start | bytes 131072 | tf_op jit(solution)/shard_map/all_to_all | solution.py:441
  13.1 6.3 %shard_map.75 = (bf16[112,1024]{1,0:T(8,128)(2,1)S(1)}, bf16[112,1024]{1,0:T(8,128)(2,1)S(1)}, bf16[112,1024]{1,0:T(8,128)(2,1)S(1)}, bf16[112,1024]{1,0:T(8,128...) custom-call(bf16[112,4096]{1,0:T(8,128)(2,1)S(1)} %get-tuple-element, ...), custom_call_target="tpu_custom_call" | custom-call | flops 4294967296 | bytes 2949120 | tf_op jit(solution)/shard_map/pallas_call | solution.py:405
  19.4 0.6 all-to-all-done.packet_ref
  20.0 1.5 %shard_map.76 = (bf16[128,128]{1,0:T(8,128)(2,1)S(1)}, s32[4,1024]{1,0:T(4,128)S(1)}, f32[128,2048]{1,0:T(8,128)S(1)}, bf16[128,1024]{1,0:T(8,128)(2,1)S(1)}, bf16[128,1024]{1,0:T(8,128)(2,1)S(1)}) custom-call(s32[2]{0:T(128)S(1)} %pad_add_fusion.1.pos_ref, bf16[8,32,128]{2,1,0:T(8,128)(2,1)S(1)} %all-to-all-done.packet_ref, ...), custom_call_target="tpu_custom_call" | custom-call | flops 134217728 | bytes 2686984 | tf_op jit(solution)/shard_map/pallas_call | solution.py:405
  21.4 0.1 collective-permute-start.4
  21.5 0.5 collective-permute-start.5
  22.0 4.1 %collective-permute-start = (bf16[112,1024]{1,0:T(8,128)(2,1)S(1)}, bf16[112,1024]{1,0:T(8,128)(2,1)S(1)}, u32[]{:S(2)}, u32[]{:S(2)}) collective-permute-start(bf16[112,1024]{1,0:T(8,128)(2,1)S(1)} %get-tuple-element.43.refs_1_), channel_id=1, source_target_pairs={{0,28},{4,0},{8,4},{12,8},{16,12},{20,16},{24,20},{28,24},{1,29},{... | collective-permute-start | bytes 688136 | tf_op jit(solution)/shard_map/ppermute | solution.py:22
  26.2 0.5 collective-permute-start.1
  26.7 1.3 %shard_map.78 = bf16[112,1024]{1,0:T(8,128)(2,1)S(1)} custom-call(bf16[112,4096]{1,0:T(8,128)(2,1)S(1)} %get-tuple-element.41.emb_ref, s32[4,1024]{1,0:T(4,128)S(1)} %get-tuple-element.46.asked_ref), custom_call_target="tpu_custom_call" | custom-call | flops 1073741824 | bytes 1163264 | tf_op jit(solution)/shard_map/pallas_call | solution.py:405
  28.0 0.2 collective-permute-start.2
  28.2 0.0 collective-permute-done.4.refs_0_
  28.3 0.0 collective-permute-done.5.refs_1_
  28.3 0.1 shard_map.80
  28.4 1.6 %collective-permute-start.6 = (bf16[128,1024]{1,0:T(8,128)(2,1)S(1)}, bf16[128,1024]{1,0:T(8,128)(2,1)S(1)}, u32[]{:S(2)}, u32[]{:S(2)}) collective-permute-start(bf16[128,1024]{1,0:T(8,128)(2,1)S(1)} %get-tuple-element.54.refs_0_), channel_id=1, source_target_pairs={{0,2},{1,3},{2,0},{3,1},{4,6},{5,7},{6,4},{7,5},{8,10},{9,11},{10,... | collective-permute-start | bytes 786440 | tf_op jit(solution)/shard_map/ppermute | solution.py:27
  30.0 0.0 copy-start.2
  30.0 0.5 collective-permute-start.7
  30.5 3.7 %shard_map.77 = (bf16[112,1024]{1,0:T(8,128)(2,1)S(1)}, bf16[112,1024]{1,0:T(8,128)(2,1)S(1)}, bf16[112,1024]{1,0:T(8,128)(2,1)S(1)}) custom-call(bf16[112,4096]{1,0:T(8,128)(2,1)S(1)} %get-tuple-element.41.emb_ref, s32[4,1024]{1,0:T(4,128)S(1)} %get-tuple-element.46.asked_ref), custom_call_target="tpu_custom_call" | custom-call | flops 3221225472 | bytes 1622016 | tf_op jit(solution)/shard_map/pallas_call | solution.py:405
  34.2 1.2 %shard_map.81 = (s32[5120,128]{1,0:T(8,128)S(1)}, s32[2048,128]{1,0:T(8,128)S(1)}, s32[1152,128]{1,0:T(8,128)S(1)}) custom-call(s32[20,1024]{1,0:T(8,128)S(1)} %pad_add_fusion.ids_ref, s32[4,1024]{1,0:T(4,128)S(1)} %get-tuple-element.46.asked_ref, s32[1,128]{1,0:T(1,128)S(1)} %get-tuple-element.47.served_ref, ...), custom_call_target="tpu_custom_call" | custom-call | bytes 4588032 | tf_op jit(solution)/shard_map/pallas_call | solution.py:405
  35.4 0.0 collective-permute-done.refs_2_.refs_5_.refs_1_
  35.4 1.7 %collective-permute-done.1.refs_4_.refs_6_.refs_2_ = bf16[112,1024]{1,0:T(8,128)(2,1)S(1)} collective-permute-done((bf16[112,1024]{1,0:T(8,128)(2,1)S(1)}, bf16[112,1024]{1,0:T(8,128)(2,1)S(1)}, u32[]{:S(2)}, u32[]{:S(2)}) %collective-permute-start.1) | collective-permute-done | bytes 229408 | tf_op jit(solution)/shard_map/ppermute | solution.py:22
  37.1 4.9 %collective-permute-done.2.refs_7_.refs_3_ = bf16[112,1024]{1,0:T(8,128)(2,1)S(1)} collective-permute-done((bf16[112,1024]{1,0:T(8,128)(2,1)S(1)}, bf16[112,1024]{1,0:T(8,128)(2,1)S(1)}, u32[]{:S(2)}, u32[]{:S(2)}) %collective-permute-start.2) | collective-permute-done | bytes 229408 | tf_op jit(solution)/shard_map/ppermute | solution.py:22
  42.0 0.0 collective-permute-done.6.refs_2_
  42.0 0.0 collective-permute-done.7.refs_3_
  42.0 0.0 copy-done.2
  42.0 0.9 %shard_map.82.mine_ref = bf16[128,2048]{1,0:T(8,128)(2,1)S(1)} custom-call(s32[2]{0:T(128)S(1)} %pad_add_fusion.1.pos_ref, s32[4,4,256]{2,1,0:T(4,128)S(1)} %copy-done.2, bf16[128,1024]{1,0:T(8,128)(2,1)S(1)} %get-tuple-element.54.refs_0_, bf16[128,1024]{1,0:T(8,128)(2,1)S(1)} %get-tuple-element.55.refs_1_, ...), custom_call_target="tpu_custom_call" | custom-call | bytes 2867208 | tf_op jit(solution)/shard_map/pallas_call | solution.py:405
  42.9 0.1 collective-permute-start.8
  42.9 0.1 shard_map.79.own_ref
  43.1 0.6 collective-permute-start.3
  43.6 1.2 %collective-permute-done.8.theirs_ref = bf16[128,2048]{1,0:T(8,128)(2,1)S(1)} collective-permute-done((bf16[128,2048]{1,0:T(8,128)(2,1)S(1)}, bf16[128,2048]{1,0:T(8,128)(2,1)S(1)}, u32[]{:S(2)}, u32[]{:S(2)}) %collective-permute-start.8) | collective-permute-done | bytes 524320 | tf_op jit(solution)/shard_map/ppermute | solution.py:27
  44.8 1.3 %shard_map.83 = (bf16[1,16,128]{2,1,0:T(8,128)(2,1)S(1)}, bf16[3,16,128]{2,1,0:T(8,128)(2,1)S(1)}, bf16[3,16,128]{2,1,0:T(8,128)(2,1)S(1)}, bf16[1,16,128]{2,1,0:T(8,128)(2,1)S(1)}, f32[112,4096]{1,0:T(8,128)S(1)}) custom-call(s32[2]{0:T(128)S(1)} %pad_add_fusion.1.pos_ref, bf16[128,2048]{1,0:T(8,128)(2,1)S(1)} %shard_map.82.mine_ref, ...), custom_call_target="tpu_custom_call" | custom-call | flops 268435456 | bytes 3866632 | tf_op jit(solution)/shard_map/pallas_call | solution.py:405
  46.1 0.0 collective-permute-done.3.near_ref
  46.1 1.6 %collective-permute-start.9 = (bf16[2,16,1024]{2,1,0:T(8,128)(2,1)S(1)}, bf16[2,16,1024]{2,1,0:T(8,128)(2,1)S(1)}, u32[]{:S(2)}, u32[]{:S(2)}) collective-permute-start(bf16[2,16,1024]{2,1,0:T(8,128)(2,1)S(1)} %shard_map.84), channel_id=1, source_target_pairs={{0,2},{1,3},{2,0},{3,1},{4,6},{5,7},{6,4},{7,5},{8,10},{9,11},{10,... | collective-permute-start | bytes 196616 | tf_op jit(solution)/shard_map/ppermute | solution.py:27
  47.7 1.2 %collective-permute-start.10 = (bf16[3,16,128]{2,1,0:T(8,128)(2,1)S(1)}, bf16[3,16,128]{2,1,0:T(8,128)(2,1)S(1)}, u32[]{:S(2)}, u32[]{:S(2)}) collective-permute-start(bf16[3,16,128]{2,1,0:T(8,128)(2,1)S(1)} %get-tuple-element.60), channel_id=1, source_target_pairs={{0,8},{4,12},{8,16},{12,20},{16,24},{20,28},{24,0},{28,4},{1,9},{5... | collective-permute-start | bytes 36872 | tf_op jit(solution)/shard_map/ppermute | solution.py:22
  49.0 4.3 %collective-permute-done.10.refs_6_ = bf16[3,16,128]{2,1,0:T(8,128)(2,1)S(1)} collective-permute-done((bf16[3,16,128]{2,1,0:T(8,128)(2,1)S(1)}, bf16[3,16,128]{2,1,0:T(8,128)(2,1)S(1)}, u32[]{:S(2)}, u32[]{:S(2)}) %collective-permute-start.10) | collective-permute-done | bytes 12320 | tf_op jit(solution)/shard_map/ppermute | solution.py:22
  53.2 0.0 collective-permute-done.9.far_ref
  53.2 0.4 shard_map.85
  53.6 1.6 %collective-permute-start.12 = (bf16[112,1024]{1,0:T(8,128)(2,1)S(1)}, bf16[112,1024]{1,0:T(8,128)(2,1)S(1)}, u32[]{:S(2)}, u32[]{:S(2)}) collective-permute-start(bf16[112,1024]{1,0:T(8,128)(2,1)S(1)} %get-tuple-element.62), channel_id=1, source_target_pairs={{0,4},{4,8},{8,12},{12,16},{16,20},{20,24},{24,28},{28,0},{1,5},{5... | collective-permute-start | bytes 688136 | tf_op jit(solution)/shard_map/ppermute | solution.py:22
  55.2 0.0 collective-permute-start.13
  55.2 3.7 %collective-permute-start.11 = (bf16[112,1024]{1,0:T(8,128)(2,1)S(1)}, bf16[112,1024]{1,0:T(8,128)(2,1)S(1)}, u32[]{:S(2)}, u32[]{:S(2)}) collective-permute-start(bf16[112,1024]{1,0:T(8,128)(2,1)S(1)} %get-tuple-element.61), channel_id=1, source_target_pairs={{0,20},{4,24},{8,28},{12,0},{16,4},{20,8},{24,12},{28,16},{1,21},{... | collective-permute-start | bytes 688136 | tf_op jit(solution)/shard_map/ppermute | solution.py:22
  58.9 0.9 %collective-permute-start.14 = (bf16[1,16,128]{2,1,0:T(8,128)(2,1)S(1)}, bf16[1,16,128]{2,1,0:T(8,128)(2,1)S(1)}, u32[]{:S(2)}, u32[]{:S(2)}) collective-permute-start(bf16[1,16,128]{2,1,0:T(8,128)(2,1)S(1)} %get-tuple-element.65), channel_id=1, source_target_pairs={{0,24},{4,28},{8,0},{12,4},{16,8},{20,12},{24,16},{28,20},{1,25},{... | collective-permute-start | bytes 12296 | tf_op jit(solution)/shard_map/ppermute | solution.py:22
  59.9 6.8 %shard_map.86.refs_4_ = f32[112,4096]{1,0:T(8,128)S(1)} custom-call(s32[20,1024]{1,0:T(8,128)S(1)} %pad_add_fusion.ids_ref, s32[4,1024]{1,0:T(4,128)S(1)} %get-tuple-element.46.asked_ref, f32[16,1024]{1,0:T(8,128)S(1)} %get-tuple-element.68.slope_ref, f32[112,4096]{1,0:T(8,128)S(1)} %get-tuple-element.58.after_ref.query_ref, ...), custom_call_target="tpu_custom_call" | custom-call | bytes 8060928 | tf_op jit(solution)/shard_map/pallas_call | solution.py:405
  66.7 0.0 collective-permute-done.12.refs_2_.refs_0_
  66.7 0.0 collective-permute-done.13.refs_3_.refs_1_
  66.7 2.8 %shard_map.87.refs_4_ = f32[112,4096]{1,0:T(8,128)S(1)} custom-call(s32[20,1024]{1,0:T(8,128)S(1)} %pad_add_fusion.ids_ref, f32[112,4096]{1,0:T(8,128)S(1)} %get-tuple-element.58.after_ref.query_ref, bf16[112,1024]{1,0:T(8,128)(2,1)S(1)} %get-tuple-element.66.refs_0_, bf16[112,1024]{1,0:T(8,128)(2,1)S(1)} %get-tuple-element.67.refs_1_, ...), custom_call_target="tpu_custom_call" | custom-call | flops 2147483648 | bytes 7553024 | tf_op jit(solution)/shard_map/pallas_call | solution.py:405
  69.5 0.0 collective-permute-done.14.refs_3_
  69.5 2.4 %collective-permute-done.11.push_ref = bf16[112,1024]{1,0:T(8,128)(2,1)S(1)} collective-permute-done((bf16[112,1024]{1,0:T(8,128)(2,1)S(1)}, bf16[112,1024]{1,0:T(8,128)(2,1)S(1)}, u32[]{:S(2)}, u32[]{:S(2)}) %collective-permute-start.11) | collective-permute-done | bytes 229408 | tf_op jit(solution)/shard_map/ppermute | solution.py:22
  71.9 3.3 %shard_map.88 = f32[50,64,128]{2,1,0:T(8,128)} custom-call(s32[2]{0:T(128)S(1)} %pad_add_fusion.1.pos_ref, s32[4,1024]{1,0:T(4,128)S(1)} %get-tuple-element.46.asked_ref, s32[1,128]{1,0:T(1,128)S(1)} %get-tuple-element.47.served_ref, bf16[112,1024]{1,0:T(8,128)(2,1)S(1)} %collective-permute-done.11.push_ref, ...), custom_call_target="tpu_custom_call" | custom-call | flops 1207959552 | bytes 4776456 | tf_op jit(solution)/shard_map/pallas_call | solution.py:405
  (1 shorter events, 0.0 us)
Async XLA Ops:
  0.0 0.9 %copy-start.1 = (bf16[2,50,512]{2,0,1:T(2,128)(2,1)S(1)}, bf16[2,50,512]{2,0,1:T(2,128)(2,1)}, u32[]{:S(2)}) copy-start(bf16[2,50,512]{2,0,1:T(2,128)(2,1)} %param.8) | copy-start | bytes 307204
  1.8 1.1 %copy-start = (bf16[2,50,4096]{2,0,1:T(2,128)(2,1)S(1)}, bf16[2,50,4096]{2,0,1:T(2,128)(2,1)}, u32[]{:S(2)}) copy-start(bf16[2,50,4096]{2,0,1:T(2,128)(2,1)} %param.7) | copy-start | bytes 2457604
  5.8 14.2 %all-to-all-start = ((bf16[8,32,128]{2,1,0:T(8,128)(2,1)}), bf16[8,32,128]{2,1,0:T(8,128)(2,1)S(1)}, u32[]{:S(2)}, u32[]{:S(2)}) async-start(bf16[8,32,128]{2,1,0:T(8,128)(2,1)} %get-tuple-element.40), calls=%async_computation | async-start | bytes 131072 | tf_op jit(solution)/shard_map/all_to_all | solution.py:441
  21.4 6.8 %collective-permute-start.4 = (bf16[128,1024]{1,0:T(8,128)(2,1)S(1)}, bf16[128,1024]{1,0:T(8,128)(2,1)S(1)}, u32[]{:S(2)}, u32[]{:S(2)}) collective-permute-start(bf16[128,1024]{1,0:T(8,128)(2,1)S(1)} %get-tuple-element.52), channel_id=1, source_target_pairs={{0,1},{1,0},{2,3},{3,2},{4,5},{5,4},{6,7},{7,6},{8,9},{9,8},{10,11... | collective-permute-start | bytes 786440 | tf_op jit(solution)/shard_map/ppermute | solution.py:27
  21.5 6.7 %collective-permute-start.5 = (bf16[128,1024]{1,0:T(8,128)(2,1)S(1)}, bf16[128,1024]{1,0:T(8,128)(2,1)S(1)}, u32[]{:S(2)}, u32[]{:S(2)}) collective-permute-start(bf16[128,1024]{1,0:T(8,128)(2,1)S(1)} %get-tuple-element.53), channel_id=1, source_target_pairs={{0,1},{1,0},{2,3},{3,2},{4,5},{5,4},{6,7},{7,6},{8,9},{9,8},{10,11... | collective-permute-start | bytes 786440 | tf_op jit(solution)/shard_map/ppermute | solution.py:27
  22.0 13.4 %collective-permute-start = (bf16[112,1024]{1,0:T(8,128)(2,1)S(1)}, bf16[112,1024]{1,0:T(8,128)(2,1)S(1)}, u32[]{:S(2)}, u32[]{:S(2)}) collective-permute-start(bf16[112,1024]{1,0:T(8,128)(2,1)S(1)} %get-tuple-element.43.refs_1_), channel_id=1, source_target_pairs={{0,28},{4,0},{8,4},{12,8},{16,12},{20,16},{24,20},{28,24},{1,29},{... | collective-permute-start | bytes 688136 | tf_op jit(solution)/shard_map/ppermute | solution.py:22
  26.2 10.9 %collective-permute-start.1 = (bf16[112,1024]{1,0:T(8,128)(2,1)S(1)}, bf16[112,1024]{1,0:T(8,128)(2,1)S(1)}, u32[]{:S(2)}, u32[]{:S(2)}) collective-permute-start(bf16[112,1024]{1,0:T(8,128)(2,1)S(1)} %get-tuple-element.44.refs_2_), channel_id=1, source_target_pairs={{0,24},{4,28},{8,0},{12,4},{16,8},{20,12},{24,16},{28,20},{1,25},{... | collective-permute-start | bytes 688136 | tf_op jit(solution)/shard_map/ppermute | solution.py:22
  28.0 14.0 %collective-permute-start.2 = (bf16[112,1024]{1,0:T(8,128)(2,1)S(1)}, bf16[112,1024]{1,0:T(8,128)(2,1)S(1)}, u32[]{:S(2)}, u32[]{:S(2)}) collective-permute-start(bf16[112,1024]{1,0:T(8,128)(2,1)S(1)} %shard_map.78), channel_id=1, source_target_pairs={{0,12},{4,16},{8,20},{12,24},{16,28},{20,0},{24,4},{28,8},{1,13},{... | collective-permute-start | bytes 688136 | tf_op jit(solution)/shard_map/ppermute | solution.py:22
  28.4 13.6 %collective-permute-start.6 = (bf16[128,1024]{1,0:T(8,128)(2,1)S(1)}, bf16[128,1024]{1,0:T(8,128)(2,1)S(1)}, u32[]{:S(2)}, u32[]{:S(2)}) collective-permute-start(bf16[128,1024]{1,0:T(8,128)(2,1)S(1)} %get-tuple-element.54.refs_0_), channel_id=1, source_target_pairs={{0,2},{1,3},{2,0},{3,1},{4,6},{5,7},{6,4},{7,5},{8,10},{9,11},{10,... | collective-permute-start | bytes 786440 | tf_op jit(solution)/shard_map/ppermute | solution.py:27
  30.0 12.0 %copy-start.2 = (s32[4,4,256]{2,1,0:T(4,128)S(1)}, s32[4,4,256]{2,1,0:T(4,128)}, u32[]{:S(2)}) copy-start(s32[4,4,256]{2,1,0:T(4,128)} %negatives_ref.1) | copy-start | bytes 49156
  30.0 12.0 %collective-permute-start.7 = (bf16[128,1024]{1,0:T(8,128)(2,1)S(1)}, bf16[128,1024]{1,0:T(8,128)(2,1)S(1)}, u32[]{:S(2)}, u32[]{:S(2)}) collective-permute-start(bf16[128,1024]{1,0:T(8,128)(2,1)S(1)} %get-tuple-element.55.refs_1_), channel_id=1, source_target_pairs={{0,2},{1,3},{2,0},{3,1},{4,6},{5,7},{6,4},{7,5},{8,10},{9,11},{10,... | collective-permute-start | bytes 786440 | tf_op jit(solution)/shard_map/ppermute | solution.py:27
  42.9 2.0 %collective-permute-start.8 = (bf16[128,2048]{1,0:T(8,128)(2,1)S(1)}, bf16[128,2048]{1,0:T(8,128)(2,1)S(1)}, u32[]{:S(2)}, u32[]{:S(2)}) collective-permute-start(bf16[128,2048]{1,0:T(8,128)(2,1)S(1)} %shard_map.82.mine_ref), channel_id=1, source_target_pairs={{0,1},{1,0},{2,3},{3,2},{4,5},{5,4},{6,7},{7,6},{8,9},{9,8},{10,11... | collective-permute-start | bytes 1572872 | tf_op jit(solution)/shard_map/ppermute | solution.py:27
  43.1 3.1 %collective-permute-start.3 = (bf16[16,1024]{1,0:T(8,128)(2,1)S(1)}, bf16[16,1024]{1,0:T(8,128)(2,1)S(1)}, u32[]{:S(2)}, u32[]{:S(2)}) collective-permute-start(bf16[16,1024]{1,0:T(8,128)(2,1)S(1)} %shard_map.79.own_ref), channel_id=1, source_target_pairs={{0,1},{1,0},{2,3},{3,2},{4,5},{5,4},{6,7},{7,6},{8,9},{9,8},{10,11... | collective-permute-start | bytes 98312 | tf_op jit(solution)/shard_map/ppermute | solution.py:27
  46.1 7.1 %collective-permute-start.9 = (bf16[2,16,1024]{2,1,0:T(8,128)(2,1)S(1)}, bf16[2,16,1024]{2,1,0:T(8,128)(2,1)S(1)}, u32[]{:S(2)}, u32[]{:S(2)}) collective-permute-start(bf16[2,16,1024]{2,1,0:T(8,128)(2,1)S(1)} %shard_map.84), channel_id=1, source_target_pairs={{0,2},{1,3},{2,0},{3,1},{4,6},{5,7},{6,4},{7,5},{8,10},{9,11},{10,... | collective-permute-start | bytes 196616 | tf_op jit(solution)/shard_map/ppermute | solution.py:27
  47.7 5.5 %collective-permute-start.10 = (bf16[3,16,128]{2,1,0:T(8,128)(2,1)S(1)}, bf16[3,16,128]{2,1,0:T(8,128)(2,1)S(1)}, u32[]{:S(2)}, u32[]{:S(2)}) collective-permute-start(bf16[3,16,128]{2,1,0:T(8,128)(2,1)S(1)} %get-tuple-element.60), channel_id=1, source_target_pairs={{0,8},{4,12},{8,16},{12,20},{16,24},{20,28},{24,0},{28,4},{1,9},{5... | collective-permute-start | bytes 36872 | tf_op jit(solution)/shard_map/ppermute | solution.py:22
  53.6 13.1 %collective-permute-start.12 = (bf16[112,1024]{1,0:T(8,128)(2,1)S(1)}, bf16[112,1024]{1,0:T(8,128)(2,1)S(1)}, u32[]{:S(2)}, u32[]{:S(2)}) collective-permute-start(bf16[112,1024]{1,0:T(8,128)(2,1)S(1)} %get-tuple-element.62), channel_id=1, source_target_pairs={{0,4},{4,8},{8,12},{12,16},{16,20},{20,24},{24,28},{28,0},{1,5},{5... | collective-permute-start | bytes 688136 | tf_op jit(solution)/shard_map/ppermute | solution.py:22
  55.2 11.5 %collective-permute-start.13 = (bf16[112,1024]{1,0:T(8,128)(2,1)S(1)}, bf16[112,1024]{1,0:T(8,128)(2,1)S(1)}, u32[]{:S(2)}, u32[]{:S(2)}) collective-permute-start(bf16[112,1024]{1,0:T(8,128)(2,1)S(1)} %get-tuple-element.63), channel_id=1, source_target_pairs={{0,8},{4,12},{8,16},{12,20},{16,24},{20,28},{24,0},{28,4},{1,9},{5... | collective-permute-start | bytes 688136 | tf_op jit(solution)/shard_map/ppermute | solution.py:22
  55.2 16.7 %collective-permute-start.11 = (bf16[112,1024]{1,0:T(8,128)(2,1)S(1)}, bf16[112,1024]{1,0:T(8,128)(2,1)S(1)}, u32[]{:S(2)}, u32[]{:S(2)}) collective-permute-start(bf16[112,1024]{1,0:T(8,128)(2,1)S(1)} %get-tuple-element.61), channel_id=1, source_target_pairs={{0,20},{4,24},{8,28},{12,0},{16,4},{20,8},{24,12},{28,16},{1,21},{... | collective-permute-start | bytes 688136 | tf_op jit(solution)/shard_map/ppermute | solution.py:22
  58.9 10.6 %collective-permute-start.14 = (bf16[1,16,128]{2,1,0:T(8,128)(2,1)S(1)}, bf16[1,16,128]{2,1,0:T(8,128)(2,1)S(1)}, u32[]{:S(2)}, u32[]{:S(2)}) collective-permute-start(bf16[1,16,128]{2,1,0:T(8,128)(2,1)S(1)} %get-tuple-element.65), channel_id=1, source_target_pairs={{0,24},{4,28},{8,0},{12,4},{16,8},{20,12},{24,16},{28,20},{1,25},{... | collective-permute-start | bytes 12296 | tf_op jit(solution)/shard_map/ppermute | solution.py:22
